TPU v7x, 512 devices: a whole 4x8x8 slice. The times are simulated.
512 devices in a mesh: enc: 16 (over x, y_hi, core), seq: 8 (over z), tp: 4 (over y_lo).
Axes of the slice: x: 4, y: 8 (y_hi: 2, y_lo: 4; y = y_hi * 4 + y_lo), z: 8, core: 2. Of those that a mesh axis runs over, the one named last changes fastest.
Arguments:
- patches: bfloat16 [64, 256, 1280], P('enc', 'seq'), may hold values from -1.5 to 1.5
- image_tokens: int32 [16, 4], replicated, may hold values from 1 to 64, 160 in all within a row
- image_gap: int32 [16, 4], replicated, may hold values from 0 to 215
- image_slot: int32 [64], replicated, may hold values from 0 to 63, each once
- norm_gain: float32 [1280], replicated, may hold values from 0.1 to 1.9
- merge_gain: float32 [1280], replicated, may hold values from 0.1 to 1.9
- w_qkv: bfloat16 [1280, 3840], P('enc', 'tp'), may hold values from -0.15625 to 0.15625
- w_out: bfloat16 [1280, 1280], P(('tp', 'enc')), may hold values from -0.625 to 0.625
- kv_merge: bfloat16 [5120, 1024], P('enc', 'tp'), may hold values from -0.078125 to 0.078125
- queries: bfloat16 [16, 1024, 4096], P('enc', 'seq', 'tp'), may hold values from -256 to 256
- text_kv: bfloat16 [16, 1024, 1024], P('enc', 'seq', 'tp'), may hold values from -6 to 6
- cache_kv: bfloat16 [16, 3072, 1024], P('enc', 'seq', 'tp'), may hold values from -6 to 6
Outputs:
- span_attention: bfloat16 [16, 1024, 4096], P('enc', 'seq', 'tp')
Inputs may be any that keep to these rules, and one draw needn't show every extreme that they name: `image_tokens`: each row sums to 160, and one image in every prompt has exactly 64 tokens. `image_slot`: a permutation of the slots.
All inputs are finite; a program needn't handle non-finite values.
Results may differ from a plain program's by a relative error of at most 0.017.
Values may be sent and summed in bfloat16 or wider, within the bound.
No kernel may reach another device: no remote copies, remote signals or barrier semaphores. Data moves between devices by JAX's collectives and lax.ppermute only.
A program may use at most 64 MiB of HBM per device.

v0:
```python
import math

import jax
import jax.numpy as jnp
from jax import lax
from jax.sharding import PartitionSpec as P

VHD = 80
MERGE = 4
QH = 32
KVH = 4
HD = 128


EPS = 1e-06
FAR = 1 << 30
NEG = -1e30


def rms_scale(values, gain):
    return values * lax.rsqrt(jnp.mean(values * values, axis=-1, keepdims=True) + EPS) * gain


def fold_scores(state, scores, visible):
    running, denom, accum = state
    if visible is not None:
        scores = jnp.where(visible, scores, NEG)
    highest = jnp.maximum(running, jnp.max(scores, axis=-1))
    factor = jnp.exp(running - highest)
    weights = jnp.exp(scores - highest[..., None])
    if visible is not None:
        weights = jnp.where(visible, weights, 0.0)
    denom = denom * factor + jnp.sum(weights, axis=-1)
    return (highest, factor, denom, weights.astype(jnp.bfloat16))


def per_device(
    patches,
    image_tokens,
    image_gap,
    image_slot,
    norm_gain,
    merge_gain,
    w_qkv,
    w_out,
    kv_merge,
    queries,
    text_kv,
    cache_kv,
):
    enc_index = lax.axis_index("enc")
    seq_index = lax.axis_index("seq")
    slot_total, slot_rows, width = patches.shape
    qkv_weight, out_weight, merge_weight = (
        lax.all_gather(w_qkv, "enc", axis=0, tiled=True),
        lax.all_gather(w_out, "enc", axis=0, tiled=True),
        lax.all_gather(kv_merge, "enc", axis=0, tiled=True),
    )
    counts_flat = image_tokens.reshape(-1)
    image_total = counts_flat.shape[0]
    local_slots = enc_index * slot_total + jnp.arange(slot_total, dtype=jnp.int32)
    matches = image_slot[None, :] == local_slots[:, None]
    slot_count = jnp.sum(jnp.where(matches, counts_flat[None, :], 0), axis=1)
    limit = MERGE * slot_count
    source = patches.astype(jnp.float32).reshape(slot_total * slot_rows, width)
    normed = rms_scale(source, norm_gain).astype(jnp.bfloat16)
    head_count = qkv_weight.shape[1] // (3 * VHD)
    qkv_rows = jnp.dot(normed, qkv_weight, preferred_element_type=jnp.float32).astype(jnp.bfloat16)
    qkv_rows = qkv_rows.reshape(slot_total, slot_rows, head_count, 3, VHD)
    query_part = qkv_rows[:, :, :, 0]
    key_value = qkv_rows[:, :, :, 1:].reshape(slot_total, slot_rows, head_count * 2 * VHD)
    patch_init = (
        jnp.full((slot_total, slot_rows, head_count), NEG, jnp.float32),
        jnp.zeros((slot_total, slot_rows, head_count), jnp.float32),
        jnp.zeros((slot_total, slot_rows, head_count, VHD), jnp.float32),
    )
    piece = lax.all_gather(key_value, "seq", axis=1, tiled=True)
    piece_rows = piece.shape[1]
    split = piece.reshape(slot_total, piece_rows, head_count, 2, VHD)
    scores = jnp.einsum(
        "sqhd,skhd->sqhk", query_part, split[:, :, :, 0], preferred_element_type=jnp.float32
    ) * (1.0 / math.sqrt(VHD))
    live = jnp.arange(piece_rows, dtype=jnp.int32)[None, :] < limit[:, None]
    highest, factor, denom, weights = fold_scores(patch_init, scores, live[:, None, None, :])
    accum = jnp.einsum(
        "sqhk,skhd->sqhd", weights, split[:, :, :, 1], preferred_element_type=jnp.float32
    )
    attended = (accum / denom[..., None]).astype(jnp.bfloat16)
    attended = attended.reshape(slot_total * slot_rows, head_count * VHD)
    partial_value = jnp.dot(attended, out_weight, preferred_element_type=jnp.float32)
    residual = source + lax.psum(partial_value.astype(jnp.bfloat16), "tp").astype(jnp.float32)
    merged_in = rms_scale(residual, merge_gain).astype(jnp.bfloat16)
    tokens_dev = slot_rows // MERGE
    merged = merged_in.reshape(slot_total * tokens_dev, MERGE * width)
    image_kv = jnp.dot(merged, merge_weight, preferred_element_type=jnp.float32).astype(
        jnp.bfloat16
    )
    kv_width = image_kv.shape[1]
    image_kv = image_kv.reshape(slot_total, tokens_dev, kv_width)
    every_image = lax.all_gather(image_kv, "enc", axis=0, tiled=True)
    per_prompt = image_tokens.shape[1]
    my_counts = lax.dynamic_index_in_dim(image_tokens, enc_index, 0, keepdims=False)
    my_gaps = lax.dynamic_index_in_dim(image_gap, enc_index, 0, keepdims=False)
    my_slots = lax.dynamic_slice_in_dim(image_slot, enc_index * per_prompt, per_prompt)
    selector = (my_slots[:, None] == jnp.arange(image_total, dtype=jnp.int32)[None, :]).astype(
        jnp.bfloat16
    )
    mine = jnp.dot(
        selector,
        every_image.reshape(image_total, tokens_dev * kv_width),
        preferred_element_type=jnp.float32,
    )
    mine = mine.astype(jnp.bfloat16).reshape(per_prompt * tokens_dev, kv_width)
    starts = jnp.cumsum(my_gaps) + jnp.cumsum(my_counts) - my_counts
    token_index = seq_index * tokens_dev + jnp.arange(tokens_dev, dtype=jnp.int32)
    image_pos = jnp.where(
        token_index[None, :] < my_counts[:, None], starts[:, None] + token_index[None, :], FAR
    ).reshape(-1)
    span_rows = text_kv.shape[1]
    positions = seq_index * span_rows + jnp.arange(span_rows, dtype=jnp.int32)
    inside = jnp.any(
        (positions[None, :] >= starts[:, None])
        & (positions[None, :] < (starts + my_counts)[:, None]),
        axis=0,
    )
    text_pos = jnp.where(inside, FAR, positions)
    span_keys = jnp.concatenate([text_kv[0], mine], axis=0)
    span_pos = jnp.concatenate([text_pos, image_pos])
    cache_block = cache_kv.shape[1]
    span_block = span_keys.shape[0]
    kv_heads = kv_width // (2 * HD)
    group_size = QH // KVH
    query_rows = queries[0].reshape(span_rows, kv_heads, group_size, HD)
    scale = 1.0 / math.sqrt(HD)

    def key_block(state, block_keys, block_pos):
        split = block_keys.reshape(block_keys.shape[0], kv_heads, 2, HD)
        scores = (
            jnp.einsum(
                "qhgd,khd->qhgk", query_rows, split[:, :, 0], preferred_element_type=jnp.float32
            )
            * scale
        )
        visible = None
        if block_pos is not None:
            visible = (block_pos[None, :] <= positions[:, None])[:, None, None, :]
        highest, factor, denom, weights = fold_scores(state, scores, visible)
        accum = state[2] * factor[..., None] + jnp.einsum(
            "qhgk,khd->qhgd", weights, split[:, :, 1], preferred_element_type=jnp.float32
        )
        return (highest, denom, accum)

    def over_blocks(state, block_rows, keys, key_pos):
        block_count = keys.shape[0] // block_rows
        shaped = keys.reshape(block_count, block_rows, kv_width)
        if key_pos is None:

            def step_cache(carry, block_keys):
                return (key_block(carry, block_keys, None), 0)

            state, unused = lax.scan(step_cache, state, shaped)
        else:

            def step_span(carry, packed):
                return (key_block(carry, packed[0], packed[1]), 0)

            state, unused = lax.scan(
                step_span, state, (shaped, key_pos.reshape(block_count, block_rows))
            )
        return state

    prompt_init = (
        jnp.full((span_rows, kv_heads, group_size), NEG, jnp.float32),
        jnp.zeros((span_rows, kv_heads, group_size), jnp.float32),
        jnp.zeros((span_rows, kv_heads, group_size, HD), jnp.float32),
    )
    state = prompt_init
    cache_piece = lax.all_gather(cache_kv[0], "seq", axis=0, tiled=True)
    span_piece = lax.all_gather(span_keys, "seq", axis=0, tiled=True)
    span_piece_pos = lax.all_gather(span_pos, "seq", axis=0, tiled=True)
    state = over_blocks(state, cache_block, cache_piece, None)
    final_state = over_blocks(state, span_block, span_piece, span_piece_pos)
    result = (final_state[2] / final_state[1][..., None]).astype(jnp.bfloat16)
    return result.reshape(1, span_rows, kv_heads * group_size * HD)


def solution(mesh):
    in_specs = (
        P("enc", "seq", None),
        P(),
        P(),
        P(),
        P(),
        P(),
        P("enc", "tp"),
        P(("tp", "enc"), None),
        P("enc", "tp"),
        P("enc", "seq", "tp"),
        P("enc", "seq", "tp"),
        P("enc", "seq", "tp"),
    )
    out_specs = P("enc", "seq", "tp")
    return jax.shard_map(
        per_device, mesh=mesh, in_specs=in_specs, out_specs=out_specs, check_vma=False
    )
```

profile of v0, /device:TPU:8, one launch (start us, length us, event | category | flops | bytes accessed | tf_op | source)
XLA Modules:
  0.0 378.4 jit_solution(4055389284735872357)
XLA Ops:
  6.5 0.7 all-gather.7.cloned.1.call-update
  7.3 1.1 fusion.29
  8.5 1.1 fusion.31
  9.7 76.5 %all-gather.7.cloned.1.call-done = bf16[1280,960]{1,0:T(8,128)(2,1)} async-done(((bf16[80,960]{1,0:T(8,128)(2,1)}), bf16[1280,960]{1,0:T(8,128)(2,1)}) %all-gather.7.cloned.1.call-update) | async-done | bytes 2457616 | tf_op jit(solution)/shard_map/all_gather | solution.py:55
  86.1 2.8 convolution_convert_fusion.2
  89.1 0.7 reshape.263
  90.3 0.8 copy.74
  91.1 0.7 all-gather.13.cloned.1.call-update
  92.1 35.2 %all-gather.1 = bf16[16,20,1280]{2,1,0:T(8,128)(2,1)S(1)} all-gather(bf16[1,20,1280]{2,1,0:T(8,128)(2,1)S(1)} %bitcast.211), channel_id=1, replica_groups=mesh['enc'=16,'seq'=8,'tp'=4] {'enc'}, dimensions={0}, use_global_device_ids=true | all-gather | bytes 870400 | tf_op jit(solution)/shard_map/all_gather | solution.py:56
  127.9 2.9 all-gather.9.cloned.1.call-done
  130.8 2.6 copy.75
  134.7 1.1 convolution_convert_fusion
  135.8 0.5 all-gather.11.cloned.1.call-update
  137.7 1.2 dynamic-slice
  139.6 11.9 %all-reduce = s32[1280]{0:T(1024)S(1)} all-reduce(s32[1280]{0:T(1024)S(1)} %add_dynamic-update-slice_fusion), channel_id=1, replica_groups=mesh['enc'=16,'seq'=8,'tp'=4] {'seq'}, use_global_device_ids=true, to_apply=%add | all-reduce | flops 1280 | bytes 10240
  151.7 22.9 %all-gather.13.cloned.1.call-done = bf16[1,3072,256]{2,1,0:T(8,128)(2,1)} async-done(((bf16[1,384,256]{2,1,0:T(8,128)(2,1)}), bf16[1,3072,256]{2,1,0:T(8,128)(2,1)}) %all-gather.13.cloned.1.call-update) | async-done | bytes 1572880 | tf_op jit(solution)/shard_map/all_gather | solution.py:178
  174.6 18.4 %while.31 = (s32[]{:T(128)}, f32[128,1,8]{0,2,1:T(8,128)S(1)}, f32[128,1,8]{0,2,1:T(8,128)S(1)}, f32[128,1,8,128]{0,3,2,1:T(8,128)S(1)}, bf16[8,384,256]{2,1,0:T...) while((s32[]{:T(128)}, f32[128,1,8]{0,2,1:T(8,128)S(1)}, ...), condition=%wide.region_3.4_spmd.clone, body=%wide.region_0.3_spmd.clone.sunk | while | flops 204085248 | bytes 7077997 | solution.py:161
  174.6 1.0 constant_dynamic-slice_fusion.8
  176.4 0.5 fusion.70
  176.9 0.9 constant_dynamic-slice_fusion.8
  178.0 0.4 bitcast_reduce_fusion.2
  178.7 0.5 fusion.70
  179.2 0.9 constant_dynamic-slice_fusion.8
  180.3 0.4 bitcast_reduce_fusion.2
  181.0 0.5 fusion.70
  181.5 0.9 constant_dynamic-slice_fusion.8
  182.6 0.4 bitcast_reduce_fusion.2
  183.3 0.5 fusion.70
  183.8 0.9 constant_dynamic-slice_fusion.8
  184.9 0.4 bitcast_reduce_fusion.2
  185.6 0.5 fusion.70
  186.1 0.9 constant_dynamic-slice_fusion.8
  187.2 0.4 bitcast_reduce_fusion.2
  187.9 0.5 fusion.70
  188.4 0.9 constant_dynamic-slice_fusion.8
  189.5 0.4 bitcast_reduce_fusion.2
  190.2 0.5 fusion.70
  190.7 0.9 constant_dynamic-slice_fusion.8
  192.5 0.5 fusion.70
  192.9 36.0 %all-reduce.3.cloned.1.call-done = bf16[128,1280]{1,0:T(8,128)(2,1)} async-done(((bf16[128,1280]{1,0:T(8,128)(2,1)}), bf16[128,1280]{1,0:T(8,128)(2,1)}) %all-reduce.3.cloned.1.call-update) | async-done | bytes 327696 | tf_op jit(solution)/shard_map/psum | solution.py:91
  229.0 1.2 multiply_reduce_fusion
  230.2 1.1 multiply_convert_fusion
  231.5 72.1 %all-gather.11.cloned.1.call-done = bf16[5120,256]{1,0:T(8,128)(2,1)} async-done(((bf16[320,256]{1,0:T(8,128)(2,1)}), bf16[5120,256]{1,0:T(8,128)(2,1)}) %all-gather.11.cloned.1.call-update) | async-done | bytes 2621456 | tf_op jit(solution)/shard_map/all_gather | solution.py:57
  303.6 2.3 fusion.28
  305.9 28.1 %all_gather.30 = bf16[64,8,256]{2,1,0:T(8,128)(2,1)S(1)} all-gather(bf16[4,8,256]{2,1,0:T(8,128)(2,1)S(1)} %fusion.28), channel_id=1, replica_groups=mesh['enc'=16,'seq'=8,'tp'=4] {'enc'}, dimensions={0}, use_global_device_ids=true | all-gather | bytes 278528 | tf_op jit(solution)/shard_map/all_gather | solution.py:100
  334.3 27.7 %all_gather.31 = bf16[1280,256]{1,0:T(8,128)(2,1)S(1)} all-gather(bf16[160,256]{1,0:T(8,128)(2,1)S(1)} %pad_maximum_fusion), channel_id=1, replica_groups=mesh['enc'=16,'seq'=8,'tp'=4] {'seq'}, dimensions={0}, use_global_device_ids=true | all-gather | bytes 737280 | tf_op jit(solution)/shard_map/all_gather | solution.py:179
  362.0 9.0 %while.30 = (s32[]{:T(128)}, f32[128,1,8]{0,2,1:T(8,128)S(1)}, f32[128,1,8]{0,2,1:T(8,128)S(1)}, f32[128,1,8,128]{0,3,2,1:T(8,128)S(1)}, s32[8,160]{1,0:T(8,128)...) while((s32[]{:T(128)}, f32[128,1,8]{0,2,1:T(8,128)S(1)}, ...), condition=%wide.region_16.17_spmd.clone, body=%wide.region_13.16_spmd.clone.sunk | while | flops 85646464 | bytes 4000753 | solution.py:167
  371.0 0.9 copy.84
  (207 shorter events, 17.3 us)
Async XLA Ops:
  6.5 79.6 %all-gather.7.cloned.1.call-start = ((), (), s32[]{:S(2)}) async-start(), calls=%async_computation | async-start | bytes 2785280 | tf_op jit(solution)/shard_map/all_gather | solution.py:55
  7.3 123.5 %all-gather.9.cloned.1.call-start = ((), (), s32[]{:S(2)}) async-start(), calls=%async_computation.1 | async-start | bytes 1474560 | tf_op jit(solution)/shard_map/all_gather | solution.py:77
  89.0 2.9 copy-start.5
  89.0 3.1 copy-start.3
  91.1 36.4 %copy-start.7 = (s32[64]{0:T(128)S(1)}, s32[64]{0:T(128)}, u32[]{:S(2)}) copy-start(s32[64]{0:T(128)} %param.19) | copy-start | bytes 772
  91.1 83.5 %all-gather.13.cloned.1.call-start = ((), (), s32[]{:S(2)}) async-start(), calls=%async_computation.4 | async-start | bytes 1769472 | tf_op jit(solution)/shard_map/all_gather | solution.py:178
  91.8 137.2 %all-reduce.3.cloned.1.call-start = ((), (), s32[]{:S(2)}) async-start(), calls=%async_computation.2 | async-start | bytes 655360 | tf_op jit(solution)/shard_map/psum | solution.py:91
  134.5 2.0 copy-start.1
  134.5 2.3 copy-start.6
  135.8 167.8 %all-gather.11.cloned.1.call-start = ((), (), s32[]{:S(2)}) async-start(), calls=%async_computation.3 | async-start | bytes 2785280 | tf_op jit(solution)/shard_map/all_gather | solution.py:57
  174.6 54.4 %copy-start = (bf16[4,32,1280]{2,1,0:T(8,128)(2,1)S(1)}, bf16[4,32,1280]{2,1,0:T(8,128)(2,1)}, u32[]{:S(2)}) copy-start(bf16[4,32,1280]{2,1,0:T(8,128)(2,1)} %param.16) | copy-start | bytes 983044
  174.6 55.6 %copy-start.4 = (f32[1280]{0:T(1024)S(1)}, f32[1280]{0:T(1024)}, u32[]{:S(2)}) copy-start(f32[1280]{0:T(1024)} %param.21) | copy-start | bytes 15364
  231.5 102.8 %copy-start.2 = (bf16[1,128,256]{2,1,0:T(8,128)(2,1)S(1)}, bf16[1,128,256]{2,1,0:T(8,128)(2,1)}, u32[]{:S(2)}) copy-start(bf16[1,128,256]{2,1,0:T(8,128)(2,1)} %param.26) | copy-start | bytes 196612
Sparse Core Ops, SparseCore 0:
  10.6 75.4 all-gather.6
  91.2 39.5 all-gather.8
  132.9 41.6 all-gather.12
  177.4 51.5 all-reduce.2
  232.1 71.4 all-gather.10
where the time goes:
time: 379 us; the launch traced here: 378 us
  waiting for transfers between devices  212 us (56%)
  blocking collectives  103 us (27%)
  local copies, waits for them, and re-layouts  19 us (5%)
  matrix products  19 us (5%)
  between operations  14 us (4%)
  other arithmetic  9.69 us (3%)
    all_gather x1, waiting for transfers between devices, per_device(): lax.all_gather(w_qkv, 'enc', axis=0, tiled=True)  76.5 us
    all_gather x1, waiting for transfers between devices, per_device(): lax.all_gather(kv_merge, 'enc', axis=0, tiled=True)  72.1 us
    psum x1, waiting for transfers between devices, per_device(): lax.psum(partial_value.astype(jnp.bfloat16), 'tp').astype(jnp.float32)  36 us
    all_gather x1, blocking collectives, per_device(): lax.all_gather(w_out, 'enc', axis=0, tiled=True)  35.2 us
    all_gather x1, blocking collectives, per_device(): every_image = lax.all_gather(image_kv, 'enc', axis=0, tiled=True)  28.1 us
    all_gather x1, blocking collectives, per_device(): span_piece = lax.all_gather(span_keys, 'seq', axis=0, tiled=True)  27.7 us
    all_gather x1, waiting for transfers between devices, per_device(): cache_piece = lax.all_gather(cache_kv[0], 'seq', axis=0, tiled=True)  22.9 us
    unnamed x1, blocking collectives  11.9 us
  transfers between devices with their start and end apart: 5, of which 5 were waited for; matrix products, arithmetic and copies ran while one was open for 8% of the time, Pallas kernels for 0%

commit v1 on v0

v1 whole, which is shorter than its diff:
```python
import math

import jax
import jax.numpy as jnp
from jax import lax
from jax.experimental import pallas as pl
from jax.experimental.pallas import tpu as pltpu
from jax.sharding import Mesh
from jax.sharding import PartitionSpec as P

VD = 1280
VHD = 80
MERGE = 4
HD = 128
GROUP = 8
IMG_ENC = 4
SLOT = 256
TOK = SLOT // MERGE
IMG_TOTAL = 160
SPAN = 1024
CACHE = 3072

EPS = 1e-06
FAR = 1 << 30
NEG = -1e30
LOG2E = math.log2(math.e)

ENC = ("x", "yh", "core")
SEQ = ("j", "h")
VMEM = pl.BlockSpec(memory_space=pltpu.VMEM)
SMEM = pl.BlockSpec(memory_space=pltpu.SMEM)
ANY = pl.BlockSpec(memory_space=pl.ANY)


def params(mib=48):
    return pltpu.CompilerParams(vmem_limit_bytes=mib << 20)


def swap(value, axis):
    return lax.ppermute(value, axis, [(0, 1), (1, 0)])


def rms_scale(values, gain):
    return values * lax.rsqrt(jnp.mean(values * values, axis=-1, keepdims=True) + EPS) * gain


def vision_kernel(ids, tokens, slots, patches, gain, own, other, out, weight):
    core, slot = ids[2], ids[3]
    for piece in range(8):
        weight[pl.ds(pl.multiple_of((piece * 2 + core) * 80, 16), 80), 0:480] = own[piece]
        weight[pl.ds(pl.multiple_of((piece * 2 + 1 - core) * 80, 16), 80), 0:480] = other[piece]
    count = jnp.int32(0)
    for i in range(slots.shape[0]):
        count = jnp.where(slots[i] == slot, tokens[i // IMG_ENC, i % IMG_ENC], count)
    rows = patches[...].reshape(SLOT, VD).astype(jnp.float32)
    normed = rms_scale(rows, gain[...]).astype(jnp.bfloat16)
    qkv = jnp.dot(normed, weight[...], preferred_element_type=jnp.float32)
    flipped = jnp.transpose(qkv).astype(jnp.bfloat16)
    live = lax.broadcasted_iota(jnp.int32, (SLOT, SLOT), 0) < MERGE * count
    for head in range(2):
        base = head * 3 * VHD
        keys = qkv[:, base + VHD : base + 2 * VHD].astype(jnp.bfloat16)
        scores = jnp.dot(
            keys, flipped[base : base + VHD], preferred_element_type=jnp.float32
        ) * (1.0 / math.sqrt(VHD))
        scores = jnp.where(live, scores, NEG)
        weights = jnp.exp(scores - jnp.max(scores, axis=0, keepdims=True))
        denom = jnp.sum(weights, axis=0, keepdims=True)
        attended = jnp.dot(
            flipped[base + 2 * VHD : base + 3 * VHD],
            weights.astype(jnp.bfloat16),
            preferred_element_type=jnp.float32,
        )
        attended = (attended / denom).astype(jnp.bfloat16)
        for peer in range(out.shape[0]):
            out[peer, head * VHD : (head + 1) * VHD, :] = attended


def merge_kernel(attended, w_out, patches, gain, kv_merge, out, merged):
    residual = patches[...].reshape(SLOT, VD).astype(jnp.float32) + lax.dot_general(
        attended[...].reshape(VD, SLOT),
        w_out[...],
        (((0,), (0,)), ((), ())),
        preferred_element_type=jnp.float32,
    )
    residual = rms_scale(residual, gain[...])
    for c in range(VD // 128):
        merged[c] = residual[:, c * 128 : (c + 1) * 128]
    total = jnp.zeros((TOK, HD), jnp.float32)
    for r in range(MERGE):
        part = [merged[c, pl.ds(r, TOK, stride=MERGE), :] for c in range(VD // 128)]
        part = jnp.concatenate(part, axis=1).astype(jnp.bfloat16)
        total += jnp.dot(
            part, kv_merge[r * VD : (r + 1) * VD, :], preferred_element_type=jnp.float32
        )
    total = total.astype(jnp.bfloat16)
    for peer in range(out.shape[0]):
        out[peer] = total


def select_kernel(ids, tokens, slots, images, out):
    prompt, plane = ids[0], ids[1]
    shape = (IMG_TOTAL, images.shape[0] * TOK)
    row = lax.broadcasted_iota(jnp.int32, shape, 0)
    column = lax.broadcasted_iota(jnp.int32, shape, 1)
    wanted = jnp.full(shape, -1, jnp.int32)
    begin = jnp.int32(0)
    for k in range(IMG_ENC):
        slot = slots[prompt * IMG_ENC + k]
        count = tokens[prompt, k]
        base = jnp.where(slot % IMG_ENC == plane, (slot // IMG_ENC) * TOK - begin, -FAR)
        inside = (row >= begin) & (row < begin + count)
        wanted = jnp.where(inside, row + base, wanted)
        begin = begin + count
    selector = (column == wanted).astype(jnp.bfloat16)
    packed = jnp.dot(
        selector, images[...].reshape(shape[1], HD), preferred_element_type=jnp.float32
    ).astype(jnp.bfloat16)
    for peer in range(out.shape[0]):
        out[peer] = packed


def stack_queries(queries, stacked):
    for g in range(GROUP):
        stacked[g * 128 : (g + 1) * 128, :] = queries[0, :, g * HD : (g + 1) * HD]


def text_kernel(ids, tokens, gaps, queries, cached, after, out, top_out, sum_out, stacked, top, accum):
    del after
    prompt, seq = ids[0], ids[4]
    stack_queries(queries, stacked)
    rows = GROUP * 128
    factor = LOG2E / math.sqrt(HD)
    begin = jnp.int32(0)
    spans = []
    for k in range(IMG_ENC):
        begin = begin + gaps[prompt, k]
        spans.append((begin, begin + tokens[prompt, k]))
        begin = begin + tokens[prompt, k]
    top[...] = jnp.full((rows, 1), NEG, jnp.float32)
    accum[...] = jnp.zeros((rows, HD), jnp.float32)
    total = jnp.zeros((rows, 1), jnp.float32)

    def block(keys, values, visible, total):
        scores = lax.dot_general(
            stacked[...], keys, (((1,), (1,)), ((), ())), preferred_element_type=jnp.float32
        )
        if visible is not None:
            scores = jnp.where(visible, scores, NEG)
        highest = jnp.maximum(top[...], jnp.max(scores, axis=-1, keepdims=True))
        scale = jnp.exp2((top[...] - highest) * factor)
        weights = jnp.exp2((scores - highest) * factor)
        top[...] = highest
        accum[...] = accum[...] * scale + jnp.dot(
            weights.astype(jnp.bfloat16), values, preferred_element_type=jnp.float32
        )
        return total * scale + jnp.sum(weights, axis=-1, keepdims=True)

    for z in range(8):
        total = block(cached[z, 0:384, 0:HD], cached[z, 0:384, HD:], None, total)
    for part in range(4):
        base = part * 256
        position = base + lax.broadcasted_iota(jnp.int32, (1, 256), 1)
        for low, high in spans:
            inside = (position >= low) & (position < high)
            position = jnp.where(inside, FAR, position)
        query = seq * 128 + lax.broadcasted_iota(jnp.int32, (rows, 1), 0) % 128
        keys = cached[2 * part : 2 * part + 2, 384:512, 0:HD].reshape(256, HD)
        values = cached[2 * part : 2 * part + 2, 384:512, HD:].reshape(256, HD)
        total = block(keys, values, position <= query, total)
    out[...] = accum[...]
    top_out[...] = top[...]
    sum_out[...] = total


def join_kernel(ids, tokens, gaps, queries, images, accum, top, total, out, stacked):
    prompt, seq = ids[0], ids[4]
    stack_queries(queries, stacked)
    rows = GROUP * 128
    factor = LOG2E / math.sqrt(HD)
    keys = (images[0] + images[2]) + (images[4] + images[6])
    values = (images[1] + images[3]) + (images[5] + images[7])
    index = lax.broadcasted_iota(jnp.int32, (1, IMG_TOTAL), 1)
    position = jnp.full((1, IMG_TOTAL), FAR, jnp.int32)
    shift = jnp.int32(0)
    begin = jnp.int32(0)
    for k in range(IMG_ENC):
        shift = shift + gaps[prompt, k]
        position = jnp.where(index >= begin, index + shift, position)
        begin = begin + tokens[prompt, k]
    query = seq * 128 + lax.broadcasted_iota(jnp.int32, (rows, 1), 0) % 128
    scores = lax.dot_general(
        stacked[...], keys, (((1,), (1,)), ((), ())), preferred_element_type=jnp.float32
    )
    scores = jnp.where(position <= query, scores, NEG)
    highest = jnp.maximum(top[...], jnp.max(scores, axis=-1, keepdims=True))
    scale = jnp.exp2((top[...] - highest) * factor)
    weights = jnp.exp2((scores - highest) * factor)
    denom = total[...] * scale + jnp.sum(weights, axis=-1, keepdims=True)
    joined = accum[...] * scale + jnp.dot(
        weights.astype(jnp.bfloat16), values, preferred_element_type=jnp.float32
    )
    joined = (joined / denom).astype(jnp.bfloat16)
    for g in range(GROUP):
        out[0, :, g * HD : (g + 1) * HD] = joined[g * 128 : (g + 1) * 128, :]


def per_device(
    patches,
    image_tokens,
    image_gap,
    image_slot,
    norm_gain,
    merge_gain,
    w_qkv,
    w_out,
    kv_merge,
    queries,
    text_kv,
    cache_kv,
):
    x, yh, core = (lax.axis_index(a) for a in ENC)
    plane, half = lax.axis_index("j"), lax.axis_index("h")
    enc = (x * 2 + yh) * 2 + core
    ids = jnp.stack([enc, plane, core, enc * IMG_ENC + plane, plane * 2 + half]).astype(jnp.int32)
    bf16, f32 = jnp.bfloat16, jnp.float32

    mine = lax.dynamic_slice_in_dim(w_qkv, half * 480, 480, axis=1)
    both = jnp.stack([mine, swap(mine, "yh")])
    both = jnp.where(yh == 0, both, both[::-1])
    along = lax.all_to_all(jnp.broadcast_to(both[None], (4, 2, 80, 480)), "x", 0, 0)
    own = along.reshape(8, 80, 480)
    other = swap(own, "core")

    sent = jnp.broadcast_to(patches[:, None], (4, 2, 32, VD)).reshape(8, 32, VD)
    image = lax.all_to_all(sent, SEQ, 0, 0)

    group = lax.all_to_all(jnp.broadcast_to(w_out[None], (4, 20, VD)), "tp", 0, 0)
    pair = jnp.stack([group, swap(group, "yh")])
    pair = jnp.where(yh == 0, pair, pair[::-1])
    pair = lax.all_to_all(jnp.broadcast_to(pair[None], (4, 2, 4, 20, VD)), "x", 0, 0)
    cores = jnp.stack([pair, swap(pair, "core")])
    cores = jnp.where(core == 0, cores, cores[::-1])
    out_weight = jnp.transpose(cores, (3, 1, 2, 0, 4, 5)).reshape(VD, VD)

    columns = lax.dynamic_slice_in_dim(kv_merge, half * HD, HD, axis=1)
    merge_weight = lax.all_gather(columns, ENC, axis=0, tiled=True)

    past = jnp.concatenate([cache_kv[0], text_kv[0]], axis=0)
    past = lax.all_to_all(jnp.broadcast_to(past[None], (8, 512, 2 * HD)), SEQ, 0, 0)

    attended = pl.pallas_call(
        vision_kernel,
        out_shape=jax.ShapeDtypeStruct((8, 2 * VHD, SLOT), bf16),
        in_specs=[SMEM] * 3 + [VMEM] * 4,
        out_specs=VMEM,
        scratch_shapes=[pltpu.VMEM((VD, 512), bf16)],
        compiler_params=params(),
        cost_estimate=pl.CostEstimate(flops=400_000_000, bytes_accessed=4_000_000, transcendentals=131072),
        name="vision",
    )(ids, image_tokens, image_slot, image, norm_gain.reshape(1, VD), own, other)
    attended = lax.all_to_all(attended, ("tp", "h"), 0, 0)

    image_kv = pl.pallas_call(
        merge_kernel,
        out_shape=jax.ShapeDtypeStruct((16, TOK, HD), bf16),
        in_specs=[VMEM] * 5,
        out_specs=VMEM,
        scratch_shapes=[pltpu.VMEM((VD // 128, SLOT, 128), f32)],
        compiler_params=params(),
        cost_estimate=pl.CostEstimate(flops=1_000_000_000, bytes_accessed=8_000_000, transcendentals=256),
        name="merge",
    )(attended, out_weight, image, merge_gain.reshape(1, VD), merge_weight)
    every = lax.all_to_all(image_kv, ENC, 0, 0)

    rows = GROUP * 128
    accum, top, total = pl.pallas_call(
        text_kernel,
        out_shape=(
            jax.ShapeDtypeStruct((rows, HD), f32),
            jax.ShapeDtypeStruct((rows, 1), f32),
            jax.ShapeDtypeStruct((rows, 1), f32),
        ),
        in_specs=[SMEM] * 3 + [VMEM] * 2 + [ANY],
        out_specs=(VMEM, VMEM, VMEM),
        scratch_shapes=[
            pltpu.VMEM((rows, HD), bf16),
            pltpu.VMEM((rows, 1), f32),
            pltpu.VMEM((rows, HD), f32),
        ],
        compiler_params=params(),
        cost_estimate=pl.CostEstimate(
            flops=2_200_000_000, bytes_accessed=4_000_000, transcendentals=rows * 4096
        ),
        name="text",
    )(ids, image_tokens, image_gap, queries, past, image_kv)

    packed = pl.pallas_call(
        select_kernel,
        out_shape=jax.ShapeDtypeStruct((8, IMG_TOTAL, HD), bf16),
        in_specs=[SMEM] * 3 + [VMEM],
        out_specs=VMEM,
        compiler_params=params(),
        cost_estimate=pl.CostEstimate(flops=42_000_000, bytes_accessed=600_000, transcendentals=0),
        name="select",
    )(ids, image_tokens, image_slot, every)
    images = lax.all_to_all(packed, SEQ, 0, 0)

    return pl.pallas_call(
        join_kernel,
        out_shape=jax.ShapeDtypeStruct((1, 128, GROUP * HD), bf16),
        in_specs=[SMEM] * 3 + [VMEM] * 5,
        out_specs=VMEM,
        scratch_shapes=[pltpu.VMEM((rows, HD), bf16)],
        compiler_params=params(),
        cost_estimate=pl.CostEstimate(
            flops=84_000_000, bytes_accessed=2_000_000, transcendentals=rows * 160
        ),
        name="join",
    )(ids, image_tokens, image_gap, queries, images, accum, top, total)


def solution(mesh):
    fine = Mesh(
        mesh.devices.reshape(4, 2, 2, 4, 2, 4), ("x", "yh", "core", "j", "h", "tp")
    )
    in_specs = (
        P(ENC, SEQ, None),
        P(),
        P(),
        P(),
        P(),
        P(),
        P(ENC, "tp"),
        P(("tp",) + ENC, None),
        P(ENC, "tp"),
        P(ENC, SEQ, "tp"),
        P(ENC, SEQ, "tp"),
        P(ENC, SEQ, "tp"),
    )
    return jax.shard_map(
        per_device, mesh=fine, in_specs=in_specs, out_specs=P(ENC, SEQ, "tp"), check_vma=False
    )
```

time: 379 us -> 265 us (0.70)
  the two profiles are of different devices: /device:TPU:8 before, /device:TPU:16 now
where the time goes in v1:
time: 265 us; the launch traced here: 264 us
  waiting for transfers between devices  124 us (47%)
  starting transfers between devices  52.1 us (20%)
  Pallas kernels  30.9 us (12%)
  local copies, waits for them, and re-layouts  22.9 us (9%)
  between operations  13.7 us (5%)
  blocking collectives  13 us (5%)
  other arithmetic  6.99 us (3%)
    all_to_all x1, waiting for transfers between devices, per_device(): lax.all_to_all(jnp.broadcast_to(past[None], (8, 512, 2 * HD)), SEQ, 0, 0)  49.7 us
    pallas_call x1, Pallas kernels, per_device(): pl.pallas_call(text_kernel, out_shape=(jax.ShapeDtypeStruct((rows, HD), f...  18.8 us
    ppermute x4, waiting for transfers between devices, swap(): return lax.ppermute(value, axis, [(0, 1), (1, 0)])  15.9 us
    all_to_all x1, waiting for transfers between devices, per_device(): image = lax.all_to_all(sent, SEQ, 0, 0)  15.6 us
    all_to_all x1, waiting for transfers between devices, per_device(): every = lax.all_to_all(image_kv, ENC, 0, 0)  13.8 us
    ppermute x4, starting transfers between devices, swap(): return lax.ppermute(value, axis, [(0, 1), (1, 0)])  13.2 us
    all_to_all x1, blocking collectives, per_device(): lax.all_to_all(jnp.broadcast_to(w_out[None], (4, 20, VD)), 'tp', 0, 0)  13 us
    all_to_all x1, starting transfers between devices, per_device(): image = lax.all_to_all(sent, SEQ, 0, 0)  10.7 us
  transfers between devices with their start and end apart: 12, of which 9 were waited for; matrix products, arithmetic and copies ran while one was open for 6% of the time, Pallas kernels for 9%

profile of v1, /device:TPU:16, one launch (start us, length us, event | category | flops | bytes accessed | tf_op | source)
XLA Modules:
  0.0 263.6 jit_solution(11659796129439865004)
XLA Ops:
  6.5 0.9 broadcast_in_dim.12
  7.4 13.0 %all_to_all.40 = bf16[4,20,1280]{2,1,0:T(8,128)(2,1)S(1)} all-to-all(bf16[4,20,1280]{2,1,0:T(8,128)(2,1)S(1)} %broadcast_in_dim.12), channel_id=1, replica_groups=mesh['x'=4,'yh'=2,'core'=2,'j'=4,'h'=2,'tp'=4] {'tp'}, dimensions={0} | all-to-all | bytes 409600 | tf_op jit(solution)/shard_map/all_to_all | solution.py:238
  20.4 3.6 %collective-permute-start.2 = (bf16[4,20,1280]{2,1,0:T(8,128)(2,1)S(1)}, bf16[4,20,1280]{2,1,0:T(8,128)(2,1)S(1)}, u32[]{:S(2)}, u32[]{:S(2)}) collective-permute-start(bf16[4,20,1280]{2,1,0:T(8,128)(2,1)S(1)} %all_to_all.40), channel_id=1, source_target_pairs={{0,64},{64,0},{1,65},{65,1},{2,66},{66,2},{3,67},{67,3},{4,68},{68... | collective-permute-start | bytes 614408 | tf_op jit(solution)/shard_map/ppermute | solution.py:40
  24.0 10.7 %collective-permute-done.2 = bf16[4,20,1280]{2,1,0:T(8,128)(2,1)S(1)} collective-permute-done((bf16[4,20,1280]{2,1,0:T(8,128)(2,1)S(1)}, bf16[4,20,1280]{2,1,0:T(8,128)(2,1)S(1)}, u32[]{:S(2)}, u32[]{:S(2)}) %collective-permute-start.2) | collective-permute-done | bytes 204832 | tf_op jit(solution)/shard_map/ppermute | solution.py:40
  34.8 0.2 copy.37
  35.0 1.6 broadcast_in_dim.13
  36.6 6.1 %all-to-all-start.4 = ((bf16[4,2,4,20,1280]{4,2,3,1,0:T(4,128)(2,1)}), bf16[4,2,4,20,1280]{4,2,3,1,0:T(4,128)(2,1)}, u32[]{:S(2)}, u32[]{:S(2)}) async-start(bf16[4,2,4,20,1280]{4,2,3,1,0:T(4,128)(2,1)} %broadcast_in_dim.13), calls=%async_computation.4 | async-start | bytes 3276800 | tf_op jit(solution)/shard_map/all_to_all | solution.py:241
  42.8 5.8 %collective-permute-start = (bf16[80,480]{1,0:T(8,128)(2,1)S(1)}, bf16[80,480]{1,0:T(8,128)(2,1)S(1)}, u32[]{:S(2)}, u32[]{:S(2)}) collective-permute-start(bf16[80,480]{1,0:T(8,128)(2,1)S(1)} %constant_dynamic-slice_fusion.1), channel_id=1, source_target_pairs={{0,64},{64,0},{1,65},{65,1},{2,66},{66,2},{3,67},{67,3},{4,68},{68... | collective-permute-start | bytes 230408 | tf_op jit(solution)/shard_map/ppermute | solution.py:40
  48.6 0.1 fusion.1
  48.7 5.2 %collective-permute-done = bf16[80,480]{1,0:T(8,128)(2,1)S(1)} collective-permute-done((bf16[80,480]{1,0:T(8,128)(2,1)S(1)}, bf16[80,480]{1,0:T(8,128)(2,1)S(1)}, u32[]{:S(2)}, u32[]{:S(2)}) %collective-permute-start) | collective-permute-done | bytes 76832 | tf_op jit(solution)/shard_map/ppermute | solution.py:40
  54.0 9.9 %all-to-all-done.4 = bf16[4,2,4,20,1280]{4,2,3,1,0:T(4,128)(2,1)} async-done(((bf16[4,2,4,20,1280]{4,2,3,1,0:T(4,128)(2,1)}), bf16[4,2,4,20,1280]{4,2,3,1,0:T(4,128)(2,1)}, u32[]{:S(2)}, u32[]{:S(2)}) %all-to-all-start.4) | async-done | bytes 1638432 | tf_op jit(solution)/shard_map/all_to_all | solution.py:241
  63.8 0.9 broadcast_in_dim.11
  64.7 3.5 %all-to-all-start.1 = ((bf16[4,2,80,480]{3,2,1,0:T(8,128)(2,1)}), bf16[4,2,80,480]{3,2,1,0:T(8,128)(2,1)S(1)}, u32[]{:S(2)}, u32[]{:S(2)}) async-start(bf16[4,2,80,480]{3,2,1,0:T(8,128)(2,1)} %broadcast_in_dim.11), calls=%async_computation.1 | async-start | bytes 1310720 | tf_op jit(solution)/shard_map/all_to_all | solution.py:231
  68.2 1.9 collective-permute-start.3
  70.2 0.6 constant_dynamic-slice_fusion
  70.9 6.9 %all-to-all-done.1 = bf16[4,2,80,480]{3,2,1,0:T(8,128)(2,1)S(1)} async-done(((bf16[4,2,80,480]{3,2,1,0:T(8,128)(2,1)}), bf16[4,2,80,480]{3,2,1,0:T(8,128)(2,1)S(1)}, u32[]{:S(2)}, u32[]{:S(2)}) %all-to-all-start.1) | async-done | bytes 614432 | tf_op jit(solution)/shard_map/all_to_all | solution.py:231
  77.8 0.9 broadcast_in_dim.10
  78.7 10.7 %all-to-all-start = ((bf16[8,32,1280]{2,1,0:T(8,128)(2,1)}), bf16[8,32,1280]{2,1,0:T(8,128)(2,1)S(1)}, u32[]{:S(2)}, u32[]{:S(2)}) async-start(bf16[8,32,1280]{2,1,0:T(8,128)(2,1)} %bitcast.5), calls=%async_computation | async-start | bytes 1310720 | tf_op jit(solution)/shard_map/all_to_all | solution.py:236
  89.4 1.9 collective-permute-start.1
  91.5 15.6 %all-to-all-done.patches = bf16[8,32,1280]{2,1,0:T(8,128)(2,1)S(1)} async-done(((bf16[8,32,1280]{2,1,0:T(8,128)(2,1)}), bf16[8,32,1280]{2,1,0:T(8,128)(2,1)S(1)}, u32[]{:S(2)}, u32[]{:S(2)}) %all-to-all-start) | async-done | bytes 655392 | tf_op jit(solution)/shard_map/all_to_all | solution.py:236
  107.2 3.0 %vision.1 = bf16[8,160,256]{2,1,0:T(8,128)(2,1)} custom-call(s32[5]{0:T(128)S(1)} %stack.50.ids, s32[16,4]{1,0:T(8,128)S(1)} %copy.42.tokens, s32[64]{0:T(128)S(1)} %copy-done.12, bf16[8,32,1280]{2,1,0:T(8,128)(2,1)S(1)} %all-to-all-done.patches, f32[1,1280]{1,0:T(1,128)S(1)} %reshape.21.gain, bf16[8,80,480]{2,1,0:T(8,128)(2,1)S(1)} %bitcast.19, ...), custom_call_target="tpu_custom_call" | custom-call | flops 400000000 | bytes 4000000 | tf_op jit(solution)/shard_map/vision/pallas_call | solution.py:252
  110.2 4.2 %all-to-all-start.2 = ((bf16[8,160,256]{2,1,0:T(8,128)(2,1)}), bf16[8,160,256]{2,1,0:T(8,128)(2,1)}, u32[]{:S(2)}, u32[]{:S(2)}) async-start(bf16[8,160,256]{2,1,0:T(8,128)(2,1)} %vision.1), calls=%async_computation.2 | async-start | bytes 1310720 | tf_op jit(solution)/shard_map/all_to_all | solution.py:262
  114.4 4.4 %pad_maximum_fusion = bf16[2,4,2,4,20,1280]{5,3,4,2,1,0:T(4,128)(2,1)S(1)} fusion(bf16[1,4,2,4,20,1280]{5,3,4,2,1,0:T(4,128)(2,1)} %bitcast.12, bf16[1,4,2,4,20,1280]{5,3,4,2,1,0:T(4,128)(2,1)} %bitcast.11), kind=kLoop, calls=%fused_computation.2 | loop fusion | flops 1638400 | bytes 6553600 | tf_op jit(solution)/shard_map/stack | solution.py:242
  118.8 1.5 fusion
  120.3 2.5 copy.38
  122.8 4.7 %reshape.23.w_out = bf16[1280,1280]{1,0:T(8,128)(2,1)S(1)} reshape(bf16[4,4,2,2,20,1280]{5,4,3,2,1,0:T(8,128)(2,1)} %copy.38) | data formatting | bytes 6553600 | tf_op jit(solution)/shard_map/reshape | solution.py:244
  127.5 5.8 %all-to-all-done.2.attended = bf16[8,160,256]{2,1,0:T(8,128)(2,1)} async-done(((bf16[8,160,256]{2,1,0:T(8,128)(2,1)}), bf16[8,160,256]{2,1,0:T(8,128)(2,1)}, u32[]{:S(2)}, u32[]{:S(2)}) %all-to-all-start.2) | async-done | bytes 655392 | tf_op jit(solution)/shard_map/all_to_all | solution.py:262
  133.3 6.4 %all-gather.2.cloned.1.call-done.kv_merge = bf16[5120,128]{1,0:T(8,128)(2,1)} async-done(((bf16[320,128]{1,0:T(8,128)(2,1)}), bf16[5120,128]{1,0:T(8,128)(2,1)}) %all-gather.2.cloned.1.call-update) | async-done | bytes 1310736 | tf_op jit(solution)/shard_map/all_gather | solution.py:247
  139.7 1.1 copy-done.2
  140.7 1.3 copy-done.3
  142.1 2.9 %merge.1.after = bf16[16,64,128]{2,1,0:T(8,128)(2,1)S(1)} custom-call(bf16[8,160,256]{2,1,0:T(8,128)(2,1)} %all-to-all-done.2.attended, bf16[1280,1280]{1,0:T(8,128)(2,1)S(1)} %reshape.23.w_out, bf16[8,32,1280]{2,1,0:T(8,128)(2,1)S(1)} %copy-done.2, f32[1,1280]{1,0:T(1,128)S(1)} %reshape.24.gain, bf16[5120,128]{1,0:T(8,128)(2,1)S(1)} %copy-done.3), custom_call_target="tpu_custom_call" | custom-call | flops 1000000000 | bytes 8000000 | tf_op jit(solution)/shard_map/merge/pallas_call | solution.py:264
  145.0 0.7 copy-done.4
  145.7 4.8 %all-to-all-start.5 = ((bf16[16,64,128]{2,1,0:T(8,128)(2,1)}), bf16[16,64,128]{2,1,0:T(8,128)(2,1)S(1)}, u32[]{:S(2)}, u32[]{:S(2)}) async-start(bf16[16,64,128]{2,1,0:T(8,128)(2,1)} %copy-done.4), calls=%async_computation.5 | async-start | bytes 524288 | tf_op jit(solution)/shard_map/all_to_all | solution.py:274
  150.5 0.9 pad_maximum_fusion.2
  151.4 13.8 %all-to-all-done.5.images = bf16[16,64,128]{2,1,0:T(8,128)(2,1)S(1)} async-done(((bf16[16,64,128]{2,1,0:T(8,128)(2,1)}), bf16[16,64,128]{2,1,0:T(8,128)(2,1)S(1)}, u32[]{:S(2)}, u32[]{:S(2)}) %all-to-all-start.5) | async-done | bytes 262176 | tf_op jit(solution)/shard_map/all_to_all | solution.py:274
  165.2 1.5 broadcast_in_dim.14
  166.7 6.0 %all-to-all-start.7 = ((bf16[8,512,256]{2,1,0:T(8,128)(2,1)}), bf16[8,512,256]{2,1,0:T(8,128)(2,1)S(1)}, u32[]{:S(2)}, u32[]{:S(2)}) async-start(bf16[8,512,256]{2,1,0:T(8,128)(2,1)} %broadcast_in_dim.14), calls=%async_computation.7 | async-start | bytes 4194304 | tf_op jit(solution)/shard_map/all_to_all | solution.py:250
  172.7 1.7 select.1
  174.5 49.7 %all-to-all-done.7.cached = bf16[8,512,256]{2,1,0:T(8,128)(2,1)S(1)} async-done(((bf16[8,512,256]{2,1,0:T(8,128)(2,1)}), bf16[8,512,256]{2,1,0:T(8,128)(2,1)S(1)}, u32[]{:S(2)}, u32[]{:S(2)}) %all-to-all-start.7) | async-done | bytes 2097184 | tf_op jit(solution)/shard_map/all_to_all | solution.py:250
  224.2 3.6 %all-to-all-start.6 = ((bf16[8,160,128]{2,1,0:T(8,128)(2,1)}), bf16[8,160,128]{2,1,0:T(8,128)(2,1)S(1)}, u32[]{:S(2)}, u32[]{:S(2)}) async-start(bf16[8,160,128]{2,1,0:T(8,128)(2,1)} %select.1), calls=%async_computation.6 | async-start | bytes 655360 | tf_op jit(solution)/shard_map/all_to_all | solution.py:307
  227.9 0.9 copy-done.10
  228.8 18.8 %text.1 = (f32[1024,128]{1,0:T(8,128)S(1)}, f32[1024,1]{1,0:T(8,128)S(1)}, f32[1024,1]{1,0:T(8,128)S(1)}) custom-call(s32[5]{0:T(128)S(1)} %stack.50.ids, s32[16,4]{1,0:T(8,128)S(1)} %copy.42.tokens, s32[16,4]{1,0:T(8,128)S(1)} %copy.43.gaps, bf16[1,128,1024]{2,1,0:T(8,128)(2,1)S(1)} %copy-done.10, bf16[8,512,256]{2,1,0:T(8,128)(2,1)S(1)} %all-to-all-done.7.cached, ...), custom_call_target="tpu_custom_call" | custom-call | flops 2200000000 | bytes 4000000 | tf_op jit(solution)/shard_map/text/pallas_call | solution.py:277
  247.6 0.8 copy-done.6
  248.4 0.8 copy-done.8
  249.2 1.0 copy-done.7
  250.3 1.0 copy-done.9
  251.3 0.9 copy-done.11
  252.3 4.5 %join.1 = bf16[1,128,1024]{2,1,0:T(8,128)(2,1)} custom-call(s32[5]{0:T(128)S(1)} %stack.50.ids, s32[16,4]{1,0:T(8,128)S(1)} %copy.42.tokens, s32[16,4]{1,0:T(8,128)S(1)} %copy.43.gaps, bf16[1,128,1024]{2,1,0:T(8,128)(2,1)S(1)} %copy-done.11, bf16[8,160,128]{2,1,0:T(8,128)(2,1)S(1)} %all-to-all-done.6.images, f32[1024,128]{1,0:T(8,128)S(1)} %get-tuple-element.8.accum, ...), custom_call_target="tpu_custom_call" | custom-call | flops 84000000 | bytes 2000000 | tf_op jit(solution)/shard_map/join/pallas_call | solution.py:309
  (46 shorter events, 0.7 us)
Async XLA Ops:
  6.5 36.1 %copy-start = (bf16[80,960]{1,0:T(8,128)(2,1)S(1)}, bf16[80,960]{1,0:T(8,128)(2,1)}, u32[]{:S(2)}) copy-start(bf16[80,960]{1,0:T(8,128)(2,1)} %param.18) | copy-start | bytes 460804
  20.4 14.3 %collective-permute-start.2 = (bf16[4,20,1280]{2,1,0:T(8,128)(2,1)S(1)}, bf16[4,20,1280]{2,1,0:T(8,128)(2,1)S(1)}, u32[]{:S(2)}, u32[]{:S(2)}) collective-permute-start(bf16[4,20,1280]{2,1,0:T(8,128)(2,1)S(1)} %all_to_all.40), channel_id=1, source_target_pairs={{0,64},{64,0},{1,65},{65,1},{2,66},{66,2},{3,67},{67,3},{4,68},{68... | collective-permute-start | bytes 614408 | tf_op jit(solution)/shard_map/ppermute | solution.py:40
  36.6 33.6 %copy-start.15 = (bf16[320,256]{1,0:T(8,128)(2,1)S(1)}, bf16[320,256]{1,0:T(8,128)(2,1)}, u32[]{:S(2)}) copy-start(bf16[320,256]{1,0:T(8,128)(2,1)} %param.20) | copy-start | bytes 491524
  36.6 41.2 %copy-start.13 = (bf16[4,32,1280]{2,1,0:T(8,128)(2,1)S(1)}, bf16[4,32,1280]{2,1,0:T(8,128)(2,1)}, u32[]{:S(2)}) copy-start(bf16[4,32,1280]{2,1,0:T(8,128)(2,1)} %param.12) | copy-start | bytes 983044
  36.6 27.2 %all-to-all-start.4 = ((bf16[4,2,4,20,1280]{4,2,3,1,0:T(4,128)(2,1)}), bf16[4,2,4,20,1280]{4,2,3,1,0:T(4,128)(2,1)}, u32[]{:S(2)}, u32[]{:S(2)}) async-start(bf16[4,2,4,20,1280]{4,2,3,1,0:T(4,128)(2,1)} %broadcast_in_dim.13), calls=%async_computation.4 | async-start | bytes 3276800 | tf_op jit(solution)/shard_map/all_to_all | solution.py:241
  42.6 48.7 %copy-start.18 = (s32[16,4]{0,1:T(4,128)S(1)}, s32[16,4]{0,1:T(4,128)}, u32[]{:S(2)}) copy-start(s32[16,4]{0,1:T(4,128)} %param.13) | copy-start | bytes 772
  42.6 48.8 %copy-start.16 = (f32[1280]{0:T(1024)S(1)}, f32[1280]{0:T(1024)}, u32[]{:S(2)}) copy-start(f32[1280]{0:T(1024)} %param.16) | copy-start | bytes 15364
  42.6 48.8 %copy-start.17 = (f32[1280]{0:T(1024)S(1)}, f32[1280]{0:T(1024)}, u32[]{:S(2)}) copy-start(f32[1280]{0:T(1024)} %param.17) | copy-start | bytes 15364
  42.7 64.5 %copy-start.12 = (s32[64]{0:T(128)S(1)}, s32[64]{0:T(128)}, u32[]{:S(2)}) copy-start(s32[64]{0:T(128)} %slots.3) | copy-start | bytes 772
  42.8 11.1 %collective-permute-start = (bf16[80,480]{1,0:T(8,128)(2,1)S(1)}, bf16[80,480]{1,0:T(8,128)(2,1)S(1)}, u32[]{:S(2)}, u32[]{:S(2)}) collective-permute-start(bf16[80,480]{1,0:T(8,128)(2,1)S(1)} %constant_dynamic-slice_fusion.1), channel_id=1, source_target_pairs={{0,64},{64,0},{1,65},{65,1},{2,66},{66,2},{3,67},{67,3},{4,68},{68... | collective-permute-start | bytes 230408 | tf_op jit(solution)/shard_map/ppermute | solution.py:40
  64.7 13.1 %all-to-all-start.1 = ((bf16[4,2,80,480]{3,2,1,0:T(8,128)(2,1)}), bf16[4,2,80,480]{3,2,1,0:T(8,128)(2,1)S(1)}, u32[]{:S(2)}, u32[]{:S(2)}) async-start(bf16[4,2,80,480]{3,2,1,0:T(8,128)(2,1)} %broadcast_in_dim.11), calls=%async_computation.1 | async-start | bytes 1310720 | tf_op jit(solution)/shard_map/all_to_all | solution.py:231
  68.2 71.5 %all-gather.2.cloned.1.call-start = ((), (), s32[]{:S(2)}) async-start(), calls=%async_computation.8 | async-start | bytes 1392640 | tf_op jit(solution)/shard_map/all_gather | solution.py:247
  68.2 46.2 %collective-permute-start.3 = (bf16[4,2,4,20,1280]{4,2,3,1,0:T(4,128)(2,1)}, bf16[4,2,4,20,1280]{4,2,3,1,0:T(4,128)(2,1)}, u32[]{:S(2)}, u32[]{:S(2)}) collective-permute-start(bf16[4,2,4,20,1280]{4,2,3,1,0:T(4,128)(2,1)} %all-to-all-done.4), channel_id=1, source_target_pairs={{0,32},{32,0},{1,33},{33,1},{2,34},{34,2},{3,35},{35,3},{4,36},{36... | collective-permute-start | bytes 4915208 | tf_op jit(solution)/shard_map/ppermute | solution.py:40
  78.7 28.5 %all-to-all-start = ((bf16[8,32,1280]{2,1,0:T(8,128)(2,1)}), bf16[8,32,1280]{2,1,0:T(8,128)(2,1)S(1)}, u32[]{:S(2)}, u32[]{:S(2)}) async-start(bf16[8,32,1280]{2,1,0:T(8,128)(2,1)} %bitcast.5), calls=%async_computation | async-start | bytes 1310720 | tf_op jit(solution)/shard_map/all_to_all | solution.py:236
  89.4 17.8 %collective-permute-start.1 = (bf16[8,80,480]{2,1,0:T(8,128)(2,1)S(1)}, bf16[8,80,480]{2,1,0:T(8,128)(2,1)S(1)}, u32[]{:S(2)}, u32[]{:S(2)}) collective-permute-start(bf16[8,80,480]{2,1,0:T(8,128)(2,1)S(1)} %bitcast.18), channel_id=1, source_target_pairs={{0,32},{32,0},{1,33},{33,1},{2,34},{34,2},{3,35},{35,3},{4,36},{36... | collective-permute-start | bytes 1843208 | tf_op jit(solution)/shard_map/ppermute | solution.py:40
  107.2 11.6 %copy-start.1 = (bf16[8,32,1280]{2,1,0:T(8,128)(2,1)}, bf16[8,32,1280]{2,1,0:T(8,128)(2,1)S(1)}, u32[]{:S(2)}) copy-start(bf16[8,32,1280]{2,1,0:T(8,128)(2,1)S(1)} %all-to-all-done.patches) | copy-start | bytes 1966084
  110.2 23.1 %all-to-all-start.2 = ((bf16[8,160,256]{2,1,0:T(8,128)(2,1)}), bf16[8,160,256]{2,1,0:T(8,128)(2,1)}, u32[]{:S(2)}, u32[]{:S(2)}) async-start(bf16[8,160,256]{2,1,0:T(8,128)(2,1)} %vision.1), calls=%async_computation.2 | async-start | bytes 1310720 | tf_op jit(solution)/shard_map/all_to_all | solution.py:262
  122.8 27.7 %copy-start.14 = (bf16[1,128,256]{2,1,0:T(8,128)(2,1)S(1)}, bf16[1,128,256]{2,1,0:T(8,128)(2,1)}, u32[]{:S(2)}) copy-start(bf16[1,128,256]{2,1,0:T(8,128)(2,1)} %param.22) | copy-start | bytes 196612
  139.7 1.1 copy-start.2
  140.7 1.3 copy-start.3
  144.9 0.7 copy-start.4
  145.7 19.6 %all-to-all-start.5 = ((bf16[16,64,128]{2,1,0:T(8,128)(2,1)}), bf16[16,64,128]{2,1,0:T(8,128)(2,1)S(1)}, u32[]{:S(2)}, u32[]{:S(2)}) async-start(bf16[16,64,128]{2,1,0:T(8,128)(2,1)} %copy-done.4), calls=%async_computation.5 | async-start | bytes 524288 | tf_op jit(solution)/shard_map/all_to_all | solution.py:274
  166.7 61.1 %copy-start.19 = (s32[16,4]{0,1:T(4,128)S(1)}, s32[16,4]{0,1:T(4,128)}, u32[]{:S(2)}) copy-start(s32[16,4]{0,1:T(4,128)} %param.14) | copy-start | bytes 772
  166.7 61.2 %copy-start.5 = (bf16[16,64,128]{2,1,0:T(8,128)(2,1)S(1)}, bf16[16,64,128]{2,1,0:T(8,128)(2,1)}, u32[]{:S(2)}) copy-start(bf16[16,64,128]{2,1,0:T(8,128)(2,1)} %copy-done.4) | copy-start | bytes 786436
  166.7 57.4 %all-to-all-start.7 = ((bf16[8,512,256]{2,1,0:T(8,128)(2,1)}), bf16[8,512,256]{2,1,0:T(8,128)(2,1)S(1)}, u32[]{:S(2)}, u32[]{:S(2)}) async-start(bf16[8,512,256]{2,1,0:T(8,128)(2,1)} %broadcast_in_dim.14), calls=%async_computation.7 | async-start | bytes 4194304 | tf_op jit(solution)/shard_map/all_to_all | solution.py:250
  224.2 25.1 %all-to-all-start.6 = ((bf16[8,160,128]{2,1,0:T(8,128)(2,1)}), bf16[8,160,128]{2,1,0:T(8,128)(2,1)S(1)}, u32[]{:S(2)}, u32[]{:S(2)}) async-start(bf16[8,160,128]{2,1,0:T(8,128)(2,1)} %select.1), calls=%async_computation.6 | async-start | bytes 655360 | tf_op jit(solution)/shard_map/all_to_all | solution.py:307
  227.9 1.0 copy-start.10
  247.6 0.8 copy-start.6
  248.4 0.8 copy-start.8
  249.2 1.0 copy-start.7
  250.3 1.0 copy-start.9
  251.3 0.9 copy-start.11
Sparse Core Ops, SparseCore 0:
  72.3 67.3 all-gather.1

commit v2 on v1

v2 whole, which is shorter than its diff:
```python
import math

import jax
import jax.numpy as jnp
from jax import lax
from jax.experimental import pallas as pl
from jax.experimental.pallas import tpu as pltpu
from jax.sharding import Mesh
from jax.sharding import PartitionSpec as P

VD = 1280
VHD = 80
MERGE = 4
HD = 128
GROUP = 8
IMG_ENC = 4
SLOT = 256
TOK = SLOT // MERGE
IMG_TOTAL = 160
SPAN = 1024
CACHE = 3072

EPS = 1e-06
FAR = 1 << 30
NEG = -1e30
LOG2E = math.log2(math.e)

ENC = ("x", "yh", "core")
SEQ = ("j", "h")
VMEM = pl.BlockSpec(memory_space=pltpu.VMEM)
SMEM = pl.BlockSpec(memory_space=pltpu.SMEM)
ANY = pl.BlockSpec(memory_space=pl.ANY)


def params(mib=48):
    return pltpu.CompilerParams(vmem_limit_bytes=mib << 20)


def swap(value, axis):
    return lax.ppermute(value, axis, [(0, 1), (1, 0)])


def rms_scale(values, gain):
    return values * lax.rsqrt(jnp.mean(values * values, axis=-1, keepdims=True) + EPS) * gain


def pack_heads_kernel(w_qkv, w_out, out, lines):
    first = jnp.where(lax.axis_index("h") == 0, w_qkv[:, 0:480], w_qkv[:, 480:960])
    for c in range(4):
        size = min(128, 480 - c * 128)
        out[c * 80 : (c + 1) * 80, 0:size] = first[:, c * 128 : c * 128 + size]
    out[240:320, 96:128] = jnp.zeros((80, 32), jnp.bfloat16)
    lines[200:208, :] = jnp.zeros((8, 128), jnp.float32)
    rows = w_out[...].astype(jnp.float32)
    for c in range(10):
        lines[pl.ds(c, 20, stride=10), :] = rows[:, c * 128 : (c + 1) * 128]
    out[320:528, :] = lines[...].astype(jnp.bfloat16)


def pack_merge_kernel(kv_merge, after, out):
    del after
    out[...] = jnp.where(lax.axis_index("h") == 0, kv_merge[:, 0:HD], kv_merge[:, HD:])


def vision_kernel(tokens, slots, patches, gain, own, other, out, weight, lines, rows_out, mixed):
    core, yh, half = lax.axis_index("core"), lax.axis_index("yh"), lax.axis_index("h")
    slot = ((lax.axis_index("x") * 2 + yh) * 2 + core) * IMG_ENC + lax.axis_index("j")
    for x in range(4):
        for rel in range(2):
            for c in range(4):
                base = x * 4 + (yh ^ rel) * 2
                tile = pl.ds(c * 128, 128)
                weight[pl.ds(pl.multiple_of((base + core) * 80, 16), 80), tile] = own[
                    x, rel, c * 80 : (c + 1) * 80, :
                ]
                weight[pl.ds(pl.multiple_of((base + 1 - core) * 80, 16), 80), tile] = other[
                    x, rel, c * 80 : (c + 1) * 80, :
                ]
    rows_out[...] = jnp.zeros(rows_out.shape, jnp.float32)
    for head in range(2):
        for rel in range(2):
            for part, piece in enumerate((own, other)):
                base = head * 128 + (rel * 2 + part) * 32
                lines[...] = piece[half * 2 + head, rel, 320:528, :].astype(jnp.float32)
                for c in range(10):
                    rows_out[base : base + 20, c * 128 : (c + 1) * 128] = lines[
                        pl.ds(c, 20, stride=10), :
                    ]
    row = lax.broadcasted_iota(jnp.int32, (128, VHD), 0)
    column = lax.broadcasted_iota(jnp.int32, (128, VHD), 1)
    wanted = ((row // 32) ^ (yh * 2 + core)) * 20 + row % 32
    order = ((column == wanted) & (row % 32 < 20)).astype(jnp.bfloat16)
    count = jnp.int32(0)
    for i in range(slots.shape[0]):
        count = jnp.where(slots[i] == slot, tokens[i // IMG_ENC, i % IMG_ENC], count)
    rows = patches[...].reshape(SLOT, VD).astype(jnp.float32)
    normed = rms_scale(rows, gain[...]).astype(jnp.bfloat16)
    qkv = jnp.dot(normed, weight[...], preferred_element_type=jnp.float32)
    flipped = jnp.transpose(qkv).astype(jnp.bfloat16)
    live = lax.broadcasted_iota(jnp.int32, (SLOT, SLOT), 0) < MERGE * count
    for head in range(2):
        base = head * 3 * VHD
        keys = qkv[:, base + VHD : base + 2 * VHD].astype(jnp.bfloat16)
        scores = jnp.dot(
            keys, flipped[base : base + VHD], preferred_element_type=jnp.float32
        ) * (1.0 / math.sqrt(VHD))
        scores = jnp.where(live, scores, NEG)
        weights = jnp.exp(scores - jnp.max(scores, axis=0, keepdims=True))
        denom = jnp.sum(weights, axis=0, keepdims=True)
        attended = jnp.dot(
            flipped[base + 2 * VHD : base + 3 * VHD],
            weights.astype(jnp.bfloat16),
            preferred_element_type=jnp.float32,
        )
        attended = (attended / denom).astype(jnp.bfloat16)
        mixed[head * 128 : (head + 1) * 128, :] = jnp.dot(
            order, attended, preferred_element_type=jnp.float32
        ).astype(jnp.bfloat16)
    partial = lax.dot_general(
        mixed[...],
        rows_out[...].astype(jnp.bfloat16),
        (((0,), (0,)), ((), ())),
        preferred_element_type=jnp.float32,
    ).astype(jnp.bfloat16)
    out[...] = partial.reshape(out.shape)


def norm_kernel(parts, patches, gain, out):
    total = patches[lax.axis_index("tp") * 2 + lax.axis_index("h")].astype(jnp.float32)
    for peer in range(8):
        total += parts[peer].astype(jnp.float32)
    total = rms_scale(total, gain[...]).astype(jnp.bfloat16)
    for peer in range(8):
        out[peer] = total


def merge_kernel(rows, own, other, out, merged, weight):
    core, yh = lax.axis_index("core"), lax.axis_index("yh")
    for x in range(4):
        for rel in range(2):
            base = x * 4 + (yh ^ rel) * 2
            weight[pl.ds(pl.multiple_of((base + core) * 320, 16), 320), :] = own[x, rel]
            weight[pl.ds(pl.multiple_of((base + 1 - core) * 320, 16), 320), :] = other[x, rel]
    normed = rows[...].reshape(SLOT, VD).astype(jnp.float32)
    for c in range(VD // 128):
        merged[c] = normed[:, c * 128 : (c + 1) * 128]
    total = jnp.zeros((TOK, HD), jnp.float32)
    for r in range(MERGE):
        part = [merged[c, pl.ds(r, TOK, stride=MERGE), :] for c in range(VD // 128)]
        part = jnp.concatenate(part, axis=1).astype(jnp.bfloat16)
        total += jnp.dot(
            part, weight[r * VD : (r + 1) * VD, :], preferred_element_type=jnp.float32
        )
    total = total.astype(jnp.bfloat16)
    for peer in range(out.shape[0]):
        out[peer] = total


def prompt_index():
    return (lax.axis_index("x") * 2 + lax.axis_index("yh")) * 2 + lax.axis_index("core")


def query_positions():
    seq = lax.axis_index("j") * 2 + lax.axis_index("h")
    return seq * 128 + lax.broadcasted_iota(jnp.int32, (1, GROUP * 128), 1) % 128


def select_kernel(tokens, slots, images, after, out):
    del after
    prompt, plane = prompt_index(), lax.axis_index("j")
    shape = (IMG_TOTAL, images.shape[0] * TOK)
    row = lax.broadcasted_iota(jnp.int32, shape, 0)
    column = lax.broadcasted_iota(jnp.int32, shape, 1)
    wanted = jnp.full(shape, -1, jnp.int32)
    begin = jnp.int32(0)
    for k in range(IMG_ENC):
        slot = slots[prompt * IMG_ENC + k]
        count = tokens[prompt, k]
        base = jnp.where(slot % IMG_ENC == plane, (slot // IMG_ENC) * TOK - begin, -FAR)
        inside = (row >= begin) & (row < begin + count)
        wanted = jnp.where(inside, row + base, wanted)
        begin = begin + count
    selector = (column == wanted).astype(jnp.bfloat16)
    packed = jnp.dot(
        selector, images[...].reshape(shape[1], HD), preferred_element_type=jnp.float32
    ).astype(jnp.bfloat16)
    for peer in range(out.shape[0]):
        out[peer] = packed


def text_kernel(tokens, gaps, queries, cached, after, out, top_out, sum_out, flipped):
    del after
    prompt = prompt_index()
    for g in range(GROUP):
        block = queries[0, :, g * HD : (g + 1) * HD].astype(jnp.float32)
        flipped[:, g * 128 : (g + 1) * 128] = jnp.transpose(block).astype(jnp.bfloat16)
    factor = LOG2E / math.sqrt(HD)
    begin = jnp.int32(0)
    spans = []
    for k in range(IMG_ENC):
        begin = begin + gaps[prompt, k]
        spans.append((begin, begin + tokens[prompt, k]))
        begin = begin + tokens[prompt, k]
    top = jnp.full((1, GROUP * 128), NEG, jnp.float32)
    total = jnp.zeros((1, GROUP * 128), jnp.float32)
    out[...] = jnp.zeros(out.shape, jnp.float32)
    query = query_positions()
    for part in range(6):
        if part < 4:
            size = 768
            window = cached[2 * part : 2 * part + 2, 0:384, :].reshape(size, 2 * HD)
        else:
            size = 512
            window = cached[4 * part - 16 : 4 * part - 12, 384:512, :].reshape(size, 2 * HD)
        scores = jnp.dot(window[:, 0:HD], flipped[...], preferred_element_type=jnp.float32)
        if part >= 4:
            position = (part - 4) * size + lax.broadcasted_iota(jnp.int32, (size, 1), 0)
            for low, high in spans:
                position = jnp.where((position >= low) & (position < high), FAR, position)
            scores = jnp.where(position <= query, scores, NEG)
        highest = jnp.maximum(top, jnp.max(scores, axis=0, keepdims=True))
        scale = jnp.exp2((top - highest) * factor)
        weights = jnp.exp2((scores - highest) * factor)
        top = highest
        total = total * scale + jnp.sum(weights, axis=0, keepdims=True)
        out[...] = out[...] * scale + lax.dot_general(
            window[:, HD:],
            weights.astype(jnp.bfloat16),
            (((0,), (0,)), ((), ())),
            preferred_element_type=jnp.float32,
        )
    top_out[...] = top
    sum_out[...] = total


def join_kernel(tokens, gaps, images, flipped, accum, top, total, out):
    prompt = prompt_index()
    factor = LOG2E / math.sqrt(HD)
    keys = (images[0] + images[2]) + (images[4] + images[6])
    values = (images[1] + images[3]) + (images[5] + images[7])
    index = lax.broadcasted_iota(jnp.int32, (IMG_TOTAL, 1), 0)
    position = index
    begin = jnp.int32(0)
    for k in range(IMG_ENC):
        position = position + jnp.where(index >= begin, gaps[prompt, k], 0)
        begin = begin + tokens[prompt, k]
    scores = jnp.dot(keys, flipped[...], preferred_element_type=jnp.float32)
    scores = jnp.where(position <= query_positions(), scores, NEG)
    highest = jnp.maximum(top[...], jnp.max(scores, axis=0, keepdims=True))
    scale = jnp.exp2((top[...] - highest) * factor)
    weights = jnp.exp2((scores - highest) * factor)
    denom = total[...] * scale + jnp.sum(weights, axis=0, keepdims=True)
    joined = accum[...] * scale + lax.dot_general(
        values,
        weights.astype(jnp.bfloat16),
        (((0,), (0,)), ((), ())),
        preferred_element_type=jnp.float32,
    )
    joined = joined / denom
    for g in range(GROUP):
        block = jnp.transpose(joined[:, g * 128 : (g + 1) * 128])
        out[0, :, g * HD : (g + 1) * HD] = block.astype(jnp.bfloat16)


def per_device(
    patches,
    image_tokens,
    image_gap,
    image_slot,
    norm_gain,
    merge_gain,
    w_qkv,
    w_out,
    kv_merge,
    queries,
    text_kv,
    cache_kv,
):
    bf16, f32 = jnp.bfloat16, jnp.float32
    lanes = GROUP * 128

    def spread(value):
        both = jnp.stack([value, swap(value, "yh")])
        own = lax.all_to_all(jnp.broadcast_to(both[None], (4,) + both.shape), "x", 0, 0)
        return own, swap(own, "core")

    def call(kernel, name, out_shape, in_specs, scratch=(), cost=(0, 0, 0)):
        return pl.pallas_call(
            kernel,
            out_shape=out_shape,
            in_specs=in_specs,
            out_specs=jax.tree.map(lambda leaf: VMEM, out_shape),
            scratch_shapes=scratch,
            compiler_params=params(),
            cost_estimate=pl.CostEstimate(
                flops=cost[0], bytes_accessed=cost[1], transcendentals=cost[2]
            ),
            name=name,
        )

    def array(shape, dtype=bf16):
        return jax.ShapeDtypeStruct(shape, dtype)

    past = jnp.concatenate([cache_kv[0], text_kv[0]], axis=0)
    past = lax.all_gather(past, SEQ, axis=0)

    heads = call(
        pack_heads_kernel,
        "pack_heads",
        array((528, 128)),
        [VMEM] * 2,
        [pltpu.VMEM((208, 128), f32)],
        (1_000_000, 400_000, 0),
    )(w_qkv, w_out)
    own, other = spread(heads)

    sent = jnp.broadcast_to(patches[:, None], (4, 2, 32, VD)).reshape(8, 32, VD)
    image = lax.all_to_all(sent, SEQ, 0, 0)

    parts = call(
        vision_kernel,
        "vision",
        array((8, 32, VD)),
        [SMEM] * 2 + [VMEM] * 4,
        [
            pltpu.VMEM((VD, 512), bf16),
            pltpu.VMEM((208, 128), f32),
            pltpu.VMEM((256, VD), f32),
            pltpu.VMEM((256, SLOT), bf16),
        ],
        (600_000_000, 5_000_000, 131072),
    )(image_tokens, image_slot, image, norm_gain.reshape(1, VD), own, other)
    parts = lax.all_to_all(parts, ("tp", "h"), 0, 0)

    columns = call(
        pack_merge_kernel, "pack_merge", array((320, 128)), [VMEM, ANY], (), (0, 300_000, 0)
    )(kv_merge, other)
    merge_own, merge_other = spread(columns)

    rows = call(
        norm_kernel, "norm", array((8, 32, VD)), [VMEM] * 3, (), (1_000_000, 2_000_000, 32)
    )(parts, image, merge_gain.reshape(1, VD))
    rows = lax.all_to_all(rows, ("tp", "h"), 0, 0)

    image_kv = call(
        merge_kernel,
        "merge",
        array((16, TOK, HD)),
        [VMEM] * 3,
        [pltpu.VMEM((VD // 128, SLOT, 128), f32), pltpu.VMEM((MERGE * VD, HD), bf16)],
        (84_000_000, 3_000_000, 0),
    )(rows, merge_own, merge_other)
    every = lax.all_to_all(image_kv, ENC, 0, 0)

    accum, top, total, flipped = call(
        text_kernel,
        "text",
        (array((HD, lanes), f32), array((1, lanes), f32), array((1, lanes), f32), array((HD, lanes))),
        [SMEM] * 2 + [VMEM] * 2 + [ANY],
        (),
        (2_200_000_000, 4_000_000, lanes * 4096),
    )(image_tokens, image_gap, queries, past, image_kv)

    packed = call(
        select_kernel,
        "select",
        array((8, IMG_TOTAL, HD)),
        [SMEM] * 2 + [VMEM, ANY],
        (),
        (42_000_000, 600_000, 0),
    )(image_tokens, image_slot, every, total)
    images = lax.all_to_all(packed, SEQ, 0, 0)

    return call(
        join_kernel,
        "join",
        array((1, 128, lanes)),
        [SMEM] * 2 + [VMEM] * 5,
        (),
        (84_000_000, 2_000_000, lanes * 160),
    )(image_tokens, image_gap, images, flipped, accum, top, total)


def solution(mesh):
    fine = Mesh(
        mesh.devices.reshape(4, 2, 2, 4, 2, 4), ("x", "yh", "core", "j", "h", "tp")
    )
    in_specs = (
        P(ENC, SEQ, None),
        P(),
        P(),
        P(),
        P(),
        P(),
        P(ENC, "tp"),
        P(("tp",) + ENC, None),
        P(ENC, "tp"),
        P(ENC, SEQ, "tp"),
        P(ENC, SEQ, "tp"),
        P(ENC, SEQ, "tp"),
    )
    return jax.shard_map(
        per_device, mesh=fine, in_specs=in_specs, out_specs=P(ENC, SEQ, "tp"), check_vma=False
    )
```

time: 265 us -> 177 us (0.67)
  the two profiles are of different devices: /device:TPU:16 before, /device:TPU:8 now
where the time goes in v2:
time: 177 us
  waiting for transfers between devices  57.1 us (32%)
  starting transfers between devices  51.1 us (29%)
  blocking collectives  31.7 us (18%)
  Pallas kernels  16.9 us (10%)
  between operations  13.6 us (8%)
  local copies, waits for them, and re-layouts  5.52 us (3%)
    ppermute x4, waiting for transfers between devices, swap(): return lax.ppermute(value, axis, [(0, 1), (1, 0)])  16.2 us
    all_to_all x1, blocking collectives, spread(): lax.all_to_all(jnp.broadcast_to(both[None], (4,) + both.shape), 'x', 0, 0)  16.1 us
    all_to_all x1, blocking collectives, per_device(): images = lax.all_to_all(packed, SEQ, 0, 0)  15.6 us
    ppermute x4, starting transfers between devices, swap(): return lax.ppermute(value, axis, [(0, 1), (1, 0)])  15.2 us
    all_to_all x1, waiting for transfers between devices, per_device(): image = lax.all_to_all(sent, SEQ, 0, 0)  12.6 us
    all_to_all x1, starting transfers between devices, per_device(): parts = lax.all_to_all(parts, ('tp', 'h'), 0, 0)  11.9 us
    all_to_all x1, starting transfers between devices, per_device(): image = lax.all_to_all(sent, SEQ, 0, 0)  10.4 us
    all_to_all x1, waiting for transfers between devices, per_device(): rows = lax.all_to_all(rows, ('tp', 'h'), 0, 0)  9.6 us
  transfers between devices with their start and end apart: 10, of which 8 were waited for; matrix products, arithmetic and copies ran while one was open for 1% of the time, Pallas kernels for 8%

profile of v2, /device:TPU:8, one launch (start us, length us, event | category | flops | bytes accessed | tf_op | source)
XLA Modules:
  0.0 176.6 jit_solution(7547761213144665754)
XLA Ops:
  6.5 0.9 copy-done
  7.5 0.8 copy-done.2
  8.3 0.1 pack_heads.1
  8.4 6.8 %collective-permute-start = (bf16[528,128]{1,0:T(8,128)(2,1)S(1)}, bf16[528,128]{1,0:T(8,128)(2,1)S(1)}, u32[]{:S(2)}, u32[]{:S(2)}) collective-permute-start(bf16[528,128]{1,0:T(8,128)(2,1)S(1)} %pack_heads.1), channel_id=1, source_target_pairs={{0,64},{64,0},{1,65},{65,1},{2,66},{66,2},{3,67},{67,3},{4,68},{68... | collective-permute-start | bytes 405512 | tf_op jit(solution)/shard_map/ppermute | solution.py:40
  15.2 7.0 %collective-permute-done = bf16[528,128]{1,0:T(8,128)(2,1)S(1)} collective-permute-done((bf16[528,128]{1,0:T(8,128)(2,1)S(1)}, bf16[528,128]{1,0:T(8,128)(2,1)S(1)}, u32[]{:S(2)}, u32[]{:S(2)}) %collective-permute-start) | collective-permute-done | bytes 135200 | tf_op jit(solution)/shard_map/ppermute | solution.py:40
  22.3 0.1 broadcast_in_dim.7
  22.4 0.0 copy-start.6
  22.4 16.1 %all_to_all.35.own = bf16[4,2,528,128]{3,2,1,0:T(8,128)(2,1)S(1)} all-to-all(bf16[4,2,528,128]{3,2,1,0:T(8,128)(2,1)S(1)} %broadcast_in_dim.7), channel_id=1, replica_groups=mesh['x'=4,'yh'=2,'core'=2,'j'=4,'h'=2,'tp'=4] {'x'}, dimensions={0} | all-to-all | bytes 2162688 | tf_op jit(solution)/shard_map/all_to_all | solution.py:284
  38.5 0.0 copy-done.6
  38.5 0.9 broadcast_in_dim.6
  39.4 10.4 %all-to-all-start = ((bf16[8,32,1280]{2,1,0:T(8,128)(2,1)}), bf16[8,32,1280]{2,1,0:T(8,128)(2,1)S(1)}, u32[]{:S(2)}, u32[]{:S(2)}) async-start(bf16[8,32,1280]{2,1,0:T(8,128)(2,1)} %bitcast), calls=%async_computation | async-start | bytes 1310720 | tf_op jit(solution)/shard_map/all_to_all | solution.py:318
  49.9 0.0 all-gather.3.cloned.1.call-start
  49.9 1.9 %collective-permute-start.1 = (bf16[4,2,528,128]{3,2,1,0:T(8,128)(2,1)S(1)}, bf16[4,2,528,128]{3,2,1,0:T(8,128)(2,1)S(1)}, u32[]{:S(2)}, u32[]{:S(2)}) collective-permute-start(bf16[4,2,528,128]{3,2,1,0:T(8,128)(2,1)S(1)} %all_to_all.35.own), channel_id=1, source_target_pairs={{0,32},{32,0},{1,33},{33,1},{2,34},{34,2},{3,35},{35,3},{4,36},{36... | collective-permute-start | bytes 3244040 | tf_op jit(solution)/shard_map/ppermute | solution.py:40
  51.8 0.0 copy-done.7
  51.8 0.0 copy-done.8
  51.9 0.8 pad_maximum_fusion.1
  52.6 0.0 all-gather.3.cloned.1.call-update
  52.6 0.0 copy-done.11
  52.6 0.1 copy.17.tokens
  52.7 0.0 copy-done.9
  52.7 12.6 %all-to-all-done.patches = bf16[8,32,1280]{2,1,0:T(8,128)(2,1)S(1)} async-done(((bf16[8,32,1280]{2,1,0:T(8,128)(2,1)}), bf16[8,32,1280]{2,1,0:T(8,128)(2,1)S(1)}, u32[]{:S(2)}, u32[]{:S(2)}) %all-to-all-start) | async-done | bytes 655392 | tf_op jit(solution)/shard_map/all_to_all | solution.py:318
  65.4 0.0 collective-permute-done.1.other.after
  65.4 0.0 copy-done.3
  65.4 3.7 %vision.1 = bf16[8,32,1280]{2,1,0:T(8,128)(2,1)} custom-call(s32[16,4]{1,0:T(8,128)S(1)} %copy.17.tokens, s32[64]{0:T(128)S(1)} %copy-done.3, bf16[8,32,1280]{2,1,0:T(8,128)(2,1)S(1)} %all-to-all-done.patches, f32[1,1280]{1,0:T(1,128)S(1)} %reshape.13.gain, bf16[4,2,528,128]{3,2,1,0:T(8,128)(2,1)S(1)} %all_to_all.35.own, ...), custom_call_target="tpu_custom_call" | custom-call | flops 600000000 | bytes 5000000 | tf_op jit(solution)/shard_map/vision/pallas_call | solution.py:320
  69.1 11.9 %all-to-all-start.2 = ((bf16[8,32,1280]{2,1,0:T(8,128)(2,1)}), bf16[8,32,1280]{2,1,0:T(8,128)(2,1)S(1)}, u32[]{:S(2)}, u32[]{:S(2)}) async-start(bf16[8,32,1280]{2,1,0:T(8,128)(2,1)} %vision.1), calls=%async_computation.2 | async-start | bytes 1310720 | tf_op jit(solution)/shard_map/all_to_all | solution.py:333
  81.0 0.0 copy-done.1
  81.1 4.4 %collective-permute-start.2 = (bf16[320,128]{1,0:T(8,128)(2,1)S(1)}, bf16[320,128]{1,0:T(8,128)(2,1)S(1)}, u32[]{:S(2)}, u32[]{:S(2)}) collective-permute-start(bf16[320,128]{1,0:T(8,128)(2,1)S(1)} %pack_merge.1), channel_id=1, source_target_pairs={{0,64},{64,0},{1,65},{65,1},{2,66},{66,2},{3,67},{67,3},{4,68},{68... | collective-permute-start | bytes 245768 | tf_op jit(solution)/shard_map/ppermute | solution.py:40
  85.5 7.1 %collective-permute-done.2 = bf16[320,128]{1,0:T(8,128)(2,1)S(1)} collective-permute-done((bf16[320,128]{1,0:T(8,128)(2,1)S(1)}, bf16[320,128]{1,0:T(8,128)(2,1)S(1)}, u32[]{:S(2)}, u32[]{:S(2)}) %collective-permute-start.2) | collective-permute-done | bytes 81952 | tf_op jit(solution)/shard_map/ppermute | solution.py:40
  92.6 0.0 copy-start.10
  92.6 5.5 %all-to-all-done.2.parts = bf16[8,32,1280]{2,1,0:T(8,128)(2,1)S(1)} async-done(((bf16[8,32,1280]{2,1,0:T(8,128)(2,1)}), bf16[8,32,1280]{2,1,0:T(8,128)(2,1)S(1)}, u32[]{:S(2)}, u32[]{:S(2)}) %all-to-all-start.2) | async-done | bytes 655392 | tf_op jit(solution)/shard_map/all_to_all | solution.py:333
  98.1 0.9 broadcast_in_dim.8
  99.1 3.5 %all-to-all-start.4 = ((bf16[4,2,320,128]{3,2,1,0:T(8,128)(2,1)}), bf16[4,2,320,128]{3,2,1,0:T(8,128)(2,1)S(1)}, u32[]{:S(2)}, u32[]{:S(2)}) async-start(bf16[4,2,320,128]{3,2,1,0:T(8,128)(2,1)} %broadcast_in_dim.8), calls=%async_computation.4 | async-start | bytes 1310720 | tf_op jit(solution)/shard_map/all_to_all | solution.py:284
  102.6 0.0 copy-done.10
  102.6 1.1 norm.1
  103.7 7.7 %all-to-all-done.4.own = bf16[4,2,320,128]{3,2,1,0:T(8,128)(2,1)S(1)} async-done(((bf16[4,2,320,128]{3,2,1,0:T(8,128)(2,1)}), bf16[4,2,320,128]{3,2,1,0:T(8,128)(2,1)S(1)}, u32[]{:S(2)}, u32[]{:S(2)}) %all-to-all-start.4) | async-done | bytes 655392 | tf_op jit(solution)/shard_map/all_to_all | solution.py:284
  111.3 6.5 %all-to-all-start.3 = ((bf16[8,32,1280]{2,1,0:T(8,128)(2,1)}), bf16[8,32,1280]{2,1,0:T(8,128)(2,1)S(1)}, u32[]{:S(2)}, u32[]{:S(2)}) async-start(bf16[8,32,1280]{2,1,0:T(8,128)(2,1)} %norm.1), calls=%async_computation.3 | async-start | bytes 1310720 | tf_op jit(solution)/shard_map/all_to_all | solution.py:343
  117.8 2.0 %collective-permute-start.3 = (bf16[4,2,320,128]{3,2,1,0:T(8,128)(2,1)S(1)}, bf16[4,2,320,128]{3,2,1,0:T(8,128)(2,1)S(1)}, u32[]{:S(2)}, u32[]{:S(2)}) collective-permute-start(bf16[4,2,320,128]{3,2,1,0:T(8,128)(2,1)S(1)} %all-to-all-done.4.own), channel_id=1, source_target_pairs={{0,32},{32,0},{1,33},{33,1},{2,34},{34,2},{3,35},{35,3},{4,36},{36... | collective-permute-start | bytes 1966088 | tf_op jit(solution)/shard_map/ppermute | solution.py:40
  119.8 2.1 %collective-permute-done.3.other = bf16[4,2,320,128]{3,2,1,0:T(8,128)(2,1)S(1)} collective-permute-done((bf16[4,2,320,128]{3,2,1,0:T(8,128)(2,1)S(1)}, bf16[4,2,320,128]{3,2,1,0:T(8,128)(2,1)S(1)}, u32[]{:S(2)}, u32[]{:S(2)}) %collective-permute-start.3) | collective-permute-done | bytes 655392 | tf_op jit(solution)/shard_map/ppermute | solution.py:40
  121.9 9.6 %all-to-all-done.3.rows = bf16[8,32,1280]{2,1,0:T(8,128)(2,1)S(1)} async-done(((bf16[8,32,1280]{2,1,0:T(8,128)(2,1)}), bf16[8,32,1280]{2,1,0:T(8,128)(2,1)S(1)}, u32[]{:S(2)}, u32[]{:S(2)}) %all-to-all-start.3) | async-done | bytes 655392 | tf_op jit(solution)/shard_map/all_to_all | solution.py:343
  131.5 1.2 merge.1.after
  132.7 3.5 %all-to-all-start.5 = ((bf16[16,64,128]{2,1,0:T(8,128)(2,1)}), bf16[16,64,128]{2,1,0:T(8,128)(2,1)S(1)}, u32[]{:S(2)}, u32[]{:S(2)}) async-start(bf16[16,64,128]{2,1,0:T(8,128)(2,1)} %merge.1.after), calls=%async_computation.5 | async-start | bytes 524288 | tf_op jit(solution)/shard_map/all_to_all | solution.py:353
  136.3 0.1 copy.18.gaps
  136.4 1.6 copy-done.4
  138.0 7.6 %text.1 = (f32[128,1024]{1,0:T(8,128)S(1)}, f32[1,1024]{1,0:T(1,128)S(1)}, f32[1,1024]{1,0:T(1,128)S(1)}, bf16[128,1024]{1,0:T(8,128)(2,1)S(1)}) custom-call(s32[16,4]{1,0:T(8,128)S(1)} %copy.17.tokens, s32[16,4]{1,0:T(8,128)S(1)} %copy.18.gaps, bf16[1,128,1024]{2,1,0:T(8,128)(2,1)S(1)} %copy-done.5, bf16[8,512,256]{2,1,0:T(8,128)(2,1)S(1)} %bitcast.10, ...), custom_call_target="tpu_custom_call" | custom-call | flops 2200000000 | bytes 4000000 | tf_op jit(solution)/shard_map/text/pallas_call | solution.py:355
  145.6 5.4 %all-to-all-done.5.images = bf16[16,64,128]{2,1,0:T(8,128)(2,1)S(1)} async-done(((bf16[16,64,128]{2,1,0:T(8,128)(2,1)}), bf16[16,64,128]{2,1,0:T(8,128)(2,1)S(1)}, u32[]{:S(2)}, u32[]{:S(2)}) %all-to-all-start.5) | async-done | bytes 262176 | tf_op jit(solution)/shard_map/all_to_all | solution.py:353
  151.0 1.0 select.1
  152.0 15.6 %all_to_all.36.images = bf16[8,160,128]{2,1,0:T(8,128)(2,1)S(1)} all-to-all(bf16[8,160,128]{2,1,0:T(8,128)(2,1)S(1)} %select.1), channel_id=1, replica_groups=mesh['x'=4,'yh'=2,'core'=2,'j'=4,'h'=2,'tp'=4] {'j','h'}, dimensions={0} | all-to-all | bytes 655360 | tf_op jit(solution)/shard_map/all_to_all | solution.py:372
  167.6 2.1 %join.1 = bf16[1,128,1024]{2,1,0:T(8,128)(2,1)} custom-call(s32[16,4]{1,0:T(8,128)S(1)} %copy.17.tokens, s32[16,4]{1,0:T(8,128)S(1)} %copy.18.gaps, bf16[8,160,128]{2,1,0:T(8,128)(2,1)S(1)} %all_to_all.36.images, bf16[128,1024]{1,0:T(8,128)(2,1)S(1)} %get-tuple-element.10.flipped, f32[128,1024]{1,0:T(8,128)S(1)} %get-tuple-element.11.accum, ...), custom_call_target="tpu_custom_call" | custom-call | flops 84000000 | bytes 2000000 | tf_op jit(solution)/shard_map/join/pallas_call | solution.py:374
  (19 shorter events, 0.1 us)
Async XLA Ops:
  6.5 0.9 copy-start
  7.5 0.8 copy-start.2
  8.4 13.8 %collective-permute-start = (bf16[528,128]{1,0:T(8,128)(2,1)S(1)}, bf16[528,128]{1,0:T(8,128)(2,1)S(1)}, u32[]{:S(2)}, u32[]{:S(2)}) collective-permute-start(bf16[528,128]{1,0:T(8,128)(2,1)S(1)} %pack_heads.1), channel_id=1, source_target_pairs={{0,64},{64,0},{1,65},{65,1},{2,66},{66,2},{3,67},{67,3},{4,68},{68... | collective-permute-start | bytes 405512 | tf_op jit(solution)/shard_map/ppermute | solution.py:40
  22.4 16.1 %copy-start.6 = (bf16[4,32,1280]{2,1,0:T(8,128)(2,1)S(1)}, bf16[4,32,1280]{2,1,0:T(8,128)(2,1)}, u32[]{:S(2)}) copy-start(bf16[4,32,1280]{2,1,0:T(8,128)(2,1)} %param.12) | copy-start | bytes 983044
  38.5 13.3 %copy-start.7 = (bf16[1,384,256]{2,1,0:T(8,128)(2,1)S(1)}, bf16[1,384,256]{2,1,0:T(8,128)(2,1)}, u32[]{:S(2)}) copy-start(bf16[1,384,256]{2,1,0:T(8,128)(2,1)} %param.23) | copy-start | bytes 589828
  38.5 13.3 %copy-start.8 = (bf16[1,128,256]{2,1,0:T(8,128)(2,1)S(1)}, bf16[1,128,256]{2,1,0:T(8,128)(2,1)}, u32[]{:S(2)}) copy-start(bf16[1,128,256]{2,1,0:T(8,128)(2,1)} %param.22) | copy-start | bytes 196612
  39.4 13.2 %copy-start.11 = (s32[16,4]{0,1:T(4,128)S(1)}, s32[16,4]{0,1:T(4,128)}, u32[]{:S(2)}) copy-start(s32[16,4]{0,1:T(4,128)} %param.13) | copy-start | bytes 772
  39.4 13.3 %copy-start.9 = (f32[1280]{0:T(1024)S(1)}, f32[1280]{0:T(1024)}, u32[]{:S(2)}) copy-start(f32[1280]{0:T(1024)} %param.16) | copy-start | bytes 15364
  39.4 26.0 %copy-start.3 = (s32[64]{0:T(128)S(1)}, s32[64]{0:T(128)}, u32[]{:S(2)}) copy-start(s32[64]{0:T(128)} %slots.3) | copy-start | bytes 772
  39.4 26.0 %all-to-all-start = ((bf16[8,32,1280]{2,1,0:T(8,128)(2,1)}), bf16[8,32,1280]{2,1,0:T(8,128)(2,1)S(1)}, u32[]{:S(2)}, u32[]{:S(2)}) async-start(bf16[8,32,1280]{2,1,0:T(8,128)(2,1)} %bitcast), calls=%async_computation | async-start | bytes 1310720 | tf_op jit(solution)/shard_map/all_to_all | solution.py:318
  49.9 86.5 %all-gather.3.cloned.1.call-start = ((), (), s32[]{:S(2)}) async-start(), calls=%async_computation.7 | async-start | bytes 2359296 | tf_op jit(solution)/shard_map/all_gather | solution.py:305
  49.9 15.5 %collective-permute-start.1 = (bf16[4,2,528,128]{3,2,1,0:T(8,128)(2,1)S(1)}, bf16[4,2,528,128]{3,2,1,0:T(8,128)(2,1)S(1)}, u32[]{:S(2)}, u32[]{:S(2)}) collective-permute-start(bf16[4,2,528,128]{3,2,1,0:T(8,128)(2,1)S(1)} %all_to_all.35.own), channel_id=1, source_target_pairs={{0,32},{32,0},{1,33},{33,1},{2,34},{34,2},{3,35},{35,3},{4,36},{36... | collective-permute-start | bytes 3244040 | tf_op jit(solution)/shard_map/ppermute | solution.py:40
  69.1 11.9 %copy-start.1 = (bf16[320,256]{1,0:T(8,128)(2,1)S(1)}, bf16[320,256]{1,0:T(8,128)(2,1)}, u32[]{:S(2)}) copy-start(bf16[320,256]{1,0:T(8,128)(2,1)} %kv_merge.1) | copy-start | bytes 491524
  69.1 29.0 %all-to-all-start.2 = ((bf16[8,32,1280]{2,1,0:T(8,128)(2,1)}), bf16[8,32,1280]{2,1,0:T(8,128)(2,1)S(1)}, u32[]{:S(2)}, u32[]{:S(2)}) async-start(bf16[8,32,1280]{2,1,0:T(8,128)(2,1)} %vision.1), calls=%async_computation.2 | async-start | bytes 1310720 | tf_op jit(solution)/shard_map/all_to_all | solution.py:333
  81.1 11.5 %collective-permute-start.2 = (bf16[320,128]{1,0:T(8,128)(2,1)S(1)}, bf16[320,128]{1,0:T(8,128)(2,1)S(1)}, u32[]{:S(2)}, u32[]{:S(2)}) collective-permute-start(bf16[320,128]{1,0:T(8,128)(2,1)S(1)} %pack_merge.1), channel_id=1, source_target_pairs={{0,64},{64,0},{1,65},{65,1},{2,66},{66,2},{3,67},{67,3},{4,68},{68... | collective-permute-start | bytes 245768 | tf_op jit(solution)/shard_map/ppermute | solution.py:40
  92.6 10.0 %copy-start.10 = (f32[1280]{0:T(1024)S(1)}, f32[1280]{0:T(1024)}, u32[]{:S(2)}) copy-start(f32[1280]{0:T(1024)} %param.17) | copy-start | bytes 15364
  99.1 12.2 %all-to-all-start.4 = ((bf16[4,2,320,128]{3,2,1,0:T(8,128)(2,1)}), bf16[4,2,320,128]{3,2,1,0:T(8,128)(2,1)S(1)}, u32[]{:S(2)}, u32[]{:S(2)}) async-start(bf16[4,2,320,128]{3,2,1,0:T(8,128)(2,1)} %broadcast_in_dim.8), calls=%async_computation.4 | async-start | bytes 1310720 | tf_op jit(solution)/shard_map/all_to_all | solution.py:284
  111.3 20.2 %all-to-all-start.3 = ((bf16[8,32,1280]{2,1,0:T(8,128)(2,1)}), bf16[8,32,1280]{2,1,0:T(8,128)(2,1)S(1)}, u32[]{:S(2)}, u32[]{:S(2)}) async-start(bf16[8,32,1280]{2,1,0:T(8,128)(2,1)} %norm.1), calls=%async_computation.3 | async-start | bytes 1310720 | tf_op jit(solution)/shard_map/all_to_all | solution.py:343
  117.8 18.5 %copy-start.12 = (s32[16,4]{0,1:T(4,128)S(1)}, s32[16,4]{0,1:T(4,128)}, u32[]{:S(2)}) copy-start(s32[16,4]{0,1:T(4,128)} %param.14) | copy-start | bytes 772
  117.8 18.6 %copy-start.5 = (bf16[1,128,1024]{2,1,0:T(8,128)(2,1)S(1)}, bf16[1,128,1024]{2,1,0:T(8,128)(2,1)}, u32[]{:S(2)}) copy-start(bf16[1,128,1024]{2,1,0:T(8,128)(2,1)} %queries.1) | copy-start | bytes 786436
  117.8 4.1 %collective-permute-start.3 = (bf16[4,2,320,128]{3,2,1,0:T(8,128)(2,1)S(1)}, bf16[4,2,320,128]{3,2,1,0:T(8,128)(2,1)S(1)}, u32[]{:S(2)}, u32[]{:S(2)}) collective-permute-start(bf16[4,2,320,128]{3,2,1,0:T(8,128)(2,1)S(1)} %all-to-all-done.4.own), channel_id=1, source_target_pairs={{0,32},{32,0},{1,33},{33,1},{2,34},{34,2},{3,35},{35,3},{4,36},{36... | collective-permute-start | bytes 1966088 | tf_op jit(solution)/shard_map/ppermute | solution.py:40
  132.7 18.3 %all-to-all-start.5 = ((bf16[16,64,128]{2,1,0:T(8,128)(2,1)}), bf16[16,64,128]{2,1,0:T(8,128)(2,1)S(1)}, u32[]{:S(2)}, u32[]{:S(2)}) async-start(bf16[16,64,128]{2,1,0:T(8,128)(2,1)} %merge.1.after), calls=%async_computation.5 | async-start | bytes 524288 | tf_op jit(solution)/shard_map/all_to_all | solution.py:353
  136.4 1.6 copy-start.4
Sparse Core Ops, SparseCore 0:
  52.8 49.6 all-gather.2

commit v3 on v2

--- a/solution.py
+++ b/solution.py
@@ -44,7 +44,7 @@
     return values * lax.rsqrt(jnp.mean(values * values, axis=-1, keepdims=True) + EPS) * gain
 
 
-def pack_heads_kernel(w_qkv, w_out, out, lines):
+def pack_kernel(w_qkv, w_out, kv_merge, out, lines):
     first = jnp.where(lax.axis_index("h") == 0, w_qkv[:, 0:480], w_qkv[:, 480:960])
     for c in range(4):
         size = min(128, 480 - c * 128)
@@ -55,20 +55,17 @@
     for c in range(10):
         lines[pl.ds(c, 20, stride=10), :] = rows[:, c * 128 : (c + 1) * 128]
     out[320:528, :] = lines[...].astype(jnp.bfloat16)
-
-
-def pack_merge_kernel(kv_merge, after, out):
-    del after
-    out[...] = jnp.where(lax.axis_index("h") == 0, kv_merge[:, 0:HD], kv_merge[:, HD:])
+    out[528:848, :] = jnp.where(lax.axis_index("h") == 0, kv_merge[:, 0:HD], kv_merge[:, HD:])
 
 
 def vision_kernel(tokens, slots, patches, gain, own, other, out, weight, lines, rows_out, mixed):
     core, yh, half = lax.axis_index("core"), lax.axis_index("yh"), lax.axis_index("h")
-    slot = ((lax.axis_index("x") * 2 + yh) * 2 + core) * IMG_ENC + lax.axis_index("j")
+    here = lax.axis_index("x")
+    slot = ((here * 2 + yh) * 2 + core) * IMG_ENC + lax.axis_index("j")
     for x in range(4):
         for rel in range(2):
             for c in range(4):
-                base = x * 4 + (yh ^ rel) * 2
+                base = (here ^ x) * 4 + (yh ^ rel) * 2
                 tile = pl.ds(c * 128, 128)
                 weight[pl.ds(pl.multiple_of((base + core) * 80, 16), 80), tile] = own[
                     x, rel, c * 80 : (c + 1) * 80, :
@@ -81,7 +78,7 @@
         for rel in range(2):
             for part, piece in enumerate((own, other)):
                 base = head * 128 + (rel * 2 + part) * 32
-                lines[...] = piece[half * 2 + head, rel, 320:528, :].astype(jnp.float32)
+                lines[...] = piece[here ^ (half * 2 + head), rel, 320:528, :].astype(jnp.float32)
                 for c in range(10):
                     rows_out[base : base + 20, c * 128 : (c + 1) * 128] = lines[
                         pl.ds(c, 20, stride=10), :
@@ -125,7 +122,8 @@
     out[...] = partial.reshape(out.shape)
 
 
-def norm_kernel(parts, patches, gain, out):
+def norm_kernel(parts, patches, gain, weights, out):
+    del weights
     total = patches[lax.axis_index("tp") * 2 + lax.axis_index("h")].astype(jnp.float32)
     for peer in range(8):
         total += parts[peer].astype(jnp.float32)
@@ -136,11 +134,11 @@
 
 def merge_kernel(rows, own, other, out, merged, weight):
     core, yh = lax.axis_index("core"), lax.axis_index("yh")
-    for x in range(4):
+    for k in range(4):
         for rel in range(2):
-            base = x * 4 + (yh ^ rel) * 2
-            weight[pl.ds(pl.multiple_of((base + core) * 320, 16), 320), :] = own[x, rel]
-            weight[pl.ds(pl.multiple_of((base + 1 - core) * 320, 16), 320), :] = other[x, rel]
+            base = (lax.axis_index("x") ^ k) * 4 + (yh ^ rel) * 2
+            weight[pl.ds(pl.multiple_of((base + core) * 320, 16), 320), :] = own[k, rel]
+            weight[pl.ds(pl.multiple_of((base + 1 - core) * 320, 16), 320), :] = other[k, rel]
     normed = rows[...].reshape(SLOT, VD).astype(jnp.float32)
     for c in range(VD // 128):
         merged[c] = normed[:, c * 128 : (c + 1) * 128]
@@ -279,10 +277,11 @@
     bf16, f32 = jnp.bfloat16, jnp.float32
     lanes = GROUP * 128
 
-    def spread(value):
-        both = jnp.stack([value, swap(value, "yh")])
-        own = lax.all_to_all(jnp.broadcast_to(both[None], (4,) + both.shape), "x", 0, 0)
-        return own, swap(own, "core")
+    def after(value, event):
+        return lax.optimization_barrier((value, event))[0]
+
+    def swap_x(value, bits):
+        return lax.ppermute(value, "x", [(i, i ^ bits) for i in range(4)])
 
     def call(kernel, name, out_shape, in_specs, scratch=(), cost=(0, 0, 0)):
         return pl.pallas_call(
@@ -305,17 +304,23 @@
     past = lax.all_gather(past, SEQ, axis=0)
 
     heads = call(
-        pack_heads_kernel,
-        "pack_heads",
-        array((528, 128)),
-        [VMEM] * 2,
+        pack_kernel,
+        "pack",
+        array((848, 128)),
+        [VMEM] * 3,
         [pltpu.VMEM((208, 128), f32)],
-        (1_000_000, 400_000, 0),
-    )(w_qkv, w_out)
-    own, other = spread(heads)
+        (1_000_000, 800_000, 0),
+    )(w_qkv, w_out, kv_merge)
+    mine, theirs = heads, swap(heads, "yh")
 
     sent = jnp.broadcast_to(patches[:, None], (4, 2, 32, VD)).reshape(8, 32, VD)
     image = lax.all_to_all(sent, SEQ, 0, 0)
+    first = [mine[0:528]] + [swap_x(mine[0:528], k) for k in (1, 2, 3)]
+    second = [theirs[0:528]] + [swap_x(theirs[0:528], k) for k in (1, 2, 3)]
+    own = jnp.stack([jnp.stack(first), jnp.stack(second)], axis=1)
+    merge_pair = jnp.stack([mine[528:848], theirs[528:848]])
+    merge_pair = jnp.stack([merge_pair, swap_x(merge_pair, 1)])
+    other = swap(after(own, (image, merge_pair)), "core")
 
     parts = call(
         vision_kernel,
@@ -330,16 +335,13 @@
         ],
         (600_000_000, 5_000_000, 131072),
     )(image_tokens, image_slot, image, norm_gain.reshape(1, VD), own, other)
+    merge_own = jnp.concatenate([merge_pair, swap_x(after(merge_pair, parts), 2)])
     parts = lax.all_to_all(parts, ("tp", "h"), 0, 0)
 
-    columns = call(
-        pack_merge_kernel, "pack_merge", array((320, 128)), [VMEM, ANY], (), (0, 300_000, 0)
-    )(kv_merge, other)
-    merge_own, merge_other = spread(columns)
-
     rows = call(
-        norm_kernel, "norm", array((8, 32, VD)), [VMEM] * 3, (), (1_000_000, 2_000_000, 32)
-    )(parts, image, merge_gain.reshape(1, VD))
+        norm_kernel, "norm", array((8, 32, VD)), [VMEM] * 3 + [ANY], (), (1_000_000, 2_000_000, 32)
+    )(parts, image, merge_gain.reshape(1, VD), merge_own)
+    merge_other = swap(after(merge_own, rows), "core")
     rows = lax.all_to_all(rows, ("tp", "h"), 0, 0)
 
     image_kv = call(

time: 177 us -> 160 us (0.904)
  waiting for transfers between devices: 57.1 us -> 39.3 us
  blocking collectives: 31.7 us -> 18.5 us
  starting transfers between devices: 51.1 us -> 63.5 us
    ppermute x0 -> x8, starting transfers between devices: none -> 26.5 us  [swap_x(): return lax.ppermute(value, 'x', [(i, i ^ bits) for i in range(4)])]
    all_to_all x1 -> x0, blocking collectives: 16.1 us -> none  [spread(): lax.all_to_all(jnp.broadcast_to(both[None], (4,) + both.shape), 'x', 0, 0)]
    ppermute x0 -> x8, waiting for transfers between devices: none -> 14.1 us  [swap_x(): return lax.ppermute(value, 'x', [(i, i ^ bits) for i in range(4)])]
    ppermute x4 -> x3, waiting for transfers between devices: 16.2 us -> 3.79 us  [swap(): return lax.ppermute(value, axis, [(0, 1), (1, 0)])]
    all_to_all x1, waiting for transfers between devices: 12.6 us -> 0.51 us  [per_device(): image = lax.all_to_all(sent, SEQ, 0, 0)]
    all_to_all x1 -> x0, waiting for transfers between devices: 7.66 us -> none  [spread(): lax.all_to_all(jnp.broadcast_to(both[None], (4,) + both.shape), 'x', 0, 0)]
    all_to_all x1, starting transfers between devices: 11.9 us -> 4.93 us  [per_device(): parts = lax.all_to_all(parts, ('tp', 'h'), 0, 0)]
    ppermute x4 -> x3, starting transfers between devices: 15.2 us -> 10.8 us  [swap(): return lax.ppermute(value, axis, [(0, 1), (1, 0)])]
  transfers between devices with their start and end apart: 10 -> 16, of which waited for: 8 -> 9; matrix products, arithmetic and copies ran while one was open for 1% -> 2% of each run, Pallas kernels for 8% -> 9%
where the time goes in v3:
time: 160 us; the launch traced here: 159 us
  starting transfers between devices  63.5 us (40%)
  waiting for transfers between devices  39.3 us (25%)
  blocking collectives  18.5 us (12%)
  Pallas kernels  16.9 us (11%)
  between operations  13.7 us (9%)
  local copies, waits for them, and re-layouts  5.57 us (3%)
  other arithmetic  1.81 us (1%)
    ppermute x8, starting transfers between devices, swap_x(): return lax.ppermute(value, 'x', [(i, i ^ bits) for i in range(4)])  26.5 us
    all_to_all x1, blocking collectives, per_device(): images = lax.all_to_all(packed, SEQ, 0, 0)  18.5 us
    ppermute x8, waiting for transfers between devices, swap_x(): return lax.ppermute(value, 'x', [(i, i ^ bits) for i in range(4)])  14.1 us
    all_to_all x1, waiting for transfers between devices, per_device(): rows = lax.all_to_all(rows, ('tp', 'h'), 0, 0)  11.9 us
    ppermute x3, starting transfers between devices, swap(): return lax.ppermute(value, axis, [(0, 1), (1, 0)])  10.8 us
    all_to_all x1, starting transfers between devices, per_device(): image = lax.all_to_all(sent, SEQ, 0, 0)  10.3 us
    pallas_call x1, Pallas kernels, per_device(): call(text_kernel, 'text', (array((HD, lanes), f32), array((1, lanes), f32...  7.59 us
    all_to_all x1, starting transfers between devices, per_device(): every = lax.all_to_all(image_kv, ENC, 0, 0)  5.74 us
  transfers between devices with their start and end apart: 16, of which 9 were waited for; matrix products, arithmetic and copies ran while one was open for 2% of the time, Pallas kernels for 9%

profile of v3, /device:TPU:8, one launch (start us, length us, event | category | flops | bytes accessed | tf_op | source)
XLA Modules:
  0.0 159.4 jit_solution(2990572174875875942)
XLA Ops:
  6.5 0.9 copy-done
  7.5 0.9 copy-done.1
  8.4 0.8 copy-done.2
  9.2 0.1 pack.1
  9.3 6.8 %collective-permute-start.3 = (bf16[848,128]{1,0:T(8,128)(2,1)S(1)}, bf16[848,128]{1,0:T(8,128)(2,1)S(1)}, u32[]{:S(2)}, u32[]{:S(2)}) collective-permute-start(bf16[848,128]{1,0:T(8,128)(2,1)S(1)} %pack.1), channel_id=1, source_target_pairs={{0,64},{64,0},{1,65},{65,1},{2,66},{66,2},{3,67},{67,3},{4,68},{68... | collective-permute-start | bytes 651272 | tf_op jit(solution)/shard_map/ppermute | solution.py:40
  16.2 3.4 %collective-permute-start = (bf16[528,128]{1,0:T(8,128)(2,1)S(1)}, bf16[528,128]{1,0:T(8,128)(2,1)S(1)}, u32[]{:S(2)}, u32[]{:S(2)}) collective-permute-start(bf16[528,128]{1,0:T(8,128)(2,1)S(1)} %get-tuple-element.20), channel_id=1, source_target_pairs={{0,128},{128,0},{256,384},{384,256},{1,129},{129,1},{257,385},{385... | collective-permute-start | bytes 405512 | tf_op jit(solution)/shard_map/ppermute | solution.py:284
  19.6 4.6 %collective-permute-start.1 = (bf16[528,128]{1,0:T(8,128)(2,1)S(1)}, bf16[528,128]{1,0:T(8,128)(2,1)S(1)}, u32[]{:S(2)}, u32[]{:S(2)}) collective-permute-start(bf16[528,128]{1,0:T(8,128)(2,1)S(1)} %get-tuple-element.20), channel_id=1, source_target_pairs={{0,256},{128,384},{256,0},{384,128},{1,257},{129,385},{257,1},{385... | collective-permute-start | bytes 405512 | tf_op jit(solution)/shard_map/ppermute | solution.py:284
  24.2 2.4 %collective-permute-start.2 = (bf16[528,128]{1,0:T(8,128)(2,1)S(1)}, bf16[528,128]{1,0:T(8,128)(2,1)S(1)}, u32[]{:S(2)}, u32[]{:S(2)}) collective-permute-start(bf16[528,128]{1,0:T(8,128)(2,1)S(1)} %get-tuple-element.20), channel_id=1, source_target_pairs={{0,384},{128,256},{256,128},{384,0},{1,385},{129,257},{257,129},{3... | collective-permute-start | bytes 405512 | tf_op jit(solution)/shard_map/ppermute | solution.py:284
  26.6 0.9 broadcast_in_dim.2
  27.5 10.3 %all-to-all-start = ((bf16[8,32,1280]{2,1,0:T(8,128)(2,1)}), bf16[8,32,1280]{2,1,0:T(8,128)(2,1)S(1)}, u32[]{:S(2)}, u32[]{:S(2)}) async-start(bf16[8,32,1280]{2,1,0:T(8,128)(2,1)} %bitcast), calls=%async_computation | async-start | bytes 1310720 | tf_op jit(solution)/shard_map/all_to_all | solution.py:317
  37.9 0.0 all-gather.3.cloned.1.call-start
  37.9 0.1 maximum_bitcast_fusion
  38.1 2.2 %collective-permute-start.4 = (bf16[528,128]{1,0:T(8,128)(2,1)S(1)}, bf16[528,128]{1,0:T(8,128)(2,1)S(1)}, u32[]{:S(2)}, u32[]{:S(2)}) collective-permute-start(bf16[528,128]{1,0:T(8,128)(2,1)S(1)} %get-tuple-element.22), channel_id=1, source_target_pairs={{0,128},{128,0},{256,384},{384,256},{1,129},{129,1},{257,385},{385... | collective-permute-start | bytes 405512 | tf_op jit(solution)/shard_map/ppermute | solution.py:284
  40.3 5.8 %collective-permute-start.5 = (bf16[528,128]{1,0:T(8,128)(2,1)S(1)}, bf16[528,128]{1,0:T(8,128)(2,1)S(1)}, u32[]{:S(2)}, u32[]{:S(2)}) collective-permute-start(bf16[528,128]{1,0:T(8,128)(2,1)S(1)} %get-tuple-element.22), channel_id=1, source_target_pairs={{0,256},{128,384},{256,0},{384,128},{1,257},{129,385},{257,1},{385... | collective-permute-start | bytes 405512 | tf_op jit(solution)/shard_map/ppermute | solution.py:284
  46.1 2.4 %collective-permute-start.6 = (bf16[528,128]{1,0:T(8,128)(2,1)S(1)}, bf16[528,128]{1,0:T(8,128)(2,1)S(1)}, u32[]{:S(2)}, u32[]{:S(2)}) collective-permute-start(bf16[528,128]{1,0:T(8,128)(2,1)S(1)} %get-tuple-element.22), channel_id=1, source_target_pairs={{0,384},{128,256},{256,128},{384,0},{1,385},{129,257},{257,129},{3... | collective-permute-start | bytes 405512 | tf_op jit(solution)/shard_map/ppermute | solution.py:284
  48.6 1.9 %collective-permute-start.7 = (bf16[2,320,128]{2,1,0:T(8,128)(2,1)S(1)}, bf16[2,320,128]{2,1,0:T(8,128)(2,1)S(1)}, u32[]{:S(2)}, u32[]{:S(2)}) collective-permute-start(bf16[2,320,128]{2,1,0:T(8,128)(2,1)S(1)} %get-tuple-element.24), channel_id=1, source_target_pairs={{0,128},{128,0},{256,384},{384,256},{1,129},{129,1},{257,385},{385... | collective-permute-start | bytes 491528 | tf_op jit(solution)/shard_map/ppermute | solution.py:284
  50.5 3.7 %collective-permute-done.6 = bf16[528,128]{1,0:T(8,128)(2,1)S(1)} collective-permute-done((bf16[528,128]{1,0:T(8,128)(2,1)S(1)}, bf16[528,128]{1,0:T(8,128)(2,1)S(1)}, u32[]{:S(2)}, u32[]{:S(2)}) %collective-permute-start.6) | collective-permute-done | bytes 135200 | tf_op jit(solution)/shard_map/ppermute | solution.py:284
  54.2 0.1 maximum_bitcast_fusion.1
  54.3 0.1 pad_maximum_fusion
  54.5 1.3 collective-permute-done.7
  55.8 0.8 pad_maximum_fusion.2
  56.5 0.5 all-to-all-done.patches
  57.0 1.9 %collective-permute-start.8 = (bf16[4,2,528,128]{3,2,0,1:T(8,128)(2,1)S(1)}, bf16[4,2,528,128]{3,2,0,1:T(8,128)(2,1)S(1)}, u32[]{:S(2)}, u32[]{:S(2)}) collective-permute-start(bf16[4,2,528,128]{3,2,0,1:T(8,128)(2,1)S(1)} %pad_maximum_fusion), channel_id=1, source_target_pairs={{0,32},{32,0},{1,33},{33,1},{2,34},{34,2},{3,35},{35,3},{4,36},{36... | collective-permute-start | bytes 3244040 | tf_op jit(solution)/shard_map/ppermute | solution.py:40
  59.0 0.7 pad_maximum_fusion.3
  59.7 0.1 copy.19.tokens
  59.8 0.1 copy.14.own
  59.9 1.7 %collective-permute-done.8 = bf16[4,2,528,128]{3,2,0,1:T(8,128)(2,1)S(1)} collective-permute-done((bf16[4,2,528,128]{3,2,0,1:T(8,128)(2,1)S(1)}, bf16[4,2,528,128]{3,2,0,1:T(8,128)(2,1)S(1)}, u32[]{:S(2)}, u32[]{:S(2)}) %collective-permute-start.8) | collective-permute-done | bytes 1081376 | tf_op jit(solution)/shard_map/ppermute | solution.py:40
  61.6 0.1 copy.15.other
  61.7 3.8 %vision.1 = bf16[8,32,1280]{2,1,0:T(8,128)(2,1)} custom-call(s32[16,4]{1,0:T(8,128)S(1)} %copy.19.tokens, s32[64]{0:T(128)S(1)} %copy-done.3, bf16[8,32,1280]{2,1,0:T(8,128)(2,1)S(1)} %all-to-all-done.patches, f32[1,1280]{1,0:T(1,128)S(1)} %reshape.11.gain, bf16[4,2,528,128]{3,2,1,0:T(8,128)(2,1)S(1)} %copy.14.own, bf16[4,2,528,128]{3,2,1,0:T(8,128)(2,1)S(1)} %copy.15.other), custom_call_target="tpu_custom_call" | custom-call | flops 600000000 | bytes 5000000 | tf_op jit(solution)/shard_map/vision/pallas_call | solution.py:325
  65.5 4.9 %all-to-all-start.1 = ((bf16[8,32,1280]{2,1,0:T(8,128)(2,1)}), bf16[8,32,1280]{2,1,0:T(8,128)(2,1)S(1)}, u32[]{:S(2)}, u32[]{:S(2)}) async-start(bf16[8,32,1280]{2,1,0:T(8,128)(2,1)} %vision.1), calls=%async_computation.1 | async-start | bytes 1310720 | tf_op jit(solution)/shard_map/all_to_all | solution.py:339
  70.4 3.7 %collective-permute-start.9 = (bf16[2,2,320,128]{3,2,1,0:T(8,128)(2,1)S(1)}, bf16[2,2,320,128]{3,2,1,0:T(8,128)(2,1)S(1)}, u32[]{:S(2)}, u32[]{:S(2)}) collective-permute-start(bf16[2,2,320,128]{3,2,1,0:T(8,128)(2,1)S(1)} %copy-done.6), channel_id=1, source_target_pairs={{0,256},{128,384},{256,0},{384,128},{1,257},{129,385},{257,1},{385... | collective-permute-start | bytes 983048 | tf_op jit(solution)/shard_map/ppermute | solution.py:284
  74.2 9.1 %collective-permute-done.9 = bf16[2,2,320,128]{3,2,1,0:T(8,128)(2,1)S(1)} collective-permute-done((bf16[2,2,320,128]{3,2,1,0:T(8,128)(2,1)S(1)}, bf16[2,2,320,128]{3,2,1,0:T(8,128)(2,1)S(1)}, u32[]{:S(2)}, u32[]{:S(2)}) %collective-permute-start.9) | collective-permute-done | bytes 327712 | tf_op jit(solution)/shard_map/ppermute | solution.py:284
  83.3 0.1 pad_maximum_fusion.1.weights.own
  83.4 3.5 %all-to-all-done.1.parts = bf16[8,32,1280]{2,1,0:T(8,128)(2,1)S(1)} async-done(((bf16[8,32,1280]{2,1,0:T(8,128)(2,1)}), bf16[8,32,1280]{2,1,0:T(8,128)(2,1)S(1)}, u32[]{:S(2)}, u32[]{:S(2)}) %all-to-all-start.1) | async-done | bytes 655392 | tf_op jit(solution)/shard_map/all_to_all | solution.py:339
  86.8 1.1 norm.1
  87.9 5.2 %all-to-all-start.2 = ((bf16[8,32,1280]{2,1,0:T(8,128)(2,1)}), bf16[8,32,1280]{2,1,0:T(8,128)(2,1)S(1)}, u32[]{:S(2)}, u32[]{:S(2)}) async-start(bf16[8,32,1280]{2,1,0:T(8,128)(2,1)} %norm.1), calls=%async_computation.2 | async-start | bytes 1310720 | tf_op jit(solution)/shard_map/all_to_all | solution.py:345
  93.1 2.0 %collective-permute-start.10 = (bf16[4,2,320,128]{3,2,1,0:T(8,128)(2,1)S(1)}, bf16[4,2,320,128]{3,2,1,0:T(8,128)(2,1)S(1)}, u32[]{:S(2)}, u32[]{:S(2)}) collective-permute-start(bf16[4,2,320,128]{3,2,1,0:T(8,128)(2,1)S(1)} %pad_maximum_fusion.1.weights.own), channel_id=1, source_target_pairs={{0,32},{32,0},{1,33},{33,1},{2,34},{34,2},{3,35},{35,3},{4,36},{36... | collective-permute-start | bytes 1966088 | tf_op jit(solution)/shard_map/ppermute | solution.py:40
  95.1 2.1 %collective-permute-done.10.other = bf16[4,2,320,128]{3,2,1,0:T(8,128)(2,1)S(1)} collective-permute-done((bf16[4,2,320,128]{3,2,1,0:T(8,128)(2,1)S(1)}, bf16[4,2,320,128]{3,2,1,0:T(8,128)(2,1)S(1)}, u32[]{:S(2)}, u32[]{:S(2)}) %collective-permute-start.10) | collective-permute-done | bytes 655392 | tf_op jit(solution)/shard_map/ppermute | solution.py:40
  97.2 11.9 %all-to-all-done.2.rows = bf16[8,32,1280]{2,1,0:T(8,128)(2,1)S(1)} async-done(((bf16[8,32,1280]{2,1,0:T(8,128)(2,1)}), bf16[8,32,1280]{2,1,0:T(8,128)(2,1)S(1)}, u32[]{:S(2)}, u32[]{:S(2)}) %all-to-all-start.2) | async-done | bytes 655392 | tf_op jit(solution)/shard_map/all_to_all | solution.py:345
  109.1 1.2 merge.1.after
  110.4 5.7 %all-to-all-start.3 = ((bf16[16,64,128]{2,1,0:T(8,128)(2,1)}), bf16[16,64,128]{2,1,0:T(8,128)(2,1)S(1)}, u32[]{:S(2)}, u32[]{:S(2)}) async-start(bf16[16,64,128]{2,1,0:T(8,128)(2,1)} %merge.1.after), calls=%async_computation.3 | async-start | bytes 524288 | tf_op jit(solution)/shard_map/all_to_all | solution.py:355
  116.1 0.1 copy.20.gaps
  116.2 1.6 copy-done.4
  117.8 7.6 %text.1 = (f32[128,1024]{1,0:T(8,128)S(1)}, f32[1,1024]{1,0:T(1,128)S(1)}, f32[1,1024]{1,0:T(1,128)S(1)}, bf16[128,1024]{1,0:T(8,128)(2,1)S(1)}) custom-call(s32[16,4]{1,0:T(8,128)S(1)} %copy.19.tokens, s32[16,4]{1,0:T(8,128)S(1)} %copy.20.gaps, bf16[1,128,1024]{2,1,0:T(8,128)(2,1)S(1)} %copy-done.5, bf16[8,512,256]{2,1,0:T(8,128)(2,1)S(1)} %bitcast.25, ...), custom_call_target="tpu_custom_call" | custom-call | flops 2200000000 | bytes 4000000 | tf_op jit(solution)/shard_map/text/pallas_call | solution.py:357
  125.4 5.5 %all-to-all-done.3.images = bf16[16,64,128]{2,1,0:T(8,128)(2,1)S(1)} async-done(((bf16[16,64,128]{2,1,0:T(8,128)(2,1)}), bf16[16,64,128]{2,1,0:T(8,128)(2,1)S(1)}, u32[]{:S(2)}, u32[]{:S(2)}) %all-to-all-start.3) | async-done | bytes 262176 | tf_op jit(solution)/shard_map/all_to_all | solution.py:355
  130.9 1.0 select.1
  131.9 18.5 %all_to_all.25.images = bf16[8,160,128]{2,1,0:T(8,128)(2,1)S(1)} all-to-all(bf16[8,160,128]{2,1,0:T(8,128)(2,1)S(1)} %select.1), channel_id=1, replica_groups=mesh['x'=4,'yh'=2,'core'=2,'j'=4,'h'=2,'tp'=4] {'j','h'}, dimensions={0} | all-to-all | bytes 655360 | tf_op jit(solution)/shard_map/all_to_all | solution.py:374
  150.4 2.1 %join.1 = bf16[1,128,1024]{2,1,0:T(8,128)(2,1)} custom-call(s32[16,4]{1,0:T(8,128)S(1)} %copy.19.tokens, s32[16,4]{1,0:T(8,128)S(1)} %copy.20.gaps, bf16[8,160,128]{2,1,0:T(8,128)(2,1)S(1)} %all_to_all.25.images, bf16[128,1024]{1,0:T(8,128)(2,1)S(1)} %get-tuple-element.16.flipped, f32[128,1024]{1,0:T(8,128)S(1)} %get-tuple-element.17.accum, ...), custom_call_target="tpu_custom_call" | custom-call | flops 84000000 | bytes 2000000 | tf_op jit(solution)/shard_map/join/pallas_call | solution.py:376
  (39 shorter events, 0.2 us)
Async XLA Ops:
  6.5 0.9 copy-start
  7.5 0.9 copy-start.1
  8.4 0.8 copy-start.2
  9.2 17.4 %copy-start.7 = (bf16[4,32,1280]{2,1,0:T(8,128)(2,1)S(1)}, bf16[4,32,1280]{2,1,0:T(8,128)(2,1)}, u32[]{:S(2)}) copy-start(bf16[4,32,1280]{2,1,0:T(8,128)(2,1)} %param.12) | copy-start | bytes 983044
  9.3 28.7 %collective-permute-start.3 = (bf16[848,128]{1,0:T(8,128)(2,1)S(1)}, bf16[848,128]{1,0:T(8,128)(2,1)S(1)}, u32[]{:S(2)}, u32[]{:S(2)}) collective-permute-start(bf16[848,128]{1,0:T(8,128)(2,1)S(1)} %pack.1), channel_id=1, source_target_pairs={{0,64},{64,0},{1,65},{65,1},{2,66},{66,2},{3,67},{67,3},{4,68},{68... | collective-permute-start | bytes 651272 | tf_op jit(solution)/shard_map/ppermute | solution.py:40
  16.2 21.7 %collective-permute-start = (bf16[528,128]{1,0:T(8,128)(2,1)S(1)}, bf16[528,128]{1,0:T(8,128)(2,1)S(1)}, u32[]{:S(2)}, u32[]{:S(2)}) collective-permute-start(bf16[528,128]{1,0:T(8,128)(2,1)S(1)} %get-tuple-element.20), channel_id=1, source_target_pairs={{0,128},{128,0},{256,384},{384,256},{1,129},{129,1},{257,385},{385... | collective-permute-start | bytes 405512 | tf_op jit(solution)/shard_map/ppermute | solution.py:284
  19.6 18.3 %collective-permute-start.1 = (bf16[528,128]{1,0:T(8,128)(2,1)S(1)}, bf16[528,128]{1,0:T(8,128)(2,1)S(1)}, u32[]{:S(2)}, u32[]{:S(2)}) collective-permute-start(bf16[528,128]{1,0:T(8,128)(2,1)S(1)} %get-tuple-element.20), channel_id=1, source_target_pairs={{0,256},{128,384},{256,0},{384,128},{1,257},{129,385},{257,1},{385... | collective-permute-start | bytes 405512 | tf_op jit(solution)/shard_map/ppermute | solution.py:284
  24.2 13.7 %collective-permute-start.2 = (bf16[528,128]{1,0:T(8,128)(2,1)S(1)}, bf16[528,128]{1,0:T(8,128)(2,1)S(1)}, u32[]{:S(2)}, u32[]{:S(2)}) collective-permute-start(bf16[528,128]{1,0:T(8,128)(2,1)S(1)} %get-tuple-element.20), channel_id=1, source_target_pairs={{0,384},{128,256},{256,128},{384,0},{1,385},{129,257},{257,129},{3... | collective-permute-start | bytes 405512 | tf_op jit(solution)/shard_map/ppermute | solution.py:284
  27.5 29.5 %all-to-all-start = ((bf16[8,32,1280]{2,1,0:T(8,128)(2,1)}), bf16[8,32,1280]{2,1,0:T(8,128)(2,1)S(1)}, u32[]{:S(2)}, u32[]{:S(2)}) async-start(bf16[8,32,1280]{2,1,0:T(8,128)(2,1)} %bitcast), calls=%async_computation | async-start | bytes 1310720 | tf_op jit(solution)/shard_map/all_to_all | solution.py:317
  37.9 78.4 %all-gather.3.cloned.1.call-start = ((), (), s32[]{:S(2)}) async-start(), calls=%async_computation.5 | async-start | bytes 2359296 | tf_op jit(solution)/shard_map/all_gather | solution.py:304
  38.1 12.4 %collective-permute-start.4 = (bf16[528,128]{1,0:T(8,128)(2,1)S(1)}, bf16[528,128]{1,0:T(8,128)(2,1)S(1)}, u32[]{:S(2)}, u32[]{:S(2)}) collective-permute-start(bf16[528,128]{1,0:T(8,128)(2,1)S(1)} %get-tuple-element.22), channel_id=1, source_target_pairs={{0,128},{128,0},{256,384},{384,256},{1,129},{129,1},{257,385},{385... | collective-permute-start | bytes 405512 | tf_op jit(solution)/shard_map/ppermute | solution.py:284
  40.3 10.2 %collective-permute-start.5 = (bf16[528,128]{1,0:T(8,128)(2,1)S(1)}, bf16[528,128]{1,0:T(8,128)(2,1)S(1)}, u32[]{:S(2)}, u32[]{:S(2)}) collective-permute-start(bf16[528,128]{1,0:T(8,128)(2,1)S(1)} %get-tuple-element.22), channel_id=1, source_target_pairs={{0,256},{128,384},{256,0},{384,128},{1,257},{129,385},{257,1},{385... | collective-permute-start | bytes 405512 | tf_op jit(solution)/shard_map/ppermute | solution.py:284
  46.1 8.1 %collective-permute-start.6 = (bf16[528,128]{1,0:T(8,128)(2,1)S(1)}, bf16[528,128]{1,0:T(8,128)(2,1)S(1)}, u32[]{:S(2)}, u32[]{:S(2)}) collective-permute-start(bf16[528,128]{1,0:T(8,128)(2,1)S(1)} %get-tuple-element.22), channel_id=1, source_target_pairs={{0,384},{128,256},{256,128},{384,0},{1,385},{129,257},{257,129},{3... | collective-permute-start | bytes 405512 | tf_op jit(solution)/shard_map/ppermute | solution.py:284
  48.6 7.2 %collective-permute-start.7 = (bf16[2,320,128]{2,1,0:T(8,128)(2,1)S(1)}, bf16[2,320,128]{2,1,0:T(8,128)(2,1)S(1)}, u32[]{:S(2)}, u32[]{:S(2)}) collective-permute-start(bf16[2,320,128]{2,1,0:T(8,128)(2,1)S(1)} %get-tuple-element.24), channel_id=1, source_target_pairs={{0,128},{128,0},{256,384},{384,256},{1,129},{129,1},{257,385},{385... | collective-permute-start | bytes 491528 | tf_op jit(solution)/shard_map/ppermute | solution.py:284
  54.3 4.7 %copy-start.8 = (bf16[1,384,256]{2,1,0:T(8,128)(2,1)S(1)}, bf16[1,384,256]{2,1,0:T(8,128)(2,1)}, u32[]{:S(2)}) copy-start(bf16[1,384,256]{2,1,0:T(8,128)(2,1)} %param.23) | copy-start | bytes 589828
  54.3 4.6 %copy-start.9 = (bf16[1,128,256]{2,1,0:T(8,128)(2,1)S(1)}, bf16[1,128,256]{2,1,0:T(8,128)(2,1)}, u32[]{:S(2)}) copy-start(bf16[1,128,256]{2,1,0:T(8,128)(2,1)} %param.22) | copy-start | bytes 196612
  54.4 5.3 %copy-start.12 = (s32[16,4]{0,1:T(4,128)S(1)}, s32[16,4]{0,1:T(4,128)}, u32[]{:S(2)}) copy-start(s32[16,4]{0,1:T(4,128)} %param.13) | copy-start | bytes 772
  54.5 5.4 %copy-start.10 = (f32[1280]{0:T(1024)S(1)}, f32[1280]{0:T(1024)}, u32[]{:S(2)}) copy-start(f32[1280]{0:T(1024)} %param.16) | copy-start | bytes 15364
  57.0 4.6 %collective-permute-start.8 = (bf16[4,2,528,128]{3,2,0,1:T(8,128)(2,1)S(1)}, bf16[4,2,528,128]{3,2,0,1:T(8,128)(2,1)S(1)}, u32[]{:S(2)}, u32[]{:S(2)}) collective-permute-start(bf16[4,2,528,128]{3,2,0,1:T(8,128)(2,1)S(1)} %pad_maximum_fusion), channel_id=1, source_target_pairs={{0,32},{32,0},{1,33},{33,1},{2,34},{34,2},{3,35},{35,3},{4,36},{36... | collective-permute-start | bytes 3244040 | tf_op jit(solution)/shard_map/ppermute | solution.py:40
  59.9 1.8 %copy-start.3 = (s32[64]{0:T(128)S(1)}, s32[64]{0:T(128)}, u32[]{:S(2)}) copy-start(s32[64]{0:T(128)} %slots.3) | copy-start | bytes 772
  65.5 4.9 %copy-start.6 = (bf16[2,2,320,128]{3,2,1,0:T(8,128)(2,1)S(1)}, bf16[2,2,320,128]{3,2,1,0:T(8,128)(2,1)}, u32[]{:S(2)}) copy-start(bf16[2,2,320,128]{3,2,1,0:T(8,128)(2,1)} %pad_maximum_fusion.2) | copy-start | bytes 983044
  65.5 8.7 %copy-start.11 = (f32[1280]{0:T(1024)S(1)}, f32[1280]{0:T(1024)}, u32[]{:S(2)}) copy-start(f32[1280]{0:T(1024)} %param.17) | copy-start | bytes 15364
  65.5 21.3 %all-to-all-start.1 = ((bf16[8,32,1280]{2,1,0:T(8,128)(2,1)}), bf16[8,32,1280]{2,1,0:T(8,128)(2,1)S(1)}, u32[]{:S(2)}, u32[]{:S(2)}) async-start(bf16[8,32,1280]{2,1,0:T(8,128)(2,1)} %vision.1), calls=%async_computation.1 | async-start | bytes 1310720 | tf_op jit(solution)/shard_map/all_to_all | solution.py:339
  70.4 12.9 %collective-permute-start.9 = (bf16[2,2,320,128]{3,2,1,0:T(8,128)(2,1)S(1)}, bf16[2,2,320,128]{3,2,1,0:T(8,128)(2,1)S(1)}, u32[]{:S(2)}, u32[]{:S(2)}) collective-permute-start(bf16[2,2,320,128]{3,2,1,0:T(8,128)(2,1)S(1)} %copy-done.6), channel_id=1, source_target_pairs={{0,256},{128,384},{256,0},{384,128},{1,257},{129,385},{257,1},{385... | collective-permute-start | bytes 983048 | tf_op jit(solution)/shard_map/ppermute | solution.py:284
  87.9 21.3 %all-to-all-start.2 = ((bf16[8,32,1280]{2,1,0:T(8,128)(2,1)}), bf16[8,32,1280]{2,1,0:T(8,128)(2,1)S(1)}, u32[]{:S(2)}, u32[]{:S(2)}) async-start(bf16[8,32,1280]{2,1,0:T(8,128)(2,1)} %norm.1), calls=%async_computation.2 | async-start | bytes 1310720 | tf_op jit(solution)/shard_map/all_to_all | solution.py:345
  93.1 23.0 %copy-start.13 = (s32[16,4]{0,1:T(4,128)S(1)}, s32[16,4]{0,1:T(4,128)}, u32[]{:S(2)}) copy-start(s32[16,4]{0,1:T(4,128)} %param.14) | copy-start | bytes 772
  93.1 23.1 %copy-start.5 = (bf16[1,128,1024]{2,1,0:T(8,128)(2,1)S(1)}, bf16[1,128,1024]{2,1,0:T(8,128)(2,1)}, u32[]{:S(2)}) copy-start(bf16[1,128,1024]{2,1,0:T(8,128)(2,1)} %queries.1) | copy-start | bytes 786436
  93.1 4.1 %collective-permute-start.10 = (bf16[4,2,320,128]{3,2,1,0:T(8,128)(2,1)S(1)}, bf16[4,2,320,128]{3,2,1,0:T(8,128)(2,1)S(1)}, u32[]{:S(2)}, u32[]{:S(2)}) collective-permute-start(bf16[4,2,320,128]{3,2,1,0:T(8,128)(2,1)S(1)} %pad_maximum_fusion.1.weights.own), channel_id=1, source_target_pairs={{0,32},{32,0},{1,33},{33,1},{2,34},{34,2},{3,35},{35,3},{4,36},{36... | collective-permute-start | bytes 1966088 | tf_op jit(solution)/shard_map/ppermute | solution.py:40
  110.4 20.5 %all-to-all-start.3 = ((bf16[16,64,128]{2,1,0:T(8,128)(2,1)}), bf16[16,64,128]{2,1,0:T(8,128)(2,1)S(1)}, u32[]{:S(2)}, u32[]{:S(2)}) async-start(bf16[16,64,128]{2,1,0:T(8,128)(2,1)} %merge.1.after), calls=%async_computation.3 | async-start | bytes 524288 | tf_op jit(solution)/shard_map/all_to_all | solution.py:355
  116.2 1.6 copy-start.4
Sparse Core Ops, SparseCore 0:
  59.8 51.2 all-gather.2

commit v4 on v3

--- a/solution.py
+++ b/solution.py
@@ -1,3 +1,4 @@
+import functools
 import math
 
 import jax
@@ -26,7 +27,9 @@
 LOG2E = math.log2(math.e)
 
 ENC = ("x", "yh", "core")
+ENC_BACK = ("core", "yh", "x")
 SEQ = ("j", "h")
+SEQ_BACK = ("h", "j")
 VMEM = pl.BlockSpec(memory_space=pltpu.VMEM)
 SMEM = pl.BlockSpec(memory_space=pltpu.SMEM)
 ANY = pl.BlockSpec(memory_space=pl.ANY)
@@ -44,7 +47,21 @@
     return values * lax.rsqrt(jnp.mean(values * values, axis=-1, keepdims=True) + EPS) * gain
 
 
-def pack_kernel(w_qkv, w_out, kv_merge, out, lines):
+def pack_kernel(
+    w_qkv_hbm, w_out_hbm, kv_merge_hbm, patches_hbm, out, sent,
+    w_qkv, w_out, kv_merge, patches, lines, arrived,
+):
+    moves = [
+        (w_qkv_hbm, w_qkv), (w_out_hbm, w_out), (kv_merge_hbm, kv_merge), (patches_hbm, patches)
+    ]
+    copies = [
+        pltpu.make_async_copy(source, target, arrived.at[i])
+        for i, (source, target) in enumerate(moves)
+    ]
+    for copy in copies:
+        copy.start()
+    for copy in copies:
+        copy.wait()
     first = jnp.where(lax.axis_index("h") == 0, w_qkv[:, 0:480], w_qkv[:, 480:960])
     for c in range(4):
         size = min(128, 480 - c * 128)
@@ -56,29 +73,30 @@
         lines[pl.ds(c, 20, stride=10), :] = rows[:, c * 128 : (c + 1) * 128]
     out[320:528, :] = lines[...].astype(jnp.bfloat16)
     out[528:848, :] = jnp.where(lax.axis_index("h") == 0, kv_merge[:, 0:HD], kv_merge[:, HD:])
+    for rank in range(8):
+        sent[rank] = patches[rank % 4]
 
 
 def vision_kernel(tokens, slots, patches, gain, own, other, out, weight, lines, rows_out, mixed):
     core, yh, half = lax.axis_index("core"), lax.axis_index("yh"), lax.axis_index("h")
-    here = lax.axis_index("x")
-    slot = ((here * 2 + yh) * 2 + core) * IMG_ENC + lax.axis_index("j")
+    slot = ((lax.axis_index("x") * 2 + yh) * 2 + core) * IMG_ENC + lax.axis_index("j")
     for x in range(4):
         for rel in range(2):
             for c in range(4):
-                base = (here ^ x) * 4 + (yh ^ rel) * 2
+                base = x * 4 + (yh ^ rel) * 2
                 tile = pl.ds(c * 128, 128)
                 weight[pl.ds(pl.multiple_of((base + core) * 80, 16), 80), tile] = own[
-                    x, rel, c * 80 : (c + 1) * 80, :
+                    rel, x, c * 80 : (c + 1) * 80, :
                 ]
                 weight[pl.ds(pl.multiple_of((base + 1 - core) * 80, 16), 80), tile] = other[
-                    x, rel, c * 80 : (c + 1) * 80, :
+                    rel, x, c * 80 : (c + 1) * 80, :
                 ]
     rows_out[...] = jnp.zeros(rows_out.shape, jnp.float32)
     for head in range(2):
         for rel in range(2):
             for part, piece in enumerate((own, other)):
                 base = head * 128 + (rel * 2 + part) * 32
-                lines[...] = piece[here ^ (half * 2 + head), rel, 320:528, :].astype(jnp.float32)
+                lines[...] = piece[rel, half * 2 + head, 320:528, :].astype(jnp.float32)
                 for c in range(10):
                     rows_out[base : base + 20, c * 128 : (c + 1) * 128] = lines[
                         pl.ds(c, 20, stride=10), :
@@ -90,8 +108,8 @@
     count = jnp.int32(0)
     for i in range(slots.shape[0]):
         count = jnp.where(slots[i] == slot, tokens[i // IMG_ENC, i % IMG_ENC], count)
-    rows = patches[...].reshape(SLOT, VD).astype(jnp.float32)
-    normed = rms_scale(rows, gain[...]).astype(jnp.bfloat16)
+    rows = [patches[z % 2 * 4 + z // 2].astype(jnp.float32) for z in range(8)]
+    normed = rms_scale(jnp.concatenate(rows), gain[...]).astype(jnp.bfloat16)
     qkv = jnp.dot(normed, weight[...], preferred_element_type=jnp.float32)
     flipped = jnp.transpose(qkv).astype(jnp.bfloat16)
     live = lax.broadcasted_iota(jnp.int32, (SLOT, SLOT), 0) < MERGE * count
@@ -124,7 +142,8 @@
 
 def norm_kernel(parts, patches, gain, weights, out):
     del weights
-    total = patches[lax.axis_index("tp") * 2 + lax.axis_index("h")].astype(jnp.float32)
+    t = lax.axis_index("tp")
+    total = patches[t % 2 * 4 + lax.axis_index("h") * 2 + t // 2].astype(jnp.float32)
     for peer in range(8):
         total += parts[peer].astype(jnp.float32)
     total = rms_scale(total, gain[...]).astype(jnp.bfloat16)
@@ -134,11 +153,11 @@
 
 def merge_kernel(rows, own, other, out, merged, weight):
     core, yh = lax.axis_index("core"), lax.axis_index("yh")
-    for k in range(4):
+    for x in range(4):
         for rel in range(2):
-            base = (lax.axis_index("x") ^ k) * 4 + (yh ^ rel) * 2
-            weight[pl.ds(pl.multiple_of((base + core) * 320, 16), 320), :] = own[k, rel]
-            weight[pl.ds(pl.multiple_of((base + 1 - core) * 320, 16), 320), :] = other[k, rel]
+            base = x * 4 + (yh ^ rel) * 2
+            weight[pl.ds(pl.multiple_of((base + core) * 320, 16), 320), :] = own[rel, x]
+            weight[pl.ds(pl.multiple_of((base + 1 - core) * 320, 16), 320), :] = other[rel, x]
     normed = rows[...].reshape(SLOT, VD).astype(jnp.float32)
     for c in range(VD // 128):
         merged[c] = normed[:, c * 128 : (c + 1) * 128]
@@ -174,7 +193,9 @@
     for k in range(IMG_ENC):
         slot = slots[prompt * IMG_ENC + k]
         count = tokens[prompt, k]
-        base = jnp.where(slot % IMG_ENC == plane, (slot // IMG_ENC) * TOK - begin, -FAR)
+        enc = slot // IMG_ENC
+        place = (enc % 2) * 8 + (enc // 2 % 2) * 4 + enc // 4
+        base = jnp.where(slot % IMG_ENC == plane, place * TOK - begin, -FAR)
         inside = (row >= begin) & (row < begin + count)
         wanted = jnp.where(inside, row + base, wanted)
         begin = begin + count
@@ -186,12 +207,19 @@
         out[peer] = packed
 
 
-def text_kernel(tokens, gaps, queries, cached, after, out, top_out, sum_out, flipped):
+def text_kernel(blocks, tokens, gaps, queries, cached, *refs):
+    if blocks[0] == 0:
+        after, out, top_out, sum_out, flipped = refs
+    else:
+        accum, top_in, sum_in, queries_in, after, out, top_out, sum_out = refs
     del after
     prompt = prompt_index()
-    for g in range(GROUP):
-        block = queries[0, :, g * HD : (g + 1) * HD].astype(jnp.float32)
-        flipped[:, g * 128 : (g + 1) * 128] = jnp.transpose(block).astype(jnp.bfloat16)
+    if blocks[0] == 0:
+        for g in range(GROUP):
+            block = queries[0, :, g * HD : (g + 1) * HD].astype(jnp.float32)
+            flipped[:, g * 128 : (g + 1) * 128] = jnp.transpose(block).astype(jnp.bfloat16)
+    else:
+        flipped = queries_in
     factor = LOG2E / math.sqrt(HD)
     begin = jnp.int32(0)
     spans = []
@@ -199,11 +227,15 @@
         begin = begin + gaps[prompt, k]
         spans.append((begin, begin + tokens[prompt, k]))
         begin = begin + tokens[prompt, k]
-    top = jnp.full((1, GROUP * 128), NEG, jnp.float32)
-    total = jnp.zeros((1, GROUP * 128), jnp.float32)
-    out[...] = jnp.zeros(out.shape, jnp.float32)
+    if blocks[0] == 0:
+        top = jnp.full((1, GROUP * 128), NEG, jnp.float32)
+        total = jnp.zeros((1, GROUP * 128), jnp.float32)
+        out[...] = jnp.zeros(out.shape, jnp.float32)
+    else:
+        top, total = top_in[...], sum_in[...]
+        out[...] = accum[...]
     query = query_positions()
-    for part in range(6):
+    for part in blocks:
         if part < 4:
             size = 768
             window = cached[2 * part : 2 * part + 2, 0:384, :].reshape(size, 2 * HD)
@@ -234,8 +266,8 @@
 def join_kernel(tokens, gaps, images, flipped, accum, top, total, out):
     prompt = prompt_index()
     factor = LOG2E / math.sqrt(HD)
-    keys = (images[0] + images[2]) + (images[4] + images[6])
-    values = (images[1] + images[3]) + (images[5] + images[7])
+    keys = (images[0] + images[1]) + (images[2] + images[3])
+    values = (images[4] + images[5]) + (images[6] + images[7])
     index = lax.broadcasted_iota(jnp.int32, (IMG_TOTAL, 1), 0)
     position = index
     begin = jnp.int32(0)
@@ -303,24 +335,29 @@
     past = jnp.concatenate([cache_kv[0], text_kv[0]], axis=0)
     past = lax.all_gather(past, SEQ, axis=0)
 
-    heads = call(
+    heads, sent = pl.pallas_call(
         pack_kernel,
-        "pack",
-        array((848, 128)),
-        [VMEM] * 3,
-        [pltpu.VMEM((208, 128), f32)],
-        (1_000_000, 800_000, 0),
-    )(w_qkv, w_out, kv_merge)
+        out_shape=(array((848, 128)), array((8, 32, VD))),
+        in_specs=[ANY] * 4,
+        out_specs=(VMEM, VMEM),
+        scratch_shapes=[
+            pltpu.VMEM((80, 960), bf16),
+            pltpu.VMEM((20, VD), bf16),
+            pltpu.VMEM((320, 256), bf16),
+            pltpu.VMEM((4, 32, VD), bf16),
+            pltpu.VMEM((208, 128), f32),
+            pltpu.SemaphoreType.DMA((4,)),
+        ],
+        cost_estimate=pl.CostEstimate(flops=1_000_000, bytes_accessed=2_000_000, transcendentals=0),
+        name="pack",
+    )(w_qkv, w_out, kv_merge, patches)
     mine, theirs = heads, swap(heads, "yh")
 
-    sent = jnp.broadcast_to(patches[:, None], (4, 2, 32, VD)).reshape(8, 32, VD)
-    image = lax.all_to_all(sent, SEQ, 0, 0)
-    first = [mine[0:528]] + [swap_x(mine[0:528], k) for k in (1, 2, 3)]
-    second = [theirs[0:528]] + [swap_x(theirs[0:528], k) for k in (1, 2, 3)]
-    own = jnp.stack([jnp.stack(first), jnp.stack(second)], axis=1)
-    merge_pair = jnp.stack([mine[528:848], theirs[528:848]])
-    merge_pair = jnp.stack([merge_pair, swap_x(merge_pair, 1)])
-    other = swap(after(own, (image, merge_pair)), "core")
+    image = lax.all_to_all(sent, SEQ_BACK, 0, 0)
+    first = lax.all_gather(mine, "x", axis=0)
+    second = lax.all_gather(theirs, "x", axis=0)
+    own = jnp.stack([first[:, 0:528], second[:, 0:528]])
+    other = swap(after(own, image), "core")
 
     parts = call(
         vision_kernel,
@@ -335,14 +372,15 @@
         ],
         (600_000_000, 5_000_000, 131072),
     )(image_tokens, image_slot, image, norm_gain.reshape(1, VD), own, other)
-    merge_own = jnp.concatenate([merge_pair, swap_x(after(merge_pair, parts), 2)])
-    parts = lax.all_to_all(parts, ("tp", "h"), 0, 0)
+    first, second = after((first, second), parts)
+    merge_own = jnp.stack([first[:, 528:848], second[:, 528:848]])
+    parts = lax.all_to_all(parts, ("h", "tp"), 0, 0)
 
     rows = call(
         norm_kernel, "norm", array((8, 32, VD)), [VMEM] * 3 + [ANY], (), (1_000_000, 2_000_000, 32)
     )(parts, image, merge_gain.reshape(1, VD), merge_own)
     merge_other = swap(after(merge_own, rows), "core")
-    rows = lax.all_to_all(rows, ("tp", "h"), 0, 0)
+    rows = lax.all_to_all(rows, ("h", "tp"), 0, 0)
 
     image_kv = call(
         merge_kernel,
@@ -352,17 +390,17 @@
         [pltpu.VMEM((VD // 128, SLOT, 128), f32), pltpu.VMEM((MERGE * VD, HD), bf16)],
         (84_000_000, 3_000_000, 0),
     )(rows, merge_own, merge_other)
-    every = lax.all_to_all(image_kv, ENC, 0, 0)
-
-    accum, top, total, flipped = call(
-        text_kernel,
-        "text",
-        (array((HD, lanes), f32), array((1, lanes), f32), array((1, lanes), f32), array((HD, lanes))),
+    every = lax.all_to_all(image_kv, ENC_BACK, 0, 0)
+
+    state = (array((HD, lanes), f32), array((1, lanes), f32), array((1, lanes), f32))
+    *state_a, flipped = call(
+        functools.partial(text_kernel, (0, 1, 2)),
+        "cached",
+        state + (array((HD, lanes)),),
         [SMEM] * 2 + [VMEM] * 2 + [ANY],
         (),
-        (2_200_000_000, 4_000_000, lanes * 4096),
+        (1_200_000_000, 3_000_000, lanes * 2304),
     )(image_tokens, image_gap, queries, past, image_kv)
-
     packed = call(
         select_kernel,
         "select",
@@ -370,8 +408,16 @@
         [SMEM] * 2 + [VMEM, ANY],
         (),
         (42_000_000, 600_000, 0),
-    )(image_tokens, image_slot, every, total)
-    images = lax.all_to_all(packed, SEQ, 0, 0)
+    )(image_tokens, image_slot, every, flipped)
+    accum, top, total = call(
+        functools.partial(text_kernel, (3, 4, 5)),
+        "text",
+        state,
+        [SMEM] * 2 + [VMEM] * 6 + [ANY],
+        (),
+        (1_000_000_000, 3_000_000, lanes * 1792),
+    )(image_tokens, image_gap, queries, past, *state_a, flipped, packed)
+    images = lax.all_to_all(packed, SEQ_BACK, 0, 0)
 
     return call(
         join_kernel,

time: 160 us -> 158 us (0.988)
  the two profiles are of different devices: /device:TPU:8 before, /device:TPU:64 now
where the time goes in v4:
time: 158 us
  waiting for transfers between devices  44.5 us (28%)
  starting transfers between devices  44.2 us (28%)
  blocking collectives  28.1 us (18%)
  Pallas kernels  20.9 us (13%)
  between operations  13.6 us (9%)
  local copies, waits for them, and re-layouts  5.52 us (3%)
    all_to_all x1, waiting for transfers between devices, per_device(): parts = lax.all_to_all(parts, ('h', 'tp'), 0, 0)  16.2 us
    all_gather x1, blocking collectives, per_device(): first = lax.all_gather(mine, 'x', axis=0)  14.4 us
    all_gather x1, blocking collectives, per_device(): second = lax.all_gather(theirs, 'x', axis=0)  13.7 us
    all_to_all x1, waiting for transfers between devices, per_device(): rows = lax.all_to_all(rows, ('h', 'tp'), 0, 0)  12.3 us
    ppermute x3, starting transfers between devices, swap(): return lax.ppermute(value, axis, [(0, 1), (1, 0)])  11.8 us
    all_to_all x1, starting transfers between devices, per_device(): image = lax.all_to_all(sent, SEQ_BACK, 0, 0)  9.98 us
    all_to_all x1, starting transfers between devices, per_device(): images = lax.all_to_all(packed, SEQ_BACK, 0, 0)  7.23 us
    all_to_all x1, waiting for transfers between devices, per_device(): images = lax.all_to_all(packed, SEQ_BACK, 0, 0)  6.51 us
  transfers between devices with their start and end apart: 9, of which 6 were waited for; matrix products, arithmetic and copies ran while one was open for 1% of the time, Pallas kernels for 9%

profile of v4, /device:TPU:64, one launch (start us, length us, event | category | flops | bytes accessed | tf_op | source)
XLA Modules:
  0.0 157.6 jit_solution(228846711752471805)
XLA Ops:
  6.5 2.2 %pack.1 = (bf16[848,128]{1,0:T(8,128)(2,1)}, bf16[8,32,1280]{2,1,0:T(8,128)(2,1)}) custom-call(bf16[80,960]{1,0:T(8,128)(2,1)} %w_qkv_hbm.1, bf16[20,1280]{1,0:T(8,128)(2,1)} %w_out_hbm.1, bf16[320,256]{1,0:T(8,128)(2,1)} %kv_merge_hbm.1, bf16[4,32,1280]{2,1,0:T(8,128)(2,1)} %patches_hbm.1), custom_call_target="tpu_custom_call" | custom-call | flops 1000000 | bytes 2000000 | tf_op jit(solution)/shard_map/pack/pallas_call | solution.py:338
  8.7 0.0 copy-start.6
  8.7 7.9 %collective-permute-start = (bf16[848,128]{1,0:T(8,128)(2,1)}, bf16[848,128]{1,0:T(8,128)(2,1)S(1)}, u32[]{:S(2)}, u32[]{:S(2)}) collective-permute-start(bf16[848,128]{1,0:T(8,128)(2,1)} %get-tuple-element.19), channel_id=1, source_target_pairs={{0,64},{64,0},{1,65},{65,1},{2,66},{66,2},{3,67},{67,3},{4,68},{68... | collective-permute-start | bytes 651272 | tf_op jit(solution)/shard_map/ppermute | solution.py:43
  16.6 10.0 %all-to-all-start = ((bf16[8,32,1280]{2,1,0:T(8,128)(2,1)}), bf16[8,32,1280]{2,1,0:T(8,128)(2,1)S(1)}, u32[]{:S(2)}, u32[]{:S(2)}) async-start(bf16[8,32,1280]{2,1,0:T(8,128)(2,1)} %get-tuple-element.18), calls=%async_computation | async-start | bytes 1310720 | tf_op jit(solution)/shard_map/all_to_all | solution.py:356
  26.6 0.0 all-gather.5.cloned.1.call-start
  26.6 0.0 copy-done.6
  26.6 14.4 %all-gather = bf16[3392,128]{1,0:T(8,128)(2,1)S(1)} all-gather(bf16[848,128]{1,0:T(8,128)(2,1)S(1)} %copy-done.6), channel_id=2, replica_groups=mesh['x'=4,'yh'=2,'core'=2,'j'=4,'h'=2,'tp'=4] {'x'}, dimensions={0}, use_global_device_ids=true | all-gather | bytes 1085440 | tf_op jit(solution)/shard_map/all_gather | solution.py:357
  41.0 0.0 collective-permute-done
  41.0 13.7 %all-gather.1 = bf16[3392,128]{1,0:T(8,128)(2,1)S(1)} all-gather(bf16[848,128]{1,0:T(8,128)(2,1)S(1)} %collective-permute-done), channel_id=3, replica_groups=mesh['x'=4,'yh'=2,'core'=2,'j'=4,'h'=2,'tp'=4] {'x'}, dimensions={0}, use_global_device_ids=true | all-gather | bytes 1085440 | tf_op jit(solution)/shard_map/all_gather | solution.py:358
  54.7 0.0 copy-done.4
  54.7 0.9 copy-done.5
  55.7 0.0 copy-start.7
  55.7 0.0 copy-start.8
  55.7 0.0 copy-start.11
  55.7 0.0 copy-start.9
  55.7 0.0 copy-start
  55.7 0.1 pad_maximum_fusion.own
  55.9 0.0 all-to-all-done.patches
  55.9 1.9 %collective-permute-start.1 = (bf16[2,4,528,128]{3,2,1,0:T(8,128)(2,1)S(1)}, bf16[2,4,528,128]{3,2,1,0:T(8,128)(2,1)S(1)}, u32[]{:S(2)}, u32[]{:S(2)}) collective-permute-start(bf16[2,4,528,128]{3,2,1,0:T(8,128)(2,1)S(1)} %pad_maximum_fusion.own), channel_id=1, source_target_pairs={{0,32},{32,0},{1,33},{33,1},{2,34},{34,2},{3,35},{35,3},{4,36},{36... | collective-permute-start | bytes 3244040 | tf_op jit(solution)/shard_map/ppermute | solution.py:43
  57.8 0.0 copy-done.7
  57.8 0.0 copy-done.8
  57.8 0.7 pad_maximum_fusion.2
  58.5 0.0 all-gather.5.cloned.1.call-update
  58.6 0.0 copy-done.11
  58.6 0.1 copy.19.tokens
  58.7 1.8 %collective-permute-done.1.other = bf16[2,4,528,128]{3,2,1,0:T(8,128)(2,1)S(1)} collective-permute-done((bf16[2,4,528,128]{3,2,1,0:T(8,128)(2,1)S(1)}, bf16[2,4,528,128]{3,2,1,0:T(8,128)(2,1)S(1)}, u32[]{:S(2)}, u32[]{:S(2)}) %collective-permute-start.1) | collective-permute-done | bytes 1081376 | tf_op jit(solution)/shard_map/ppermute | solution.py:43
  60.5 3.7 %vision.1 = bf16[8,32,1280]{2,1,0:T(8,128)(2,1)} custom-call(s32[16,4]{1,0:T(8,128)S(1)} %copy.19.tokens, s32[64]{0:T(128)S(1)} %copy-done, bf16[8,32,1280]{2,1,0:T(8,128)(2,1)S(1)} %all-to-all-done.patches, f32[1,1280]{1,0:T(1,128)S(1)} %reshape.6.gain, bf16[2,4,528,128]{3,2,1,0:T(8,128)(2,1)S(1)} %pad_maximum_fusion.own, ...), custom_call_target="tpu_custom_call" | custom-call | flops 600000000 | bytes 5000000 | tf_op jit(solution)/shard_map/vision/pallas_call | solution.py:362
  64.2 3.8 %all-to-all-start.1 = ((bf16[8,32,1280]{2,1,0:T(8,128)(2,1)}), bf16[8,32,1280]{2,1,0:T(8,128)(2,1)S(1)}, u32[]{:S(2)}, u32[]{:S(2)}) async-start(bf16[8,32,1280]{2,1,0:T(8,128)(2,1)} %vision.1), calls=%async_computation.1 | async-start | bytes 1310720 | tf_op jit(solution)/shard_map/all_to_all | solution.py:377
  68.0 1.1 slice_bitcast_fusion.2
  69.1 0.1 pad_maximum_fusion.1.weights.own
  69.2 16.2 %all-to-all-done.1.parts = bf16[8,32,1280]{2,1,0:T(8,128)(2,1)S(1)} async-done(((bf16[8,32,1280]{2,1,0:T(8,128)(2,1)}), bf16[8,32,1280]{2,1,0:T(8,128)(2,1)S(1)}, u32[]{:S(2)}, u32[]{:S(2)}) %all-to-all-start.1) | async-done | bytes 655392 | tf_op jit(solution)/shard_map/all_to_all | solution.py:377
  85.4 1.1 norm.1
  86.4 5.0 %all-to-all-start.2 = ((bf16[8,32,1280]{2,1,0:T(8,128)(2,1)}), bf16[8,32,1280]{2,1,0:T(8,128)(2,1)S(1)}, u32[]{:S(2)}, u32[]{:S(2)}) async-start(bf16[8,32,1280]{2,1,0:T(8,128)(2,1)} %norm.1), calls=%async_computation.2 | async-start | bytes 1310720 | tf_op jit(solution)/shard_map/all_to_all | solution.py:383
  91.4 2.0 %collective-permute-start.2 = (bf16[2,4,320,128]{3,2,1,0:T(8,128)(2,1)S(1)}, bf16[2,4,320,128]{3,2,1,0:T(8,128)(2,1)S(1)}, u32[]{:S(2)}, u32[]{:S(2)}) collective-permute-start(bf16[2,4,320,128]{3,2,1,0:T(8,128)(2,1)S(1)} %pad_maximum_fusion.1.weights.own), channel_id=1, source_target_pairs={{0,32},{32,0},{1,33},{33,1},{2,34},{34,2},{3,35},{35,3},{4,36},{36... | collective-permute-start | bytes 1966088 | tf_op jit(solution)/shard_map/ppermute | solution.py:43
  93.5 2.1 %collective-permute-done.2.other = bf16[2,4,320,128]{3,2,1,0:T(8,128)(2,1)S(1)} collective-permute-done((bf16[2,4,320,128]{3,2,1,0:T(8,128)(2,1)S(1)}, bf16[2,4,320,128]{3,2,1,0:T(8,128)(2,1)S(1)}, u32[]{:S(2)}, u32[]{:S(2)}) %collective-permute-start.2) | collective-permute-done | bytes 655392 | tf_op jit(solution)/shard_map/ppermute | solution.py:43
  95.5 12.3 %all-to-all-done.2.rows = bf16[8,32,1280]{2,1,0:T(8,128)(2,1)S(1)} async-done(((bf16[8,32,1280]{2,1,0:T(8,128)(2,1)}), bf16[8,32,1280]{2,1,0:T(8,128)(2,1)S(1)}, u32[]{:S(2)}, u32[]{:S(2)}) %all-to-all-start.2) | async-done | bytes 655392 | tf_op jit(solution)/shard_map/all_to_all | solution.py:383
  107.8 1.2 merge.1.refs_0_
  109.0 6.4 %all-to-all-start.3 = ((bf16[16,64,128]{2,1,0:T(8,128)(2,1)}), bf16[16,64,128]{2,1,0:T(8,128)(2,1)S(1)}, u32[]{:S(2)}, u32[]{:S(2)}) async-start(bf16[16,64,128]{2,1,0:T(8,128)(2,1)} %merge.1.refs_0_), calls=%async_computation.3 | async-start | bytes 524288 | tf_op jit(solution)/shard_map/all_to_all | solution.py:393
  115.4 0.1 copy.20.gaps
  115.5 1.6 %copy-done.1 = bf16[4096,256]{1,0:T(8,128)(2,1)S(1)} copy-done((bf16[4096,256]{1,0:T(8,128)(2,1)S(1)}, bf16[4096,256]{1,0:T(8,128)(2,1)}, u32[]{:S(2)}) %copy-start.1) | copy-done | bytes 2097176
  117.1 4.6 %cached.1 = (f32[128,1024]{1,0:T(8,128)S(1)}, f32[1,1024]{1,0:T(1,128)S(1)}, f32[1,1024]{1,0:T(1,128)S(1)}, bf16[128,1024]{1,0:T(8,128)(2,1)S(1)}) custom-call(s32[16,4]{1,0:T(8,128)S(1)} %copy.19.tokens, s32[16,4]{1,0:T(8,128)S(1)} %copy.20.gaps, bf16[1,128,1024]{2,1,0:T(8,128)(2,1)S(1)} %copy-done.3, bf16[8,512,256]{2,1,0:T(8,128)(2,1)S(1)} %bitcast.13, ...), custom_call_target="tpu_custom_call" | custom-call | flops 1200000000 | bytes 3000000 | tf_op jit(solution)/shard_map/cached/pallas_call | solution.py:396
  121.7 5.7 %all-to-all-done.3.images = bf16[16,64,128]{2,1,0:T(8,128)(2,1)S(1)} async-done(((bf16[16,64,128]{2,1,0:T(8,128)(2,1)}), bf16[16,64,128]{2,1,0:T(8,128)(2,1)S(1)}, u32[]{:S(2)}, u32[]{:S(2)}) %all-to-all-start.3) | async-done | bytes 262176 | tf_op jit(solution)/shard_map/all_to_all | solution.py:393
  127.4 1.8 %select.1.refs_4_ = bf16[8,160,128]{2,1,0:T(8,128)(2,1)} custom-call(s32[16,4]{1,0:T(8,128)S(1)} %copy.19.tokens, s32[64]{0:T(128)S(1)} %copy-done, bf16[16,64,128]{2,1,0:T(8,128)(2,1)S(1)} %all-to-all-done.3.images, bf16[128,1024]{1,0:T(8,128)(2,1)S(1)} %get-tuple-element.24.after.refs_3_.flipped), custom_call_target="tpu_custom_call" | custom-call | flops 42000000 | bytes 600000 | tf_op jit(solution)/shard_map/select/pallas_call | solution.py:404
  129.2 7.2 %all-to-all-start.4 = ((bf16[8,160,128]{2,1,0:T(8,128)(2,1)}), bf16[8,160,128]{2,1,0:T(8,128)(2,1)S(1)}, u32[]{:S(2)}, u32[]{:S(2)}) async-start(bf16[8,160,128]{2,1,0:T(8,128)(2,1)} %select.1.refs_4_), calls=%async_computation.4 | async-start | bytes 655360 | tf_op jit(solution)/shard_map/all_to_all | solution.py:420
  136.4 1.6 %copy-done.2 = bf16[4096,256]{1,0:T(8,128)(2,1)S(1)} copy-done((bf16[4096,256]{1,0:T(8,128)(2,1)S(1)}, bf16[4096,256]{1,0:T(8,128)(2,1)}, u32[]{:S(2)}) %copy-start.2) | copy-done | bytes 2097176
  138.0 4.2 %text.1 = (f32[128,1024]{1,0:T(8,128)S(1)}, f32[1,1024]{1,0:T(1,128)S(1)}, f32[1,1024]{1,0:T(1,128)S(1)}) custom-call(s32[16,4]{1,0:T(8,128)S(1)} %copy.19.tokens, s32[16,4]{1,0:T(8,128)S(1)} %copy.20.gaps, bf16[1,128,1024]{2,1,0:T(8,128)(2,1)S(1)} %copy-done.3, bf16[8,512,256]{2,1,0:T(8,128)(2,1)S(1)} %bitcast.14, ...), custom_call_target="tpu_custom_call" | custom-call | flops 1000000000 | bytes 3000000 | tf_op jit(solution)/shard_map/text/pallas_call | solution.py:412
  142.2 6.5 %all-to-all-done.4.images = bf16[8,160,128]{2,1,0:T(8,128)(2,1)S(1)} async-done(((bf16[8,160,128]{2,1,0:T(8,128)(2,1)}), bf16[8,160,128]{2,1,0:T(8,128)(2,1)S(1)}, u32[]{:S(2)}, u32[]{:S(2)}) %all-to-all-start.4) | async-done | bytes 327712 | tf_op jit(solution)/shard_map/all_to_all | solution.py:420
  148.7 2.1 %join.1 = bf16[1,128,1024]{2,1,0:T(8,128)(2,1)} custom-call(s32[16,4]{1,0:T(8,128)S(1)} %copy.19.tokens, s32[16,4]{1,0:T(8,128)S(1)} %copy.20.gaps, bf16[8,160,128]{2,1,0:T(8,128)(2,1)S(1)} %all-to-all-done.4.images, bf16[128,1024]{1,0:T(8,128)(2,1)S(1)} %get-tuple-element.24.after.refs_3_.flipped, f32[128,1024]{1,0:T(8,128)S(1)} %get-tuple-element.28.accum, ...), custom_call_target="tpu_custom_call" | custom-call | flops 84000000 | bytes 2000000 | tf_op jit(solution)/shard_map/join/pallas_call | solution.py:422
  (17 shorter events, 0.1 us)
Async XLA Ops:
  8.7 17.9 %copy-start.6 = (bf16[848,128]{1,0:T(8,128)(2,1)S(1)}, bf16[848,128]{1,0:T(8,128)(2,1)}, u32[]{:S(2)}) copy-start(bf16[848,128]{1,0:T(8,128)(2,1)} %get-tuple-element.19) | copy-start | bytes 651268
  8.7 32.3 %collective-permute-start = (bf16[848,128]{1,0:T(8,128)(2,1)}, bf16[848,128]{1,0:T(8,128)(2,1)S(1)}, u32[]{:S(2)}, u32[]{:S(2)}) collective-permute-start(bf16[848,128]{1,0:T(8,128)(2,1)} %get-tuple-element.19), channel_id=1, source_target_pairs={{0,64},{64,0},{1,65},{65,1},{2,66},{66,2},{3,67},{67,3},{4,68},{68... | collective-permute-start | bytes 651272 | tf_op jit(solution)/shard_map/ppermute | solution.py:43
  16.6 39.2 %all-to-all-start = ((bf16[8,32,1280]{2,1,0:T(8,128)(2,1)}), bf16[8,32,1280]{2,1,0:T(8,128)(2,1)S(1)}, u32[]{:S(2)}, u32[]{:S(2)}) async-start(bf16[8,32,1280]{2,1,0:T(8,128)(2,1)} %get-tuple-element.18), calls=%async_computation | async-start | bytes 1310720 | tf_op jit(solution)/shard_map/all_to_all | solution.py:356
  26.6 88.9 %all-gather.5.cloned.1.call-start = ((), (), s32[]{:S(2)}) async-start(), calls=%async_computation.5 | async-start | bytes 2359296 | tf_op jit(solution)/shard_map/all_gather | solution.py:336
  41.0 13.8 %copy-start.4 = (bf16[3392,128]{1,0:T(8,128)(2,1)}, bf16[3392,128]{1,0:T(8,128)(2,1)S(1)}, u32[]{:S(2)}) copy-start(bf16[3392,128]{1,0:T(8,128)(2,1)S(1)} %all-gather) | copy-start | bytes 2605060
  54.7 0.9 copy-start.5
  55.7 2.1 %copy-start.7 = (bf16[1,384,256]{2,1,0:T(8,128)(2,1)S(1)}, bf16[1,384,256]{2,1,0:T(8,128)(2,1)}, u32[]{:S(2)}) copy-start(bf16[1,384,256]{2,1,0:T(8,128)(2,1)} %param.23) | copy-start | bytes 589828
  55.7 2.1 %copy-start.8 = (bf16[1,128,256]{2,1,0:T(8,128)(2,1)S(1)}, bf16[1,128,256]{2,1,0:T(8,128)(2,1)}, u32[]{:S(2)}) copy-start(bf16[1,128,256]{2,1,0:T(8,128)(2,1)} %param.22) | copy-start | bytes 196612
  55.7 2.9 %copy-start.11 = (s32[16,4]{0,1:T(4,128)S(1)}, s32[16,4]{0,1:T(4,128)}, u32[]{:S(2)}) copy-start(s32[16,4]{0,1:T(4,128)} %param.13) | copy-start | bytes 772
  55.7 2.9 %copy-start.9 = (f32[1280]{0:T(1024)S(1)}, f32[1280]{0:T(1024)}, u32[]{:S(2)}) copy-start(f32[1280]{0:T(1024)} %param.16) | copy-start | bytes 15364
  55.7 4.7 %copy-start = (s32[64]{0:T(128)S(1)}, s32[64]{0:T(128)}, u32[]{:S(2)}) copy-start(s32[64]{0:T(128)} %slots.3) | copy-start | bytes 772
  55.9 4.6 %collective-permute-start.1 = (bf16[2,4,528,128]{3,2,1,0:T(8,128)(2,1)S(1)}, bf16[2,4,528,128]{3,2,1,0:T(8,128)(2,1)S(1)}, u32[]{:S(2)}, u32[]{:S(2)}) collective-permute-start(bf16[2,4,528,128]{3,2,1,0:T(8,128)(2,1)S(1)} %pad_maximum_fusion.own), channel_id=1, source_target_pairs={{0,32},{32,0},{1,33},{33,1},{2,34},{34,2},{3,35},{35,3},{4,36},{36... | collective-permute-start | bytes 3244040 | tf_op jit(solution)/shard_map/ppermute | solution.py:43
  64.2 3.8 %copy-start.10 = (f32[1280]{0:T(1024)S(1)}, f32[1280]{0:T(1024)}, u32[]{:S(2)}) copy-start(f32[1280]{0:T(1024)} %param.17) | copy-start | bytes 15364
  64.2 21.1 %all-to-all-start.1 = ((bf16[8,32,1280]{2,1,0:T(8,128)(2,1)}), bf16[8,32,1280]{2,1,0:T(8,128)(2,1)S(1)}, u32[]{:S(2)}, u32[]{:S(2)}) async-start(bf16[8,32,1280]{2,1,0:T(8,128)(2,1)} %vision.1), calls=%async_computation.1 | async-start | bytes 1310720 | tf_op jit(solution)/shard_map/all_to_all | solution.py:377
  86.4 21.4 %all-to-all-start.2 = ((bf16[8,32,1280]{2,1,0:T(8,128)(2,1)}), bf16[8,32,1280]{2,1,0:T(8,128)(2,1)S(1)}, u32[]{:S(2)}, u32[]{:S(2)}) async-start(bf16[8,32,1280]{2,1,0:T(8,128)(2,1)} %norm.1), calls=%async_computation.2 | async-start | bytes 1310720 | tf_op jit(solution)/shard_map/all_to_all | solution.py:383
  91.4 24.0 %copy-start.12 = (s32[16,4]{0,1:T(4,128)S(1)}, s32[16,4]{0,1:T(4,128)}, u32[]{:S(2)}) copy-start(s32[16,4]{0,1:T(4,128)} %param.14) | copy-start | bytes 772
  91.4 24.1 %copy-start.3 = (bf16[1,128,1024]{2,1,0:T(8,128)(2,1)S(1)}, bf16[1,128,1024]{2,1,0:T(8,128)(2,1)}, u32[]{:S(2)}) copy-start(bf16[1,128,1024]{2,1,0:T(8,128)(2,1)} %queries.3) | copy-start | bytes 786436
  91.4 4.1 %collective-permute-start.2 = (bf16[2,4,320,128]{3,2,1,0:T(8,128)(2,1)S(1)}, bf16[2,4,320,128]{3,2,1,0:T(8,128)(2,1)S(1)}, u32[]{:S(2)}, u32[]{:S(2)}) collective-permute-start(bf16[2,4,320,128]{3,2,1,0:T(8,128)(2,1)S(1)} %pad_maximum_fusion.1.weights.own), channel_id=1, source_target_pairs={{0,32},{32,0},{1,33},{33,1},{2,34},{34,2},{3,35},{35,3},{4,36},{36... | collective-permute-start | bytes 1966088 | tf_op jit(solution)/shard_map/ppermute | solution.py:43
  109.0 18.4 %all-to-all-start.3 = ((bf16[16,64,128]{2,1,0:T(8,128)(2,1)}), bf16[16,64,128]{2,1,0:T(8,128)(2,1)S(1)}, u32[]{:S(2)}, u32[]{:S(2)}) async-start(bf16[16,64,128]{2,1,0:T(8,128)(2,1)} %merge.1.refs_0_), calls=%async_computation.3 | async-start | bytes 524288 | tf_op jit(solution)/shard_map/all_to_all | solution.py:393
  115.5 1.6 %copy-start.1 = (bf16[4096,256]{1,0:T(8,128)(2,1)S(1)}, bf16[4096,256]{1,0:T(8,128)(2,1)}, u32[]{:S(2)}) copy-start(bf16[4096,256]{1,0:T(8,128)(2,1)} %all-gather.5.cloned.1.call-done) | copy-start | bytes 6291460
  129.2 19.5 %all-to-all-start.4 = ((bf16[8,160,128]{2,1,0:T(8,128)(2,1)}), bf16[8,160,128]{2,1,0:T(8,128)(2,1)S(1)}, u32[]{:S(2)}, u32[]{:S(2)}) async-start(bf16[8,160,128]{2,1,0:T(8,128)(2,1)} %select.1.refs_4_), calls=%async_computation.4 | async-start | bytes 655360 | tf_op jit(solution)/shard_map/all_to_all | solution.py:420
  136.4 1.6 %copy-start.2 = (bf16[4096,256]{1,0:T(8,128)(2,1)S(1)}, bf16[4096,256]{1,0:T(8,128)(2,1)}, u32[]{:S(2)}) copy-start(bf16[4096,256]{1,0:T(8,128)(2,1)} %all-gather.5.cloned.1.call-done) | copy-start | bytes 6291460
Sparse Core Ops, SparseCore 0:
  58.7 46.3 all-gather.4

commit v5 on v4

--- a/solution.py
+++ b/solution.py
@@ -156,8 +156,8 @@
     for x in range(4):
         for rel in range(2):
             base = x * 4 + (yh ^ rel) * 2
-            weight[pl.ds(pl.multiple_of((base + core) * 320, 16), 320), :] = own[rel, x]
-            weight[pl.ds(pl.multiple_of((base + 1 - core) * 320, 16), 320), :] = other[rel, x]
+            weight[pl.ds(pl.multiple_of((base + core) * 320, 16), 320), :] = own[x, rel]
+            weight[pl.ds(pl.multiple_of((base + 1 - core) * 320, 16), 320), :] = other[x, rel]
     normed = rows[...].reshape(SLOT, VD).astype(jnp.float32)
     for c in range(VD // 128):
         merged[c] = normed[:, c * 128 : (c + 1) * 128]
@@ -354,9 +354,9 @@
     mine, theirs = heads, swap(heads, "yh")
 
     image = lax.all_to_all(sent, SEQ_BACK, 0, 0)
-    first = lax.all_gather(mine, "x", axis=0)
-    second = lax.all_gather(theirs, "x", axis=0)
-    own = jnp.stack([first[:, 0:528], second[:, 0:528]])
+    first = lax.all_gather(mine[0:528], "x", axis=0)
+    second = lax.all_gather(theirs[0:528], "x", axis=0)
+    own = jnp.stack([first, second])
     other = swap(after(own, image), "core")
 
     parts = call(
@@ -372,8 +372,8 @@
         ],
         (600_000_000, 5_000_000, 131072),
     )(image_tokens, image_slot, image, norm_gain.reshape(1, VD), own, other)
-    first, second = after((first, second), parts)
-    merge_own = jnp.stack([first[:, 528:848], second[:, 528:848]])
+    merge_pair = after(jnp.stack([mine[528:848], theirs[528:848]]), parts)
+    merge_own = lax.all_gather(merge_pair, "x", axis=0)
     parts = lax.all_to_all(parts, ("h", "tp"), 0, 0)
 
     rows = call(

time: 158 us -> 156 us (0.987)
  waiting for transfers between devices: 44.5 us -> 31.7 us
  blocking collectives: 28.1 us -> 39.4 us
  local copies, waits for them, and re-layouts: 5.52 us -> 3.43 us
    all_to_all x1, waiting for transfers between devices: 16.2 us -> 3.71 us  [per_device(): parts = lax.all_to_all(parts, ('h', 'tp'), 0, 0)]
    all_gather x2 -> x3, blocking collectives: 28.1 us -> 39.4 us  [the longest x1 13.3 us: per_device(): merge_own = lax.all_gather(merge_pair, 'x', axis=0)]
    unnamed x28 -> x24, local copies, waits for them, and re-layouts: 4.32 us -> 3.39 us
  transfers between devices with their start and end apart: 9 -> 9, of which waited for: 6 -> 6; matrix products, arithmetic and copies ran while one was open for 1% -> 1% of each run, Pallas kernels for 9% -> 10%
where the time goes in v5:
time: 156 us; the launch traced here: 155 us
  starting transfers between devices  45.1 us (29%)
  blocking collectives  39.4 us (25%)
  waiting for transfers between devices  31.7 us (20%)
  Pallas kernels  20.9 us (13%)
  between operations  13.6 us (9%)
  local copies, waits for them, and re-layouts  3.43 us (2%)
    all_gather x1, blocking collectives, per_device(): merge_own = lax.all_gather(merge_pair, 'x', axis=0)  13.3 us
    all_gather x1, blocking collectives, per_device(): first = lax.all_gather(mine[0:528], 'x', axis=0)  13.2 us
    all_gather x1, blocking collectives, per_device(): second = lax.all_gather(theirs[0:528], 'x', axis=0)  12.9 us
    all_to_all x1, waiting for transfers between devices, per_device(): rows = lax.all_to_all(rows, ('h', 'tp'), 0, 0)  11.9 us
    ppermute x3, starting transfers between devices, swap(): return lax.ppermute(value, axis, [(0, 1), (1, 0)])  11.8 us
    all_to_all x1, starting transfers between devices, per_device(): image = lax.all_to_all(sent, SEQ_BACK, 0, 0)  10.1 us
    all_to_all x1, starting transfers between devices, per_device(): images = lax.all_to_all(packed, SEQ_BACK, 0, 0)  7.98 us
    all_to_all x1, waiting for transfers between devices, per_device(): images = lax.all_to_all(packed, SEQ_BACK, 0, 0)  6.49 us
  transfers between devices with their start and end apart: 9, of which 6 were waited for; matrix products, arithmetic and copies ran while one was open for 1% of the time, Pallas kernels for 10%

profile of v5, /device:TPU:64, one launch (start us, length us, event | category | flops | bytes accessed | tf_op | source)
XLA Modules:
  0.0 154.9 jit_solution(5674497908952131700)
XLA Ops:
  6.5 2.2 %pack.1 = (bf16[848,128]{1,0:T(8,128)(2,1)}, bf16[8,32,1280]{2,1,0:T(8,128)(2,1)}) custom-call(bf16[80,960]{1,0:T(8,128)(2,1)} %w_qkv_hbm.1, bf16[20,1280]{1,0:T(8,128)(2,1)} %w_out_hbm.1, bf16[320,256]{1,0:T(8,128)(2,1)} %kv_merge_hbm.1, bf16[4,32,1280]{2,1,0:T(8,128)(2,1)} %patches_hbm.1), custom_call_target="tpu_custom_call" | custom-call | flops 1000000 | bytes 2000000 | tf_op jit(solution)/shard_map/pack/pallas_call | solution.py:338
  8.7 0.0 copy-start.4
  8.7 10.1 %all-to-all-start = ((bf16[8,32,1280]{2,1,0:T(8,128)(2,1)}), bf16[8,32,1280]{2,1,0:T(8,128)(2,1)S(1)}, u32[]{:S(2)}, u32[]{:S(2)}) async-start(bf16[8,32,1280]{2,1,0:T(8,128)(2,1)} %get-tuple-element.17), calls=%async_computation | async-start | bytes 1310720 | tf_op jit(solution)/shard_map/all_to_all | solution.py:356
  18.9 0.0 all-gather.6.cloned.1.call-start
  18.9 0.0 copy-done.4
  18.9 7.7 %collective-permute-start = (bf16[848,128]{1,0:T(8,128)(2,1)S(1)}, bf16[848,128]{1,0:T(8,128)(2,1)S(1)}, u32[]{:S(2)}, u32[]{:S(2)}) collective-permute-start(bf16[848,128]{1,0:T(8,128)(2,1)S(1)} %copy-done.4), channel_id=1, source_target_pairs={{0,64},{64,0},{1,65},{65,1},{2,66},{66,2},{3,67},{67,3},{4,68},{68... | collective-permute-start | bytes 651272 | tf_op jit(solution)/shard_map/ppermute | solution.py:43
  26.6 13.2 %all-gather = bf16[2112,128]{1,0:T(8,128)(2,1)S(1)} all-gather(bf16[528,128]{1,0:T(8,128)(2,1)S(1)} %slice.12), channel_id=2, replica_groups=mesh['x'=4,'yh'=2,'core'=2,'j'=4,'h'=2,'tp'=4] {'x'}, dimensions={0}, use_global_device_ids=true | all-gather | bytes 675840 | tf_op jit(solution)/shard_map/all_gather | solution.py:357
  39.8 0.0 collective-permute-done
  39.8 12.9 %all-gather.1 = bf16[2112,128]{1,0:T(8,128)(2,1)S(1)} all-gather(bf16[528,128]{1,0:T(8,128)(2,1)S(1)} %slice.16), channel_id=3, replica_groups=mesh['x'=4,'yh'=2,'core'=2,'j'=4,'h'=2,'tp'=4] {'x'}, dimensions={0}, use_global_device_ids=true | all-gather | bytes 675840 | tf_op jit(solution)/shard_map/all_gather | solution.py:358
  52.7 0.0 copy-start.5
  52.7 0.0 copy-start.6
  52.7 0.0 copy-start.9
  52.7 0.1 pad_maximum_fusion.own
  52.9 0.0 all-to-all-done.patches
  52.9 2.1 %collective-permute-start.1 = (bf16[2,4,528,128]{3,2,1,0:T(8,128)(2,1)S(1)}, bf16[2,4,528,128]{3,2,1,0:T(8,128)(2,1)S(1)}, u32[]{:S(2)}, u32[]{:S(2)}) collective-permute-start(bf16[2,4,528,128]{3,2,1,0:T(8,128)(2,1)S(1)} %pad_maximum_fusion.own), channel_id=1, source_target_pairs={{0,32},{32,0},{1,33},{33,1},{2,34},{34,2},{3,35},{35,3},{4,36},{36... | collective-permute-start | bytes 3244040 | tf_op jit(solution)/shard_map/ppermute | solution.py:43
  54.9 0.0 copy-done.5
  54.9 0.0 copy-done.6
  54.9 0.7 pad_maximum_fusion.1
  55.7 0.0 all-gather.6.cloned.1.call-update
  55.7 0.0 copy-done.9
  55.7 0.1 copy.27.tokens
  55.8 0.0 copy-done.7
  55.8 1.8 %collective-permute-done.1.other = bf16[2,4,528,128]{3,2,1,0:T(8,128)(2,1)S(1)} collective-permute-done((bf16[2,4,528,128]{3,2,1,0:T(8,128)(2,1)S(1)}, bf16[2,4,528,128]{3,2,1,0:T(8,128)(2,1)S(1)}, u32[]{:S(2)}, u32[]{:S(2)}) %collective-permute-start.1) | collective-permute-done | bytes 1081376 | tf_op jit(solution)/shard_map/ppermute | solution.py:43
  57.6 0.0 copy-done
  57.6 3.8 %vision.1 = bf16[8,32,1280]{2,1,0:T(8,128)(2,1)} custom-call(s32[16,4]{1,0:T(8,128)S(1)} %copy.27.tokens, s32[64]{0:T(128)S(1)} %copy-done, bf16[8,32,1280]{2,1,0:T(8,128)(2,1)S(1)} %all-to-all-done.patches, f32[1,1280]{1,0:T(1,128)S(1)} %reshape.6.gain, bf16[2,4,528,128]{3,2,1,0:T(8,128)(2,1)S(1)} %pad_maximum_fusion.own, ...), custom_call_target="tpu_custom_call" | custom-call | flops 600000000 | bytes 5000000 | tf_op jit(solution)/shard_map/vision/pallas_call | solution.py:362
  61.4 4.2 %all-to-all-start.1 = ((bf16[8,32,1280]{2,1,0:T(8,128)(2,1)}), bf16[8,32,1280]{2,1,0:T(8,128)(2,1)S(1)}, u32[]{:S(2)}, u32[]{:S(2)}) async-start(bf16[8,32,1280]{2,1,0:T(8,128)(2,1)} %vision.1), calls=%async_computation.1 | async-start | bytes 1310720 | tf_op jit(solution)/shard_map/all_to_all | solution.py:377
  65.6 0.0 copy-done.8
  65.7 13.3 %all-gather.2 = bf16[8,320,128]{2,1,0:T(8,128)(2,1)S(1)} all-gather(bf16[2,320,128]{2,1,0:T(8,128)(2,1)S(1)} %pad_maximum_fusion.2), channel_id=4, replica_groups=mesh['x'=4,'yh'=2,'core'=2,'j'=4,'h'=2,'tp'=4] {'x'}, dimensions={0}, use_global_device_ids=true | all-gather | bytes 819200 | tf_op jit(solution)/shard_map/all_gather | solution.py:376
  79.0 3.7 %all-to-all-done.1.parts = bf16[8,32,1280]{2,1,0:T(8,128)(2,1)S(1)} async-done(((bf16[8,32,1280]{2,1,0:T(8,128)(2,1)}), bf16[8,32,1280]{2,1,0:T(8,128)(2,1)S(1)}, u32[]{:S(2)}, u32[]{:S(2)}) %all-to-all-start.1) | async-done | bytes 655392 | tf_op jit(solution)/shard_map/all_to_all | solution.py:377
  82.7 1.1 norm.1
  83.8 4.9 %all-to-all-start.2 = ((bf16[8,32,1280]{2,1,0:T(8,128)(2,1)}), bf16[8,32,1280]{2,1,0:T(8,128)(2,1)S(1)}, u32[]{:S(2)}, u32[]{:S(2)}) async-start(bf16[8,32,1280]{2,1,0:T(8,128)(2,1)} %norm.1), calls=%async_computation.2 | async-start | bytes 1310720 | tf_op jit(solution)/shard_map/all_to_all | solution.py:383
  88.7 2.0 %collective-permute-start.2 = (bf16[4,2,320,128]{3,2,1,0:T(8,128)(2,1)S(1)}, bf16[4,2,320,128]{3,2,1,0:T(8,128)(2,1)S(1)}, u32[]{:S(2)}, u32[]{:S(2)}) collective-permute-start(bf16[4,2,320,128]{3,2,1,0:T(8,128)(2,1)S(1)} %bitcast.11), channel_id=1, source_target_pairs={{0,32},{32,0},{1,33},{33,1},{2,34},{34,2},{3,35},{35,3},{4,36},{36... | collective-permute-start | bytes 1966088 | tf_op jit(solution)/shard_map/ppermute | solution.py:43
  90.8 2.1 %collective-permute-done.2.other = bf16[4,2,320,128]{3,2,1,0:T(8,128)(2,1)S(1)} collective-permute-done((bf16[4,2,320,128]{3,2,1,0:T(8,128)(2,1)S(1)}, bf16[4,2,320,128]{3,2,1,0:T(8,128)(2,1)S(1)}, u32[]{:S(2)}, u32[]{:S(2)}) %collective-permute-start.2) | collective-permute-done | bytes 655392 | tf_op jit(solution)/shard_map/ppermute | solution.py:43
  92.8 11.9 %all-to-all-done.2.rows = bf16[8,32,1280]{2,1,0:T(8,128)(2,1)S(1)} async-done(((bf16[8,32,1280]{2,1,0:T(8,128)(2,1)}), bf16[8,32,1280]{2,1,0:T(8,128)(2,1)S(1)}, u32[]{:S(2)}, u32[]{:S(2)}) %all-to-all-start.2) | async-done | bytes 655392 | tf_op jit(solution)/shard_map/all_to_all | solution.py:383
  104.7 1.2 merge.1.refs_0_
  105.9 6.0 %all-to-all-start.3 = ((bf16[16,64,128]{2,1,0:T(8,128)(2,1)}), bf16[16,64,128]{2,1,0:T(8,128)(2,1)S(1)}, u32[]{:S(2)}, u32[]{:S(2)}) async-start(bf16[16,64,128]{2,1,0:T(8,128)(2,1)} %merge.1.refs_0_), calls=%async_computation.3 | async-start | bytes 524288 | tf_op jit(solution)/shard_map/all_to_all | solution.py:393
  111.9 0.0 copy-done.10
  111.9 0.1 copy.28.gaps
  112.0 0.0 copy-done.3
  112.0 1.6 %copy-done.1 = bf16[4096,256]{1,0:T(8,128)(2,1)S(1)} copy-done((bf16[4096,256]{1,0:T(8,128)(2,1)S(1)}, bf16[4096,256]{1,0:T(8,128)(2,1)}, u32[]{:S(2)}) %copy-start.1) | copy-done | bytes 2097176
  113.6 4.6 %cached.1 = (f32[128,1024]{1,0:T(8,128)S(1)}, f32[1,1024]{1,0:T(1,128)S(1)}, f32[1,1024]{1,0:T(1,128)S(1)}, bf16[128,1024]{1,0:T(8,128)(2,1)S(1)}) custom-call(s32[16,4]{1,0:T(8,128)S(1)} %copy.27.tokens, s32[16,4]{1,0:T(8,128)S(1)} %copy.28.gaps, bf16[1,128,1024]{2,1,0:T(8,128)(2,1)S(1)} %copy-done.3, bf16[8,512,256]{2,1,0:T(8,128)(2,1)S(1)} %bitcast.13, ...), custom_call_target="tpu_custom_call" | custom-call | flops 1200000000 | bytes 3000000 | tf_op jit(solution)/shard_map/cached/pallas_call | solution.py:396
  118.2 5.7 %all-to-all-done.3.images = bf16[16,64,128]{2,1,0:T(8,128)(2,1)S(1)} async-done(((bf16[16,64,128]{2,1,0:T(8,128)(2,1)}), bf16[16,64,128]{2,1,0:T(8,128)(2,1)S(1)}, u32[]{:S(2)}, u32[]{:S(2)}) %all-to-all-start.3) | async-done | bytes 262176 | tf_op jit(solution)/shard_map/all_to_all | solution.py:393
  123.9 1.8 %select.1.refs_4_ = bf16[8,160,128]{2,1,0:T(8,128)(2,1)} custom-call(s32[16,4]{1,0:T(8,128)S(1)} %copy.27.tokens, s32[64]{0:T(128)S(1)} %copy-done, bf16[16,64,128]{2,1,0:T(8,128)(2,1)S(1)} %all-to-all-done.3.images, bf16[128,1024]{1,0:T(8,128)(2,1)S(1)} %get-tuple-element.22.after.refs_3_.flipped), custom_call_target="tpu_custom_call" | custom-call | flops 42000000 | bytes 600000 | tf_op jit(solution)/shard_map/select/pallas_call | solution.py:404
  125.6 8.0 %all-to-all-start.4 = ((bf16[8,160,128]{2,1,0:T(8,128)(2,1)}), bf16[8,160,128]{2,1,0:T(8,128)(2,1)S(1)}, u32[]{:S(2)}, u32[]{:S(2)}) async-start(bf16[8,160,128]{2,1,0:T(8,128)(2,1)} %select.1.refs_4_), calls=%async_computation.4 | async-start | bytes 655360 | tf_op jit(solution)/shard_map/all_to_all | solution.py:420
  133.6 1.6 %copy-done.2 = bf16[4096,256]{1,0:T(8,128)(2,1)S(1)} copy-done((bf16[4096,256]{1,0:T(8,128)(2,1)S(1)}, bf16[4096,256]{1,0:T(8,128)(2,1)}, u32[]{:S(2)}) %copy-start.2) | copy-done | bytes 2097176
  135.2 4.2 %text.1 = (f32[128,1024]{1,0:T(8,128)S(1)}, f32[1,1024]{1,0:T(1,128)S(1)}, f32[1,1024]{1,0:T(1,128)S(1)}) custom-call(s32[16,4]{1,0:T(8,128)S(1)} %copy.27.tokens, s32[16,4]{1,0:T(8,128)S(1)} %copy.28.gaps, bf16[1,128,1024]{2,1,0:T(8,128)(2,1)S(1)} %copy-done.3, bf16[8,512,256]{2,1,0:T(8,128)(2,1)S(1)} %bitcast.14, ...), custom_call_target="tpu_custom_call" | custom-call | flops 1000000000 | bytes 3000000 | tf_op jit(solution)/shard_map/text/pallas_call | solution.py:412
  139.4 6.5 %all-to-all-done.4.images = bf16[8,160,128]{2,1,0:T(8,128)(2,1)S(1)} async-done(((bf16[8,160,128]{2,1,0:T(8,128)(2,1)}), bf16[8,160,128]{2,1,0:T(8,128)(2,1)S(1)}, u32[]{:S(2)}, u32[]{:S(2)}) %all-to-all-start.4) | async-done | bytes 327712 | tf_op jit(solution)/shard_map/all_to_all | solution.py:420
  145.9 2.1 %join.1 = bf16[1,128,1024]{2,1,0:T(8,128)(2,1)} custom-call(s32[16,4]{1,0:T(8,128)S(1)} %copy.27.tokens, s32[16,4]{1,0:T(8,128)S(1)} %copy.28.gaps, bf16[8,160,128]{2,1,0:T(8,128)(2,1)S(1)} %all-to-all-done.4.images, bf16[128,1024]{1,0:T(8,128)(2,1)S(1)} %get-tuple-element.22.after.refs_3_.flipped, f32[128,1024]{1,0:T(8,128)S(1)} %get-tuple-element.26.accum, ...), custom_call_target="tpu_custom_call" | custom-call | flops 84000000 | bytes 2000000 | tf_op jit(solution)/shard_map/join/pallas_call | solution.py:422
  (15 shorter events, 0.1 us)
Async XLA Ops:
  8.7 10.1 %copy-start.4 = (bf16[848,128]{1,0:T(8,128)(2,1)S(1)}, bf16[848,128]{1,0:T(8,128)(2,1)}, u32[]{:S(2)}) copy-start(bf16[848,128]{1,0:T(8,128)(2,1)} %get-tuple-element.18) | copy-start | bytes 651268
  8.7 44.1 %all-to-all-start = ((bf16[8,32,1280]{2,1,0:T(8,128)(2,1)}), bf16[8,32,1280]{2,1,0:T(8,128)(2,1)S(1)}, u32[]{:S(2)}, u32[]{:S(2)}) async-start(bf16[8,32,1280]{2,1,0:T(8,128)(2,1)} %get-tuple-element.17), calls=%async_computation | async-start | bytes 1310720 | tf_op jit(solution)/shard_map/all_to_all | solution.py:356
  18.9 93.1 %all-gather.6.cloned.1.call-start = ((), (), s32[]{:S(2)}) async-start(), calls=%async_computation.5 | async-start | bytes 2359296 | tf_op jit(solution)/shard_map/all_gather | solution.py:336
  18.9 20.9 %collective-permute-start = (bf16[848,128]{1,0:T(8,128)(2,1)S(1)}, bf16[848,128]{1,0:T(8,128)(2,1)S(1)}, u32[]{:S(2)}, u32[]{:S(2)}) collective-permute-start(bf16[848,128]{1,0:T(8,128)(2,1)S(1)} %copy-done.4), channel_id=1, source_target_pairs={{0,64},{64,0},{1,65},{65,1},{2,66},{66,2},{3,67},{67,3},{4,68},{68... | collective-permute-start | bytes 651272 | tf_op jit(solution)/shard_map/ppermute | solution.py:43
  52.7 2.2 %copy-start.5 = (bf16[1,384,256]{2,1,0:T(8,128)(2,1)S(1)}, bf16[1,384,256]{2,1,0:T(8,128)(2,1)}, u32[]{:S(2)}) copy-start(bf16[1,384,256]{2,1,0:T(8,128)(2,1)} %param.23) | copy-start | bytes 589828
  52.7 2.2 %copy-start.6 = (bf16[1,128,256]{2,1,0:T(8,128)(2,1)S(1)}, bf16[1,128,256]{2,1,0:T(8,128)(2,1)}, u32[]{:S(2)}) copy-start(bf16[1,128,256]{2,1,0:T(8,128)(2,1)} %param.22) | copy-start | bytes 196612
  52.7 3.0 %copy-start.9 = (s32[16,4]{0,1:T(4,128)S(1)}, s32[16,4]{0,1:T(4,128)}, u32[]{:S(2)}) copy-start(s32[16,4]{0,1:T(4,128)} %param.13) | copy-start | bytes 772
  52.7 3.0 %copy-start.7 = (f32[1280]{0:T(1024)S(1)}, f32[1280]{0:T(1024)}, u32[]{:S(2)}) copy-start(f32[1280]{0:T(1024)} %param.16) | copy-start | bytes 15364
  52.7 4.9 %copy-start = (s32[64]{0:T(128)S(1)}, s32[64]{0:T(128)}, u32[]{:S(2)}) copy-start(s32[64]{0:T(128)} %slots.3) | copy-start | bytes 772
  52.9 4.7 %collective-permute-start.1 = (bf16[2,4,528,128]{3,2,1,0:T(8,128)(2,1)S(1)}, bf16[2,4,528,128]{3,2,1,0:T(8,128)(2,1)S(1)}, u32[]{:S(2)}, u32[]{:S(2)}) collective-permute-start(bf16[2,4,528,128]{3,2,1,0:T(8,128)(2,1)S(1)} %pad_maximum_fusion.own), channel_id=1, source_target_pairs={{0,32},{32,0},{1,33},{33,1},{2,34},{34,2},{3,35},{35,3},{4,36},{36... | collective-permute-start | bytes 3244040 | tf_op jit(solution)/shard_map/ppermute | solution.py:43
  61.4 4.3 %copy-start.8 = (f32[1280]{0:T(1024)S(1)}, f32[1280]{0:T(1024)}, u32[]{:S(2)}) copy-start(f32[1280]{0:T(1024)} %param.17) | copy-start | bytes 15364
  61.4 21.3 %all-to-all-start.1 = ((bf16[8,32,1280]{2,1,0:T(8,128)(2,1)}), bf16[8,32,1280]{2,1,0:T(8,128)(2,1)S(1)}, u32[]{:S(2)}, u32[]{:S(2)}) async-start(bf16[8,32,1280]{2,1,0:T(8,128)(2,1)} %vision.1), calls=%async_computation.1 | async-start | bytes 1310720 | tf_op jit(solution)/shard_map/all_to_all | solution.py:377
  83.8 20.9 %all-to-all-start.2 = ((bf16[8,32,1280]{2,1,0:T(8,128)(2,1)}), bf16[8,32,1280]{2,1,0:T(8,128)(2,1)S(1)}, u32[]{:S(2)}, u32[]{:S(2)}) async-start(bf16[8,32,1280]{2,1,0:T(8,128)(2,1)} %norm.1), calls=%async_computation.2 | async-start | bytes 1310720 | tf_op jit(solution)/shard_map/all_to_all | solution.py:383
  88.7 23.2 %copy-start.10 = (s32[16,4]{0,1:T(4,128)S(1)}, s32[16,4]{0,1:T(4,128)}, u32[]{:S(2)}) copy-start(s32[16,4]{0,1:T(4,128)} %param.14) | copy-start | bytes 772
  88.7 23.3 %copy-start.3 = (bf16[1,128,1024]{2,1,0:T(8,128)(2,1)S(1)}, bf16[1,128,1024]{2,1,0:T(8,128)(2,1)}, u32[]{:S(2)}) copy-start(bf16[1,128,1024]{2,1,0:T(8,128)(2,1)} %queries.3) | copy-start | bytes 786436
  88.7 4.1 %collective-permute-start.2 = (bf16[4,2,320,128]{3,2,1,0:T(8,128)(2,1)S(1)}, bf16[4,2,320,128]{3,2,1,0:T(8,128)(2,1)S(1)}, u32[]{:S(2)}, u32[]{:S(2)}) collective-permute-start(bf16[4,2,320,128]{3,2,1,0:T(8,128)(2,1)S(1)} %bitcast.11), channel_id=1, source_target_pairs={{0,32},{32,0},{1,33},{33,1},{2,34},{34,2},{3,35},{35,3},{4,36},{36... | collective-permute-start | bytes 1966088 | tf_op jit(solution)/shard_map/ppermute | solution.py:43
  105.9 17.9 %all-to-all-start.3 = ((bf16[16,64,128]{2,1,0:T(8,128)(2,1)}), bf16[16,64,128]{2,1,0:T(8,128)(2,1)S(1)}, u32[]{:S(2)}, u32[]{:S(2)}) async-start(bf16[16,64,128]{2,1,0:T(8,128)(2,1)} %merge.1.refs_0_), calls=%async_computation.3 | async-start | bytes 524288 | tf_op jit(solution)/shard_map/all_to_all | solution.py:393
  112.0 1.6 %copy-start.1 = (bf16[4096,256]{1,0:T(8,128)(2,1)S(1)}, bf16[4096,256]{1,0:T(8,128)(2,1)}, u32[]{:S(2)}) copy-start(bf16[4096,256]{1,0:T(8,128)(2,1)} %all-gather.6.cloned.1.call-done) | copy-start | bytes 6291460
  125.6 20.3 %all-to-all-start.4 = ((bf16[8,160,128]{2,1,0:T(8,128)(2,1)}), bf16[8,160,128]{2,1,0:T(8,128)(2,1)S(1)}, u32[]{:S(2)}, u32[]{:S(2)}) async-start(bf16[8,160,128]{2,1,0:T(8,128)(2,1)} %select.1.refs_4_), calls=%async_computation.4 | async-start | bytes 655360 | tf_op jit(solution)/shard_map/all_to_all | solution.py:420
  133.6 1.6 %copy-start.2 = (bf16[4096,256]{1,0:T(8,128)(2,1)S(1)}, bf16[4096,256]{1,0:T(8,128)(2,1)}, u32[]{:S(2)}) copy-start(bf16[4096,256]{1,0:T(8,128)(2,1)} %all-gather.6.cloned.1.call-done) | copy-start | bytes 6291460
Sparse Core Ops, SparseCore 0:
  55.8 46.9 all-gather.5
